TPU v7x, 256 devices: a whole 4x4x8 slice. The times are simulated.
256 devices in a mesh: ctx: 128 (over z, y_hi, x, core), head: 2 (over y_lo).
Axes of the slice: x: 4, y: 4 (y_hi: 2, y_lo: 2; y = y_hi * 2 + y_lo), z: 8, core: 2. Of those that a mesh axis runs over, the one named last changes fastest.
Arguments:
- teacher_queries: bfloat16 [65536, 4096], P('ctx', 'head'), may hold values from -13.5 to 13.5
- teacher_keys: bfloat16 [65536, 1024], P('ctx', 'head'), may hold values from -6 to 6
- query_projection: float32 [32, 128, 128], P('head'), may hold values from -0.5 to 0.5
- key_projection: float32 [8, 384, 128], P('head'), may hold values from -0.3125 to 0.3125
- block_offsets: int32 [1024, 24], P('ctx'), may hold values from 0 to 24, as said below
- valid_counts: int32 [1024], P('ctx'), may hold values from 1 to 24, as said below
Outputs:
- query_gradient: float32 [32, 128, 128], P('head')
- key_gradient: float32 [8, 384, 128], P('head')
- mean_divergence: float32 [], replicated
Inputs may be any that keep to these rules, and one draw needn't show every extreme that they name: `block_offsets`: each row holds distinct offsets, the first of them 0 (a block's own diagonal block); the largest offset is reached in every draw. `valid_counts`: both ends are reached in every draw.
All inputs are finite; a program needn't handle non-finite values.
Results may differ from a plain program's by a relative error of at most 0.0003.
Values may be sent and summed in bfloat16 or wider, within the bound.
No kernel may reach another device: no remote copies, remote signals or barrier semaphores. Data moves between devices by JAX's collectives and lax.ppermute only.
A program may use at most 64 MiB of HBM per device.

v0:
```python
import math

import jax
import jax.numpy as jnp
from jax import lax
from jax.sharding import PartitionSpec as P

HEADS = 32
KV_HEADS = 8
HEAD_DIM = 128
BLOCK = 64
REACH = 4


def shifted(x, axis, by):
    count = lax.axis_size(axis)
    pairs = [(i, i + by) for i in range(count) if 0 <= i + by < count]
    return lax.ppermute(x, axis, pairs)


def block_map(query_block, cand_keys, offsets, usable):
    scores = jnp.einsum(
        "tgrd,cugd->grtcu", query_block, cand_keys, preferred_element_type=jnp.float32
    ) / math.sqrt(query_block.shape[-1])
    width = query_block.shape[0]
    query_pos = jnp.arange(width)[:, None, None]
    key_pos = jnp.arange(width)[None, None, :]
    allowed = ((offsets[None, :, None] != 0) | (key_pos <= query_pos)) & usable[None, :, None]
    scores = jnp.where(allowed, scores, -jnp.inf)
    top_score = jnp.max(scores, axis=(3, 4), keepdims=True)
    weights = jnp.exp(scores - top_score)
    per_block = jnp.sum(weights, axis=4)
    shares = per_block / jnp.sum(per_block, axis=3, keepdims=True)
    return jnp.mean(shares, axis=2)


def gate_terms(gate_query, cand_gate, teacher_map, usable):
    logits = jnp.einsum(
        "bgre,bcge->bgrc", gate_query, cand_gate, precision=lax.Precision.HIGHEST
    ) / math.sqrt(gate_query.shape[-1])
    mask = usable[:, None, None, :]
    logits = jnp.where(mask, logits, -jnp.inf)
    log_gate = logits - jax.nn.logsumexp(logits, axis=3, keepdims=True)
    log_gate = jnp.where(mask, log_gate, 0.0)
    terms = jnp.where(
        mask, jax.scipy.special.xlogy(teacher_map, teacher_map) - teacher_map * log_gate, 0.0
    )
    return jnp.sum(terms)


def body(
    teacher_queries, teacher_keys, query_projection, key_projection, block_offsets, valid_counts
):
    group_size = HEADS // KV_HEADS
    local_kv = teacher_keys.shape[1] // HEAD_DIM
    blocks_here = teacher_keys.shape[0] // BLOCK
    cand_slots = block_offsets.shape[1]
    pieces = [teacher_keys]
    moving = teacher_keys
    for relay_step in range(REACH - 1):
        moving = shifted(moving, "ctx", 1)
        pieces.insert(0, moving)
    window = jnp.concatenate(pieces, axis=0)
    window_blocks = window.reshape(REACH * blocks_here, BLOCK, local_kv, HEAD_DIM)
    first_block = lax.axis_index("ctx") * blocks_here
    row_index = first_block + jnp.arange(blocks_here, dtype=jnp.int32)
    key_block = row_index[:, None] - block_offsets
    slot_index = jnp.arange(cand_slots, dtype=jnp.int32)
    usable = (slot_index[None, :] < valid_counts[:, None]) & (key_block >= 0)
    local_index = (
        (REACH - 1) * blocks_here
        + jnp.arange(blocks_here, dtype=jnp.int32)[:, None]
        - block_offsets
    )
    query_blocks = teacher_queries.reshape(blocks_here, BLOCK, local_kv, group_size, HEAD_DIM)

    def one_block(inputs):
        query_block, index_row, offsets, usable_row = inputs
        return block_map(query_block, window_blocks[index_row], offsets, usable_row)

    teacher_map = lax.map(one_block, (query_blocks, local_index, block_offsets, usable))
    pooled_query = jnp.mean(query_blocks, axis=1, dtype=jnp.float32)
    pooled_key = jnp.concatenate(
        [
            jnp.max(window_blocks, axis=1).astype(jnp.float32),
            jnp.min(window_blocks, axis=1).astype(jnp.float32),
            jnp.mean(window_blocks, axis=1, dtype=jnp.float32),
        ],
        axis=-1,
    )

    def local_loss(query_weights, key_weights):
        gate_query = jnp.einsum(
            "bgrd,grde->bgre",
            pooled_query,
            query_weights.reshape(local_kv, group_size, HEAD_DIM, query_weights.shape[2]),
            precision=lax.Precision.HIGHEST,
        )
        gate_key = jnp.einsum(
            "ngf,gfe->nge", pooled_key, key_weights, precision=lax.Precision.HIGHEST
        )
        return gate_terms(gate_query, gate_key[local_index], teacher_map, usable)

    local_total, grads = jax.value_and_grad(local_loss, argnums=(0, 1))(
        query_projection, key_projection
    )
    block_total = blocks_here * lax.axis_size("ctx")
    grad_scale = 1.0 / math.sqrt(block_total)
    query_sum, key_sum = lax.psum((grads[0], grads[1]), "ctx")
    kl_total = lax.psum(local_total, ("ctx", "head"))
    return (query_sum * grad_scale, key_sum * grad_scale, kl_total / (block_total * HEADS))


def solution(mesh):
    placed = (
        P("ctx", "head"),
        P("ctx", "head"),
        P("head", None, None),
        P("head", None, None),
        P("ctx", None),
        P("ctx"),
    )
    return jax.shard_map(
        body,
        mesh=mesh,
        in_specs=placed,
        out_specs=(P("head", None, None), P("head", None, None), P()),
        check_vma=False,
    )
```

profile of v0, /device:TPU:1, one launch (start us, length us, event | category | flops | bytes accessed | tf_op | source)
XLA Modules:
  0.0 1462.0 jit_solution(5562680888750567726)
XLA Ops:
  7.2 4.6 collective-permute-start
  11.9 6.4 collective-permute-done
  18.3 4.3 collective-permute-start.1
  24.8 3.9 collective-permute-done.1
  28.7 4.5 collective-permute-start.2
  48.1 116.4 %while.11 = (s32[]{:T(128)}, f32[8,4,4,24]{3,2,1,0:T(4,128)}, s32[8,24]{1,0:T(8,128)}, pred[8,24]{1,0:T(8,128)(4,1)S(1)}, s32[8,24]{1,0:T(8,128)S(1)}, /*index=5...) while((s32[]{:T(128)}, f32[8,4,4,24]{3,2,1,0:T(4,128)}, s32[8,24]{1,0:T(8,128)}, ...), condition=%wide.region_6.7_spmd.clone, body=%wide.region_1.6_spmd.sunk.clone | while | flops 415460448 | bytes 18632436 | solution.py:81
  57.8 4.0 fusion.42
  68.5 3.8 fusion.41
  72.3 4.0 fusion.42
  83.0 3.8 fusion.41
  86.9 4.0 fusion.42
  97.6 3.8 fusion.41
  101.4 4.0 fusion.42
  112.1 3.8 fusion.41
  115.9 4.0 fusion.42
  126.6 3.8 fusion.41
  130.5 4.0 fusion.42
  141.2 3.8 fusion.41
  145.0 4.0 fusion.42
  155.7 3.8 fusion.41
  159.6 4.0 fusion.42
  175.4 7.1 scatter_fusion
  184.9 93.7 %psum.23 = f32[]{:T(128)} all-reduce(f32[]{:T(128)} %get-tuple-element.73), channel_id=1, replica_groups=mesh['ctx'=128,'head'=2] {'ctx','head'}, use_global_device_ids=true, to_apply=%region_17.18 | all-reduce | flops 1 | bytes 8 | tf_op jit(solution)/shard_map/psum | solution.py:110
  279.3 1170.4 %all-reduce.3.cloned.1.call-done = (f32[16,128,128]{2,1,0:T(8,128)}, f32[4,384,128]{2,1,0:T(8,128)}) async-done(((f32[16,128,128]{2,1,0:T(8,128)}, f32[4,384,128]{2,1,0:T(8,128)}), (f32[16,128,128]{2,1,0:T(8,128)}, f32[4,384,128]{2,1,0:T(8,128)})) %all-reduce.3.cloned.1.call-update) | async-done | bytes 1835024 | tf_op jit(solution)/shard_map/psum | solution.py:109
  (178 shorter events, 91.9 us)
Async XLA Ops:
  7.2 30.1 %copy-start = (f32[16,128,128]{2,1,0:T(8,128)S(1)}, f32[16,128,128]{2,1,0:T(8,128)}, u32[]{:S(2)}) copy-start(f32[16,128,128]{2,1,0:T(8,128)} %param.10) | copy-start | bytes 3145732
  7.2 1442.5 %all-reduce.3.cloned.1.call-start = ((), (), s32[]{:S(2)}) async-start(), calls=%async_computation | async-start | bytes 3670016 | tf_op jit(solution)/shard_map/psum | solution.py:109
  7.2 11.1 collective-permute-start
  18.3 14.9 %copy-start.8 = (bf16[512,512]{1,0:T(8,128)(2,1)}, bf16[512,512]{1,0:T(8,128)(2,1)S(1)}, u32[]{:S(2)}) copy-start(bf16[512,512]{1,0:T(8,128)(2,1)S(1)} %collective-permute-done) | copy-start | bytes 1572868
  18.3 10.4 collective-permute-start.1
  28.7 10.9 collective-permute-start.2
  36.4 3.2 copy-start.1
  36.5 3.1 copy-start.7
  36.5 3.1 copy-start.9
  48.1 2.7 copy-start.10
  57.8 4.9 copy-start.11
  62.6 2.7 copy-start.10
  72.3 4.9 copy-start.11
  77.2 2.7 copy-start.10
  86.8 4.9 copy-start.11
  91.7 2.7 copy-start.10
  101.4 4.9 copy-start.11
  115.9 4.9 copy-start.11
  130.5 4.9 copy-start.11
  135.4 2.7 copy-start.10
  145.0 4.9 copy-start.11
  159.6 4.9 copy-start.11
  167.2 15.4 %copy-start.4 = (f32[32,4,128]{2,0,1:T(8,128)S(1)}, f32[32,4,128]{2,0,1:T(8,128)}, u32[]{:S(2)}) copy-start(f32[32,4,128]{2,0,1:T(8,128)} %copy-done.3) | copy-start | bytes 196612
  167.2 15.4 %copy-start.6 = (f32[32,4,128]{2,0,1:T(8,128)S(1)}, f32[32,4,128]{2,0,1:T(8,128)}, u32[]{:S(2)}) copy-start(f32[32,4,128]{2,0,1:T(8,128)} %copy-done.5) | copy-start | bytes 196612
  (6 other events, 12.0 us)
Sparse Core Ops, SparseCore 0:
  185.1 1264.5 all-reduce.2
where the time goes:
time: 1470 us; the launch traced here: 1460 us
  waiting for transfers between devices  1180 us (80%)
  blocking collectives  93.7 us (6%)
  other arithmetic  61.9 us (4%)
  local copies, waits for them, and re-layouts  51.9 us (4%)
  matrix products  43 us (3%)
  between operations  16.1 us (1%)
    psum x1, waiting for transfers between devices, body(): query_sum, key_sum = lax.psum((grads[0], grads[1]), 'ctx')  1170 us
    psum x1, blocking collectives, body(): kl_total = lax.psum(local_total, ('ctx', 'head'))  93.7 us
    reduce_sum x8, other arithmetic, block_map(): shares = per_block / jnp.sum(per_block, axis=3, keepdims=True)  31.7 us
    dot_general x8, matrix products, block_map(): jnp.einsum('tgrd,cugd->grtcu', query_block, cand_keys, preferred_element_...  30.7 us
  transfers between devices with their start and end apart: 4, of which 4 were waited for; matrix products, arithmetic and copies ran while one was open for 1% of the time, Pallas kernels for 0%

commit v1 on v0

v1 whole, which is shorter than its diff:
```python
import math

import jax
import jax.numpy as jnp
from jax import lax
from jax.experimental import pallas as pl
from jax.experimental.pallas import tpu as pltpu
from jax.sharding import Mesh, PartitionSpec as P

HEADS = 32
KV_HEADS = 8
HEAD_DIM = 128
BLOCK = 64
CAND = 24
REACH = 4

ROWS = 8
SPAN = 24
CHIP_BLOCKS = 2 * ROWS
WINDOW = SPAN + CHIP_BLOCKS
PADDED = 48
KV_HERE = 2
GROUP = HEADS // KV_HEADS
Q_COLS = KV_HERE * GROUP * HEAD_DIM
K_COLS = KV_HERE * HEAD_DIM
DUMMY = 31
SLOT_ROWS = 32
LANES = GROUP * CHIP_BLOCKS
SHARES = 8
GRAD_ROWS = KV_HERE * GROUP * HEAD_DIM + KV_HERE * 3 * HEAD_DIM
SHARE_ROWS = GRAD_ROWS // SHARES
LOW = -1e30
EXP_SCALE = math.log2(math.e) / math.sqrt(HEAD_DIM)
HIGH = lax.Precision.HIGHEST


def dot_f32(a, b, dims):
    return lax.dot_general(
        a, b, (dims, ((), ())), precision=HIGH, preferred_element_type=jnp.float32
    )


def kernel(
    core_ref, rho_ref, groups_ref,
    q_own_ref, q_other_ref, k_own_ref, k_other_ref, k_prev_ref, k_far_ref,
    usable_ref, wq_ref, wk_ref,
    out_ref,
    keys, pooled_key, pooled_query, slot_max, slot_sum, shares,
):
    core = core_ref[0]
    half = ROWS * BLOCK
    own_at = pl.multiple_of((SPAN + ROWS * core) * BLOCK, half)
    other_at = pl.multiple_of((SPAN + ROWS * (1 - core)) * BLOCK, half)
    prev_own_at = pl.multiple_of((ROWS + ROWS * core) * BLOCK, half)
    prev_other_at = pl.multiple_of((ROWS + ROWS * (1 - core)) * BLOCK, half)
    places = (
        (0, k_far_ref, 0),
        (prev_own_at, k_prev_ref, 0),
        (prev_other_at, k_prev_ref, half),
        (own_at, k_own_ref, 0),
        (other_at, k_other_ref, 0),
    )
    for at, source, first in places:
        tile = source[first:first + half, :]
        keys[pl.ds(at, half), :] = tile
        wide = tile.astype(jnp.float32).reshape(ROWS, BLOCK, K_COLS)
        row = at // BLOCK if isinstance(at, int) else pl.multiple_of(lax.div(at, BLOCK), ROWS)
        top = jnp.max(wide, axis=1)
        low = jnp.min(wide, axis=1)
        mean = jnp.sum(wide, axis=1) * (1.0 / BLOCK)
        for g in range(KV_HERE):
            cols = slice(g * HEAD_DIM, (g + 1) * HEAD_DIM)
            for part, value in enumerate((top, low, mean)):
                pooled_key[g, pl.ds(row, ROWS), part * HEAD_DIM:(part + 1) * HEAD_DIM] = (
                    value[:, cols]
                )
    for g in range(KV_HERE):
        pooled_key[g, WINDOW:PADDED, :] = jnp.zeros((PADDED - WINDOW, 3 * HEAD_DIM), jnp.float32)
    shares[...] = jnp.zeros_like(shares)

    width = GROUP * BLOCK
    lane = lax.broadcasted_iota(jnp.int32, (BLOCK, width), 1) % BLOCK
    causal = lax.broadcasted_iota(jnp.int32, (BLOCK, width), 0) <= lane
    slot_row = lax.broadcasted_iota(jnp.int32, (SLOT_ROWS, width), 0)
    live = slot_row <= SPAN
    spread = jnp.where(
        lax.broadcasted_iota(jnp.int32, (width, LANES), 0) // BLOCK
        == lax.broadcasted_iota(jnp.int32, (width, LANES), 1) // CHIP_BLOCKS,
        1.0 / BLOCK, 0.0,
    ).astype(jnp.bfloat16)
    lane_block = lax.broadcasted_iota(jnp.int32, (SLOT_ROWS, LANES), 1) % CHIP_BLOCKS

    def one_group(s, block, g, queries, first_slot, diagonal):
        rows = [rho_ref[s * CAND + first_slot + i] for i in range(4)]
        tiles = []
        for row in rows:
            n = block + jnp.minimum(row, SPAN)
            tiles.append(
                keys[pl.ds(pl.multiple_of(n * BLOCK, BLOCK), BLOCK),
                     g * HEAD_DIM:(g + 1) * HEAD_DIM]
            )
        scores = lax.dot_general(
            jnp.concatenate(tiles, axis=0), queries, (((1,), (1,)), ((), ())),
            preferred_element_type=jnp.float32,
        )
        for i, row in enumerate(rows):
            part = scores[i * BLOCK:(i + 1) * BLOCK, :]
            if diagonal and i == 0:
                part = jnp.where(causal, part, LOW)
            top = jnp.max(part, axis=0, keepdims=True)
            total = jnp.sum(jnp.exp2((part - top) * EXP_SCALE), axis=0, keepdims=True)
            slot_max[pl.ds(row, 1), :] = top
            slot_sum[pl.ds(row, 1), :] = total

    def one_block(s, q_ref, at, block):
        for g in range(KV_HERE):
            queries = jnp.concatenate(
                [
                    q_ref[pl.ds(at, BLOCK), (g * GROUP + r) * HEAD_DIM:(g * GROUP + r + 1) * HEAD_DIM]
                    for r in range(GROUP)
                ],
                axis=0,
            )
            for r in range(GROUP):
                pooled_query[g, pl.ds(r * CHIP_BLOCKS + s, 1), :] = jnp.sum(
                    queries[r * BLOCK:(r + 1) * BLOCK, :].astype(jnp.float32), axis=0, keepdims=True
                ) * (1.0 / BLOCK)
            slot_max[...] = jnp.full_like(slot_max, LOW)
            slot_sum[...] = jnp.zeros_like(slot_sum)
            one_group(s, block, g, queries, 0, True)

            @pl.loop(1, groups_ref[s])
            def _(i):
                one_group(s, block, g, queries, i * 4, False)

            tops = jnp.where(live, slot_max[...], LOW)
            top = jnp.max(tops, axis=0, keepdims=True)
            weight = jnp.where(live, slot_sum[...] * jnp.exp2((tops - top) * EXP_SCALE), 0.0)
            share = weight / jnp.sum(weight, axis=0, keepdims=True)
            coarse = share.astype(jnp.bfloat16)
            fine = (share - coarse.astype(jnp.float32)).astype(jnp.bfloat16)
            mean = (
                jnp.dot(coarse, spread, preferred_element_type=jnp.float32)
                + jnp.dot(fine, spread, preferred_element_type=jnp.float32)
            )
            mine = jnp.where(lane_block == s, mean, 0.0)
            shares[g, pl.ds(block, SLOT_ROWS), :] += mine

    for source in range(2):
        q_ref = (q_own_ref, q_other_ref)[source]
        first = ROWS * core if source == 0 else ROWS * (1 - core)

        @pl.loop(0, ROWS)
        def _(j):
            one_block(source * ROWS + j, q_ref, pl.multiple_of(j * BLOCK, BLOCK), first + j)

    scale = 1.0 / math.sqrt(HEAD_DIM)
    usable = usable_ref[...] > 0.0
    divergence = jnp.zeros((1, LANES), jnp.float32)

    def put(row, value):
        done = 0
        while done < value.shape[0]:
            share_index, inside = divmod(row + done, SHARE_ROWS)
            count = min(value.shape[0] - done, SHARE_ROWS - inside)
            out_ref[share_index, inside:inside + count, :] = value[done:done + count, :]
            done += count

    for g in range(KV_HERE):
        gate_key = dot_f32(pooled_key[g], wk_ref[g], ((1,), (0,)))
        gate_query = jnp.concatenate(
            [
                dot_f32(
                    pooled_query[g, r * CHIP_BLOCKS:(r + 1) * CHIP_BLOCKS, :],
                    wq_ref[g * GROUP + r], ((1,), (0,)),
                )
                for r in range(GROUP)
            ],
            axis=0,
        )
        logits = dot_f32(gate_key, gate_query, ((1,), (1,))) * scale
        logits = jnp.where(usable, logits, LOW)
        top = jnp.max(logits, axis=0, keepdims=True)
        weight = jnp.where(usable, jnp.exp(logits - top), 0.0)
        mass = jnp.sum(weight, axis=0, keepdims=True)
        log_gate = jnp.where(usable, logits - top - jnp.log(mass), 0.0)
        target = shares[g]
        positive = target > 0.0
        log_target = jnp.log(jnp.where(positive, target, 1.0))
        terms = jnp.where(usable, target * (log_target - log_gate), 0.0)
        divergence += jnp.sum(terms, axis=0, keepdims=True)
        target = jnp.where(usable, target, 0.0)
        slope = (weight / mass) * jnp.sum(target, axis=0, keepdims=True) - target
        slope = slope * (scale / 32.0)
        d_query = dot_f32(slope, gate_key, ((0,), (0,)))
        d_key = dot_f32(slope, gate_query, ((1,), (0,)))
        for r in range(GROUP):
            picked = slice(r * CHIP_BLOCKS, (r + 1) * CHIP_BLOCKS)
            put(
                (g * GROUP + r) * HEAD_DIM,
                dot_f32(pooled_query[g, picked, :], d_query[picked, :], ((0,), (0,))),
            )
        put(
            KV_HERE * GROUP * HEAD_DIM + g * 3 * HEAD_DIM,
            dot_f32(pooled_key[g], d_key, ((0,), (0,))),
        )
    total = jnp.sum(divergence)
    for i in range(SHARES):
        out_ref[i, SHARE_ROWS:SHARE_ROWS + 8, :] = jnp.full((8, HEAD_DIM), total, jnp.float32)


def swap(x, axis):
    return lax.ppermute(x, axis, [(0, 1), (1, 0)])


def body(
    teacher_queries, teacher_keys, query_projection, key_projection, block_offsets, valid_counts
):
    chips = ("z", "yh", "x")
    places = ("z", "yh", "x", "core")
    count = lax.axis_size(places)
    core = lax.axis_index("core")
    chip = lax.axis_index(chips)
    half = ROWS * BLOCK

    note = jnp.concatenate(
        [block_offsets, valid_counts[:, None], jnp.zeros((ROWS, K_COLS - CAND - 1), jnp.int32)], axis=1
    ).astype(jnp.bfloat16)
    note = jnp.concatenate([note, jnp.zeros_like(note)], axis=0)
    k_mine = lax.dynamic_slice_in_dim(teacher_keys, core * K_COLS, K_COLS, 1)
    k_give = lax.dynamic_slice_in_dim(teacher_keys, (1 - core) * K_COLS, K_COLS, 1)
    k_other = swap(jnp.concatenate([k_give, note], axis=0), "core")
    note_other = k_other[half:half + ROWS, :CAND + 1].astype(jnp.int32)
    k_other = k_other[:half]
    k_prev = lax.ppermute(
        jnp.concatenate([k_mine, k_other], axis=0), places,
        [(i, i + 2) for i in range(count - 2)],
    )
    k_far = lax.ppermute(
        jnp.where(core == 1, k_mine, k_other), places, [(i, i + 4) for i in range(count - 4)]
    )
    q_other = swap(
        lax.dynamic_slice_in_dim(teacher_queries, (1 - core) * Q_COLS, Q_COLS, 1), "core"
    )

    offsets = jnp.concatenate([block_offsets, note_other[:, :CAND]], axis=0)
    counts = jnp.concatenate([valid_counts, note_other[:, CAND]], axis=0)
    step = jnp.arange(CHIP_BLOCKS, dtype=jnp.int32)
    block = jnp.where(step < ROWS, core * ROWS + step, (1 - core) * ROWS + step - ROWS)
    key_block = chip * CHIP_BLOCKS + block[:, None] - offsets
    usable = (jnp.arange(CAND, dtype=jnp.int32)[None, :] < counts[:, None]) & (key_block >= 0)
    rho = jnp.where(usable, SPAN - offsets, DUMMY)
    place = jnp.where(usable, block[:, None] + rho, -1)
    hit = jnp.any(
        place[None, :, :] == jnp.arange(PADDED, dtype=jnp.int32)[:, None, None], axis=2
    )
    hit = jnp.tile(hit.astype(jnp.float32), (1, GROUP))
    groups = (counts + 3) // 4

    wq = lax.dynamic_slice_in_dim(query_projection, core * KV_HERE * GROUP, KV_HERE * GROUP, 0)
    wk = lax.dynamic_slice_in_dim(key_projection, core * KV_HERE, KV_HERE, 0)

    whole = lambda *shape: pl.BlockSpec(shape, lambda i, c, r, n: (0,) * len(shape))
    parts = pl.pallas_call(
        kernel,
        grid_spec=pltpu.PrefetchScalarGridSpec(
            num_scalar_prefetch=3,
            grid=(1,),
            in_specs=[
                pl.BlockSpec((half, Q_COLS), lambda i, c, r, n: (0, c[0])),
                whole(half, Q_COLS),
                whole(half, K_COLS),
                whole(half, K_COLS),
                whole(2 * half, K_COLS),
                whole(half, K_COLS),
                whole(PADDED, LANES),
                whole(KV_HERE * GROUP, HEAD_DIM, HEAD_DIM),
                whole(KV_HERE, 3 * HEAD_DIM, HEAD_DIM),
            ],
            out_specs=whole(SHARES, SHARE_ROWS + 8, HEAD_DIM),
            scratch_shapes=[
                pltpu.VMEM((WINDOW * BLOCK, K_COLS), jnp.bfloat16),
                pltpu.VMEM((KV_HERE, PADDED, 3 * HEAD_DIM), jnp.float32),
                pltpu.VMEM((KV_HERE, LANES, HEAD_DIM), jnp.float32),
                pltpu.VMEM((SLOT_ROWS, GROUP * BLOCK), jnp.float32),
                pltpu.VMEM((SLOT_ROWS, GROUP * BLOCK), jnp.float32),
                pltpu.VMEM((KV_HERE, PADDED, LANES), jnp.float32),
            ],
        ),
        out_shape=jax.ShapeDtypeStruct((SHARES, SHARE_ROWS + 8, HEAD_DIM), jnp.float32),
        compiler_params=pltpu.CompilerParams(vmem_limit_bytes=40 * 1024 * 1024),
        name="gate",
    )(
        core.reshape(1).astype(jnp.int32), rho.reshape(-1), groups,
        teacher_queries, q_other, k_mine, k_other, k_prev, k_far, hit, wq, wk,
    )

    got = lax.all_to_all(parts, ("yh", "x"), 0, 0)
    got = jnp.sum(got, axis=0)
    for far in (1, 2, 4):
        got = got + lax.ppermute(got, "z", [(i, i ^ far) for i in range(8)])
    total = got[SHARE_ROWS:SHARE_ROWS + 1, :]
    total = total + swap(total, "head")
    total = total + swap(total, "core")
    spread = jnp.broadcast_to(got[:SHARE_ROWS], (SHARES, SHARE_ROWS, HEAD_DIM))
    mine = lax.all_to_all(spread, ("yh", "x"), 0, 0).reshape(GRAD_ROWS, HEAD_DIM)
    other = swap(mine, "core")
    first = jnp.where(core == 0, mine, other)
    second = jnp.where(core == 0, other, mine)
    cut = KV_HERE * GROUP * HEAD_DIM
    query_gradient = jnp.concatenate([first[:cut], second[:cut]], axis=0)
    key_gradient = jnp.concatenate([first[cut:], second[cut:]], axis=0)
    return (
        query_gradient.reshape(2 * KV_HERE * GROUP, HEAD_DIM, HEAD_DIM),
        key_gradient.reshape(2 * KV_HERE, 3 * HEAD_DIM, HEAD_DIM),
        total[0, 0] / (1024 * HEADS),
    )


def solution(mesh):
    split = Mesh(mesh.devices.reshape(8, 2, 4, 2, 2), ("z", "yh", "x", "core", "head"))
    ctx = ("z", "yh", "x", "core")
    placed = (
        P(ctx, "head"),
        P(ctx, "head"),
        P("head", None, None),
        P("head", None, None),
        P(ctx, None),
        P(ctx),
    )
    return jax.shard_map(
        body,
        mesh=split,
        in_specs=placed,
        out_specs=(P("head", None, None), P("head", None, None), P()),
        check_vma=False,
    )
```

time: 1470 us -> 153 us (0.10)
  waiting for transfers between devices: 1180 us -> 19.3 us
  blocking collectives: 93.7 us -> 35.3 us
  other arithmetic: 61.9 us -> 7.41 us
  matrix products: 43 us -> 0 us
  local copies, waits for them, and re-layouts: 51.9 us -> 10.4 us
  Pallas kernels: 0 us -> 41 us
  starting transfers between devices: 13.4 us -> 37.2 us
    psum x1 -> x0, waiting for transfers between devices: 1170 us -> none  [body(): query_sum, key_sum = lax.psum((grads[0], grads[1]), 'ctx')]
    psum x1 -> x0, blocking collectives: 93.7 us -> none  [body(): kl_total = lax.psum(local_total, ('ctx', 'head'))]
    dot_general x15 -> x0, matrix products: 43 us -> none  [the longest x8 30.7 us: block_map(): jnp.einsum('tgrd,cugd->grtcu', query_block, cand_keys, preferred_element_...]
    pallas_call x0 -> x1, Pallas kernels: none -> 41 us  [body(): pl.pallas_call(kernel, grid_spec=pltpu.PrefetchScalarGridSpec(num_scalar_...]
    reduce_sum x20 -> x1, other arithmetic: 36.6 us -> 0.05 us  [body(): got = jnp.sum(got, axis=0)]
    all_to_all x0 -> x2, blocking collectives: none -> 35.3 us  [the longest x1 21.3 us: body(): got = lax.all_to_all(parts, ('yh', 'x'), 0, 0)]
    gather x9 -> x0, local copies, waits for them, and re-layouts: 26 us -> none  [the longest x8 25.1 us: one_block(): return block_map(query_block, window_blocks[index_row], offsets, usable_row)]
    ppermute x3 -> x10, starting transfers between devices: 13.4 us -> 37.2 us  [the longest x3 16.8 us: body(): got = got + lax.ppermute(got, 'z', [(i, i ^ far) for i in range(8)])]
  transfers between devices with their start and end apart: 4 -> 10, of which waited for: 4 -> 6; matrix products, arithmetic and copies ran while one was open for 1% -> 6% of each run, Pallas kernels for 0% -> 0%
where the time goes in v1:
time: 153 us
  Pallas kernels  41 us (27%)
  starting transfers between devices  37.2 us (24%)
  blocking collectives  35.3 us (23%)
  waiting for transfers between devices  19.3 us (13%)
  local copies, waits for them, and re-layouts  10.4 us (7%)
  other arithmetic  7.41 us (5%)
  between operations  1.99 us (1%)
    pallas_call x1, Pallas kernels, body(): pl.pallas_call(kernel, grid_spec=pltpu.PrefetchScalarGridSpec(num_scalar_...  41 us
    all_to_all x1, blocking collectives, body(): got = lax.all_to_all(parts, ('yh', 'x'), 0, 0)  21.3 us
    ppermute x3, starting transfers between devices, body(): got = got + lax.ppermute(got, 'z', [(i, i ^ far) for i in range(8)])  16.8 us
    all_to_all x1, blocking collectives, body(): lax.all_to_all(spread, ('yh', 'x'), 0, 0).reshape(GRAD_ROWS, HEAD_DIM)  14 us
    ppermute x5, starting transfers between devices, swap(): return lax.ppermute(x, axis, [(0, 1), (1, 0)])  13.9 us
    ppermute x1, waiting for transfers between devices, body(): lax.ppermute(jnp.where(core == 1, k_mine, k_other), places, [(i, i + 4) f...  10.3 us
    ppermute x3, waiting for transfers between devices, body(): got = got + lax.ppermute(got, 'z', [(i, i ^ far) for i in range(8)])  7.14 us
    ppermute x1, starting transfers between devices, body(): lax.ppermute(jnp.where(core == 1, k_mine, k_other), places, [(i, i + 4) f...  4.25 us
  transfers between devices with their start and end apart: 10, of which 6 were waited for; matrix products, arithmetic and copies ran while one was open for 6% of the time, Pallas kernels for 0%

profile of v1, /device:TPU:1, one launch (start us, length us, event | category | flops | bytes accessed | tf_op | source)
XLA Modules:
  0.0 152.7 jit_solution(4844973843919731711)
XLA Ops:
  2.2 1.0 constant_dynamic-slice_fusion.4
  3.4 3.3 %collective-permute-start = (bf16[528,256]{1,0:T(8,128)(2,1)S(1)}, bf16[528,256]{1,0:T(8,128)(2,1)}, u32[]{:S(2)}, u32[]{:S(2)}) collective-permute-start(bf16[528,256]{1,0:T(8,128)(2,1)S(1)} %maximum_maximum_fusion), channel_id=1, source_target_pairs={{0,2},{2,0},{1,3},{3,1},{4,6},{6,4},{5,7},{7,5},{8,10},{10,8},{9,1... | collective-permute-start | bytes 811016 | tf_op jit(solution)/shard_map/ppermute | solution.py:213
  6.7 2.3 %constant_dynamic-slice_fusion.3 = bf16[512,1024]{1,0:T(8,128)(2,1)} fusion(bf16[512,2048]{1,0:T(8,128)(2,1)} %q_own_ref.1, s32[]{:T(128)S(6)} %select_n.75), kind=kLoop, calls=%fused_computation.22 | loop fusion | bytes 2097156 | tf_op jit(solution)/shard_map/dynamic_slice | solution.py:243
  9.0 1.9 %constant_dynamic-slice_fusion.wk_ref = f32[2,384,128]{2,1,0:T(8,128)} fusion(f32[4,384,128]{2,1,0:T(8,128)} %param.9, s32[]{:T(128)S(6)} %select_n.81), kind=kLoop, calls=%fused_computation.19 | loop fusion | bytes 786436 | tf_op jit(solution)/shard_map/dynamic_slice | solution.py:261
  11.8 1.8 %broadcast_select_fusion.2 = (bf16[512,256]{1,0:T(8,128)(2,1)}, bf16[512,256]{1,0:T(8,128)(2,1)S(1)}, bf16[512,256]{1,0:T(8,128)(2,1)S(1)}) fusion(pred[]{:T(512)S(6)} %eq.21, bf16[528,256]{1,0:T(8,128)(2,1)} %collective-permute-done, bf16[512,512]{1,0:T(8,128)(2,1)} %param.7, s32[]{:T(128)S(6)} %select_n.76), kind=kLoop, calls=%fused_computation.6 | loop fusion | flops 131072 | bytes 1310725 | tf_op jit(solution)/shard_map/jit(_where)/select_n | solution.py:240
  15.1 2.2 %collective-permute-start.2 = (bf16[1024,256]{1,0:T(8,128)(2,1)}, bf16[1024,256]{1,0:T(8,128)(2,1)}, u32[]{:S(2)}, u32[]{:S(2)}) collective-permute-start(bf16[1024,256]{1,0:T(8,128)(2,1)} %pad_maximum_fusion.2), channel_id=1, source_target_pairs={{0,4},{2,6},{4,8},{6,10},{8,12},{10,14},{12,16},{14,18},{16,20},{1... | collective-permute-start | bytes 1572872 | tf_op jit(solution)/shard_map/ppermute | solution.py:235
  17.3 4.2 %collective-permute-start.3 = (bf16[512,256]{1,0:T(8,128)(2,1)}, bf16[512,256]{1,0:T(8,128)(2,1)}, u32[]{:S(2)}, u32[]{:S(2)}) collective-permute-start(bf16[512,256]{1,0:T(8,128)(2,1)} %get-tuple-element.3), channel_id=1, source_target_pairs={{0,8},{2,10},{4,12},{6,14},{8,16},{10,18},{12,20},{14,22},{16,24},... | collective-permute-start | bytes 786440 | tf_op jit(solution)/shard_map/ppermute | solution.py:239
  23.0 10.3 %collective-permute-done.3.k_far_ref = bf16[512,256]{1,0:T(8,128)(2,1)} collective-permute-done((bf16[512,256]{1,0:T(8,128)(2,1)}, bf16[512,256]{1,0:T(8,128)(2,1)}, u32[]{:S(2)}, u32[]{:S(2)}) %collective-permute-start.3) | collective-permute-done | bytes 262176 | tf_op jit(solution)/shard_map/ppermute | solution.py:239
  34.2 1.0 copy-done.4
  35.2 1.0 copy-done.5
  36.2 41.0 %gate.1 = f32[8,232,128]{2,1,0:T(8,128)S(1)} custom-call(s32[1]{0:T(128)} %bitcast.core_ref, s32[384]{0:T(512)S(1)} %select_n.73.rho_ref, s32[16]{0:T(128)S(1)} %get-tuple-element.5.groups_ref, bf16[512,2048]{1,0:T(8,128)(2,1)S(1)} %copy-done.1, bf16[512,1024]{1,0:T(8,128)(2,1)} %collective-permute-done.1.q_other_ref, ...), custom_call_target="tpu_custom_call" | custom-call | tf_op jit(solution)/shard_map/gate/pallas_call | solution.py:264
  77.3 21.3 %all_to_all.10 = f32[8,232,128]{2,1,0:T(8,128)S(1)} all-to-all(f32[8,232,128]{2,1,0:T(8,128)S(1)} %gate.1), channel_id=1, replica_groups=mesh['z'=8,'yh'=2,'x'=4,'core'=2,'head'=2] {'yh','x'}, dimensions={0} | all-to-all | bytes 1900544 | tf_op jit(solution)/shard_map/all_to_all | solution.py:298
  98.7 1.3 collective-permute-start.4
  99.9 2.5 %collective-permute-done.4 = f32[232,128]{1,0:T(8,128)S(1)} collective-permute-done((f32[232,128]{1,0:T(8,128)S(1)}, f32[232,128]{1,0:T(8,128)S(1)}, u32[]{:S(2)}, u32[]{:S(2)}) %collective-permute-start.4) | collective-permute-done | bytes 118816 | tf_op jit(solution)/shard_map/ppermute | solution.py:301
  102.4 7.1 %collective-permute-start.5 = (f32[232,128]{1,0:T(8,128)S(1)}, f32[232,128]{1,0:T(8,128)S(1)}, u32[]{:S(2)}, u32[]{:S(2)}) collective-permute-start(f32[232,128]{1,0:T(8,128)S(1)} %add.113), channel_id=1, source_target_pairs={{0,64},{32,96},{64,0},{96,32},{128,192},{160,224},{192,128},{224,1... | collective-permute-start | bytes 356360 | tf_op jit(solution)/shard_map/ppermute | solution.py:301
  109.5 2.2 %collective-permute-done.5 = f32[232,128]{1,0:T(8,128)S(1)} collective-permute-done((f32[232,128]{1,0:T(8,128)S(1)}, f32[232,128]{1,0:T(8,128)S(1)}, u32[]{:S(2)}, u32[]{:S(2)}) %collective-permute-start.5) | collective-permute-done | bytes 118816 | tf_op jit(solution)/shard_map/ppermute | solution.py:301
  111.8 8.4 %collective-permute-start.6 = (f32[232,128]{1,0:T(8,128)S(1)}, f32[232,128]{1,0:T(8,128)S(1)}, u32[]{:S(2)}, u32[]{:S(2)}) collective-permute-start(f32[232,128]{1,0:T(8,128)S(1)} %add.114), channel_id=1, source_target_pairs={{0,128},{32,160},{64,192},{96,224},{128,0},{160,32},{192,64},{224,... | collective-permute-start | bytes 356360 | tf_op jit(solution)/shard_map/ppermute | solution.py:301
  120.2 2.4 %collective-permute-done.6 = f32[232,128]{1,0:T(8,128)S(1)} collective-permute-done((f32[232,128]{1,0:T(8,128)S(1)}, f32[232,128]{1,0:T(8,128)S(1)}, u32[]{:S(2)}, u32[]{:S(2)}) %collective-permute-start.6) | collective-permute-done | bytes 118816 | tf_op jit(solution)/shard_map/ppermute | solution.py:301
  122.8 14.0 %all_to_all.11 = f32[8,224,128]{2,1,0:T(8,128)S(1)} all-to-all(f32[8,224,128]{2,1,0:T(8,128)S(1)} %broadcast_in_dim.31), channel_id=1, replica_groups=mesh['z'=8,'yh'=2,'x'=4,'core'=2,'head'=2] {'yh','x'}, dimensions={0} | all-to-all | bytes 1835008 | tf_op jit(solution)/shard_map/all_to_all | solution.py:306
  136.8 8.1 %collective-permute-start.7 = (f32[1792,128]{1,0:T(8,128)S(1)}, f32[1792,128]{1,0:T(8,128)S(1)}, u32[]{:S(2)}, u32[]{:S(2)}) collective-permute-start(f32[1792,128]{1,0:T(8,128)S(1)} %bitcast.12), channel_id=1, source_target_pairs={{0,2},{2,0},{1,3},{3,1},{4,6},{6,4},{5,7},{7,5},{8,10},{10,8},{9,1... | collective-permute-start | bytes 2752520 | tf_op jit(solution)/shard_map/ppermute | solution.py:213
  144.9 1.3 collective-permute-start.8
  146.2 1.1 collective-permute-done.8
  147.3 1.2 collective-permute-start.9
  150.5 1.0 pad_maximum_fusion
  (54 shorter events, 8.6 us)
Async XLA Ops:
  0.6 10.3 %copy-start = (f32[16,128,128]{2,1,0:T(8,128)S(1)}, f32[16,128,128]{2,1,0:T(8,128)}, u32[]{:S(2)}) copy-start(f32[16,128,128]{2,1,0:T(8,128)} %param.8) | copy-start | bytes 3145732
  3.4 8.4 %collective-permute-start = (bf16[528,256]{1,0:T(8,128)(2,1)S(1)}, bf16[528,256]{1,0:T(8,128)(2,1)}, u32[]{:S(2)}, u32[]{:S(2)}) collective-permute-start(bf16[528,256]{1,0:T(8,128)(2,1)S(1)} %maximum_maximum_fusion), channel_id=1, source_target_pairs={{0,2},{2,0},{1,3},{3,1},{4,6},{6,4},{5,7},{7,5},{8,10},{10,8},{9,1... | collective-permute-start | bytes 811016 | tf_op jit(solution)/shard_map/ppermute | solution.py:213
  9.0 24.3 %collective-permute-start.1 = (bf16[512,1024]{1,0:T(8,128)(2,1)}, bf16[512,1024]{1,0:T(8,128)(2,1)}, u32[]{:S(2)}, u32[]{:S(2)}) collective-permute-start(bf16[512,1024]{1,0:T(8,128)(2,1)} %constant_dynamic-slice_fusion.3), channel_id=1, source_target_pairs={{0,2},{2,0},{1,3},{3,1},{4,6},{6,4},{5,7},{7,5},{8,10},{10,8},{9,1... | collective-permute-start | bytes 3145736 | tf_op jit(solution)/shard_map/ppermute | solution.py:213
  9.0 13.4 %copy-start.7 = (s32[8]{0:T(128)S(1)}, s32[8]{0:T(128)}, u32[]{:S(2)}) copy-start(s32[8]{0:T(128)} %param.11) | copy-start | bytes 100
  9.0 13.5 %copy-start.6 = (s32[8,24]{1,0:T(8,128)S(1)}, s32[8,24]{1,0:T(8,128)}, u32[]{:S(2)}) copy-start(s32[8,24]{1,0:T(8,128)} %param.10) | copy-start | bytes 2308
  9.0 24.2 %copy-start.1 = (bf16[512,2048]{1,0:T(8,128)(2,1)S(1)}, bf16[512,2048]{1,0:T(8,128)(2,1)}, u32[]{:S(2)}) copy-start(bf16[512,2048]{1,0:T(8,128)(2,1)} %q_own_ref.1) | copy-start | bytes 6291460
  14.5 0.7 copy-start.2
  15.1 18.1 %collective-permute-start.2 = (bf16[1024,256]{1,0:T(8,128)(2,1)}, bf16[1024,256]{1,0:T(8,128)(2,1)}, u32[]{:S(2)}, u32[]{:S(2)}) collective-permute-start(bf16[1024,256]{1,0:T(8,128)(2,1)} %pad_maximum_fusion.2), channel_id=1, source_target_pairs={{0,4},{2,6},{4,8},{6,10},{8,12},{10,14},{12,16},{14,18},{16,20},{1... | collective-permute-start | bytes 1572872 | tf_op jit(solution)/shard_map/ppermute | solution.py:235
  17.3 15.9 %collective-permute-start.3 = (bf16[512,256]{1,0:T(8,128)(2,1)}, bf16[512,256]{1,0:T(8,128)(2,1)}, u32[]{:S(2)}, u32[]{:S(2)}) collective-permute-start(bf16[512,256]{1,0:T(8,128)(2,1)} %get-tuple-element.3), channel_id=1, source_target_pairs={{0,8},{2,10},{4,12},{6,14},{8,16},{10,18},{12,20},{14,22},{16,24},... | collective-permute-start | bytes 786440 | tf_op jit(solution)/shard_map/ppermute | solution.py:239
  33.3 1.0 copy-start.3
  34.2 1.0 copy-start.4
  35.2 1.0 copy-start.5
  98.7 3.8 %collective-permute-start.4 = (f32[232,128]{1,0:T(8,128)S(1)}, f32[232,128]{1,0:T(8,128)S(1)}, u32[]{:S(2)}, u32[]{:S(2)}) collective-permute-start(f32[232,128]{1,0:T(8,128)S(1)} %reduce_sum.9), channel_id=1, source_target_pairs={{0,32},{32,0},{64,96},{96,64},{128,160},{160,128},{192,224},{224,1... | collective-permute-start | bytes 356360 | tf_op jit(solution)/shard_map/ppermute | solution.py:301
  102.4 9.3 %collective-permute-start.5 = (f32[232,128]{1,0:T(8,128)S(1)}, f32[232,128]{1,0:T(8,128)S(1)}, u32[]{:S(2)}, u32[]{:S(2)}) collective-permute-start(f32[232,128]{1,0:T(8,128)S(1)} %add.113), channel_id=1, source_target_pairs={{0,64},{32,96},{64,0},{96,32},{128,192},{160,224},{192,128},{224,1... | collective-permute-start | bytes 356360 | tf_op jit(solution)/shard_map/ppermute | solution.py:301
  111.8 10.9 %collective-permute-start.6 = (f32[232,128]{1,0:T(8,128)S(1)}, f32[232,128]{1,0:T(8,128)S(1)}, u32[]{:S(2)}, u32[]{:S(2)}) collective-permute-start(f32[232,128]{1,0:T(8,128)S(1)} %add.114), channel_id=1, source_target_pairs={{0,128},{32,160},{64,192},{96,224},{128,0},{160,32},{192,64},{224,... | collective-permute-start | bytes 356360 | tf_op jit(solution)/shard_map/ppermute | solution.py:301
  136.8 12.5 %collective-permute-start.7 = (f32[1792,128]{1,0:T(8,128)S(1)}, f32[1792,128]{1,0:T(8,128)S(1)}, u32[]{:S(2)}, u32[]{:S(2)}) collective-permute-start(f32[1792,128]{1,0:T(8,128)S(1)} %bitcast.12), channel_id=1, source_target_pairs={{0,2},{2,0},{1,3},{3,1},{4,6},{6,4},{5,7},{7,5},{8,10},{10,8},{9,1... | collective-permute-start | bytes 2752520 | tf_op jit(solution)/shard_map/ppermute | solution.py:213
  144.9 2.4 %collective-permute-start.8 = (f32[1,128]{1,0:T(1,128)S(1)}, f32[1,128]{1,0:T(1,128)S(1)}, u32[]{:S(2)}, u32[]{:S(2)}) collective-permute-start(f32[1,128]{1,0:T(1,128)S(1)} %slice.51), channel_id=1, source_target_pairs={{0,1},{1,0},{2,3},{3,2},{4,5},{5,4},{6,7},{7,6},{8,9},{9,8},{10,11... | collective-permute-start | bytes 1544 | tf_op jit(solution)/shard_map/ppermute | solution.py:213
  147.3 2.0 %collective-permute-start.9 = (f32[1,128]{1,0:T(1,128)S(1)}, f32[1,128]{1,0:T(1,128)S(1)}, u32[]{:S(2)}, u32[]{:S(2)}) collective-permute-start(f32[1,128]{1,0:T(1,128)S(1)} %slice_add_fusion), channel_id=1, source_target_pairs={{0,2},{2,0},{1,3},{3,1},{4,6},{6,4},{5,7},{7,5},{8,10},{10,8},{9,1... | collective-permute-start | bytes 1544 | tf_op jit(solution)/shard_map/ppermute | solution.py:213

commit v2 on v0

v2 whole, which is shorter than its diff:
```python
import math

import jax
import jax.numpy as jnp
from jax import lax
from jax.experimental import pallas as pl
from jax.experimental.pallas import tpu as pltpu
from jax.sharding import Mesh, PartitionSpec as P

HEADS = 32
KV_HEADS = 8
HEAD_DIM = 128
BLOCK = 64
CAND = 24
REACH = 4

ROWS = 8
SPAN = 24
CHIP_BLOCKS = 2 * ROWS
PADDED = 48
KV_HERE = 2
GROUP = HEADS // KV_HEADS
HEADS_HERE = KV_HERE * GROUP
Q_COLS = HEADS_HERE * HEAD_DIM
K_COLS = KV_HERE * HEAD_DIM
POOL = 3 * HEAD_DIM
WIDTH = GROUP * BLOCK
DUMMY = 31
SLOT_ROWS = 32
LANES = GROUP * CHIP_BLOCKS
SHARES = 8
KEY_ROWS = KV_HERE * POOL // SHARES
PART_ROWS = 2 * CHIP_BLOCKS + KEY_ROWS + 8
SUM_ROWS = HEAD_DIM + KEY_ROWS
UNROLL = 3
LOW = -1e30
EXP_SCALE = math.log2(math.e) / math.sqrt(HEAD_DIM)
HIGH = lax.Precision.HIGHEST


def dot_f32(a, b, dims):
    return lax.dot_general(
        a, b, (dims, ((), ())), precision=HIGH, preferred_element_type=jnp.float32
    )


def pool_keys(tile):
    wide = tile.astype(jnp.float32).reshape(ROWS, BLOCK, K_COLS)
    top = jnp.max(wide, axis=1)
    low = jnp.min(wide, axis=1)
    mean = jnp.sum(wide, axis=1) * (1.0 / BLOCK)
    return [
        jnp.concatenate(
            [v[:, g * HEAD_DIM:(g + 1) * HEAD_DIM] for v in (top, low, mean)], axis=1
        )
        for g in range(KV_HERE)
    ]


def enlist(groups_ref, work):
    def per_block(s, filled):
        def one(i, filled):
            work[filled] = s * CAND + i * 4
            return filled + 1
        return lax.fori_loop(0, groups_ref[s], one, filled)

    filled = lax.fori_loop(0, CHIP_BLOCKS, per_block, 0)
    spare = work[jnp.maximum(filled - 1, 0)]
    for extra in range(UNROLL - 1):
        work[filled + extra] = spare
    return filled


def position(core, s):
    return jnp.where(s < ROWS, ROWS * core + s, ROWS * (1 - core) + s - ROWS)


def slot_loop(filled, work, list_ref, tile_start, keys, queries, slot_max, slot_sum, diagonal):
    lane = lax.broadcasted_iota(jnp.int32, (BLOCK, WIDTH), 1) % BLOCK
    key_row = lax.broadcasted_iota(jnp.int32, (BLOCK, WIDTH), 0)

    @pl.loop(0, (filled + UNROLL - 1) // UNROLL)
    def _(step):
        found = []
        for e in range(UNROLL):
            first = work[step * UNROLL + e]
            s = first // CAND
            rows = [list_ref[first + i] for i in range(4)]
            starts = [pl.multiple_of(tile_start(s, row) * BLOCK, BLOCK) for row in rows]
            if diagonal:
                keep = key_row <= lane + jnp.where(first == s * CAND, 0, BLOCK)
            for g in range(KV_HERE):
                tiles = [
                    keys[pl.ds(start, BLOCK), g * HEAD_DIM:(g + 1) * HEAD_DIM] for start in starts
                ]
                scores = lax.dot_general(
                    jnp.concatenate(tiles, axis=0), queries[s * KV_HERE + g],
                    (((1,), (1,)), ((), ())), preferred_element_type=jnp.float32,
                )
                for i, row in enumerate(rows):
                    part = scores[i * BLOCK:(i + 1) * BLOCK, :]
                    if diagonal and i == 0:
                        part = jnp.where(keep, part, LOW)
                    top = jnp.max(part, axis=0, keepdims=True)
                    total = jnp.sum(
                        jnp.exp2((part - top) * EXP_SCALE), axis=0, keepdims=True
                    )
                    found.append((s * KV_HERE + g, row, top, total))
        for index, row, top, total in found:
            slot_max[index, pl.ds(row, 1), :] = top
            slot_sum[index, pl.ds(row, 1), :] = total


def near_kernel(
    core_ref, list_ref, groups_ref,
    q_own_ref, q_other_ref, k_own_ref, k_other_ref, wq_ref, wk_ref,
    queries, slot_max, slot_sum, pooled_query, gate_query, pooled_key, gate_key,
    keys, work,
):
    core = core_ref[0]
    half = ROWS * BLOCK
    for source, ref in ((core, k_own_ref), (1 - core, k_other_ref)):
        tile = ref[...]
        keys[pl.ds(pl.multiple_of(source * half, half), half), :] = tile
        for g, pooled in enumerate(pool_keys(tile)):
            pooled_key[g, pl.ds(pl.multiple_of(source * ROWS, ROWS), ROWS), :] = pooled

    def prepare(s, q_ref, at):
        for g in range(KV_HERE):
            for r in range(GROUP):
                head = g * GROUP + r
                tile = q_ref[pl.ds(at, BLOCK), head * HEAD_DIM:(head + 1) * HEAD_DIM]
                queries[s * KV_HERE + g, r * BLOCK:(r + 1) * BLOCK, :] = tile
                pooled_query[g, pl.ds(r * CHIP_BLOCKS + s, 1), :] = jnp.sum(
                    tile.astype(jnp.float32), axis=0, keepdims=True
                ) * (1.0 / BLOCK)

    for source in range(2):
        q_ref = (q_own_ref, q_other_ref)[source]

        @pl.loop(0, ROWS)
        def _(j):
            prepare(source * ROWS + j, q_ref, pl.multiple_of(j * BLOCK, BLOCK))

    slot_max[...] = jnp.full_like(slot_max, LOW)
    slot_sum[...] = jnp.zeros_like(slot_sum)
    filled = enlist(groups_ref, work)
    slot_loop(
        filled, work, list_ref,
        lambda s, row: position(core, s) + jnp.minimum(row, SPAN) - SPAN,
        keys, queries, slot_max, slot_sum, True,
    )
    for g in range(KV_HERE):
        gate_key[g] = dot_f32(pooled_key[g], wk_ref[g], ((1,), (0,)))
        for r in range(GROUP):
            picked = slice(r * CHIP_BLOCKS, (r + 1) * CHIP_BLOCKS)
            gate_query[g, picked, :] = dot_f32(
                pooled_query[g, picked, :], wq_ref[g * GROUP + r], ((1,), (0,))
            )


def far_kernel(
    core_ref, list_ref, groups_ref,
    k_prev_own_ref, k_prev_other_ref, k_far_ref, queries,
    max_ref, sum_ref, pooled_query, gate_query, near_key, near_gate_key, usable_ref, wk_ref,
    out_ref,
    keys, slot_max, slot_sum, pooled_key, shares, work,
):
    core = core_ref[0]
    half = ROWS * BLOCK
    for place, ref in ((0, k_far_ref), (1 + core, k_prev_own_ref), (2 - core, k_prev_other_ref)):
        tile = ref[...]
        at = place * half if isinstance(place, int) else pl.multiple_of(place * half, half)
        row = place * ROWS if isinstance(place, int) else pl.multiple_of(place * ROWS, ROWS)
        keys[pl.ds(at, half), :] = tile
        for g, pooled in enumerate(pool_keys(tile)):
            pooled_key[g, pl.ds(row, ROWS), :] = pooled
    for g in range(KV_HERE):
        pooled_key[g, SPAN:SPAN + CHIP_BLOCKS, :] = near_key[g]
    slot_max[...] = max_ref[...]
    slot_sum[...] = sum_ref[...]
    shares[...] = jnp.zeros_like(shares)

    filled = enlist(groups_ref, work)
    slot_loop(
        filled, work, list_ref,
        lambda s, row: jnp.where(row <= SPAN, position(core, s) + row, 0),
        keys, queries, slot_max, slot_sum, False,
    )

    live = lax.broadcasted_iota(jnp.int32, (SLOT_ROWS, WIDTH), 0) <= SPAN
    spread = jnp.where(
        lax.broadcasted_iota(jnp.int32, (WIDTH, LANES), 0) // BLOCK
        == lax.broadcasted_iota(jnp.int32, (WIDTH, LANES), 1) // CHIP_BLOCKS,
        1.0 / BLOCK, 0.0,
    ).astype(jnp.bfloat16)
    lane_block = lax.broadcasted_iota(jnp.int32, (SLOT_ROWS, LANES), 1) % CHIP_BLOCKS

    @pl.loop(0, CHIP_BLOCKS // 4)
    def _(step):
        found = []
        for e in range(4):
            s = step * 4 + e
            for g in range(KV_HERE):
                tops = jnp.where(live, slot_max[s * KV_HERE + g], LOW)
                top = jnp.max(tops, axis=0, keepdims=True)
                weight = jnp.where(
                    live, slot_sum[s * KV_HERE + g] * jnp.exp2((tops - top) * EXP_SCALE), 0.0
                )
                share = weight / jnp.sum(weight, axis=0, keepdims=True)
                coarse = share.astype(jnp.bfloat16)
                fine = (share - coarse.astype(jnp.float32)).astype(jnp.bfloat16)
                mean = (
                    jnp.dot(coarse, spread, preferred_element_type=jnp.float32)
                    + jnp.dot(fine, spread, preferred_element_type=jnp.float32)
                )
                found.append((g, position(core, s), jnp.where(lane_block == s, mean, 0.0)))
        for g, block, mine in found:
            shares[g, pl.ds(block, SLOT_ROWS), :] += mine

    scale = 1.0 / math.sqrt(HEAD_DIM)
    window = SPAN + CHIP_BLOCKS
    usable = usable_ref[...] > 0.0
    divergence = jnp.zeros((1, LANES), jnp.float32)
    key_base = 2 * CHIP_BLOCKS
    for g in range(KV_HERE):
        far_gate_key = dot_f32(pooled_key[g, 0:SPAN, :], wk_ref[g], ((1,), (0,)))
        gate_key = jnp.concatenate([far_gate_key, near_gate_key[g]], axis=0)
        logits = dot_f32(gate_key, gate_query[g], ((1,), (1,))) * scale
        logits = jnp.where(usable, logits, LOW)
        top = jnp.max(logits, axis=0, keepdims=True)
        weight = jnp.where(usable, jnp.exp(logits - top), 0.0)
        mass = jnp.sum(weight, axis=0, keepdims=True)
        log_gate = jnp.where(usable, logits - top - jnp.log(mass), 0.0)
        target = shares[g, 0:window, :]
        log_target = jnp.log(jnp.where(target > 0.0, target, 1.0))
        terms = jnp.where(usable, target * (log_target - log_gate), 0.0)
        divergence += jnp.sum(terms, axis=0, keepdims=True)
        target = jnp.where(usable, target, 0.0)
        slope = (weight / mass) * jnp.sum(target, axis=0, keepdims=True) - target
        slope = slope * (scale / 32.0)
        d_query = dot_f32(slope, gate_key, ((0,), (0,)))
        d_key = dot_f32(slope, gate_query[g], ((1,), (0,)))
        for r in range(GROUP):
            picked = slice(r * CHIP_BLOCKS, (r + 1) * CHIP_BLOCKS)
            out_ref[g * GROUP + r, 0:CHIP_BLOCKS, :] = pooled_query[g, picked, :]
            out_ref[g * GROUP + r, CHIP_BLOCKS:key_base, :] = d_query[picked, :]
        key_part = dot_f32(pooled_key[g], d_key, ((0,), (0,)))
        for i in range(SHARES // KV_HERE):
            out_ref[g * (SHARES // KV_HERE) + i, key_base:key_base + KEY_ROWS, :] = (
                key_part[i * KEY_ROWS:(i + 1) * KEY_ROWS, :]
            )
    total = jnp.sum(divergence)
    for i in range(SHARES):
        out_ref[i, PART_ROWS - 8:PART_ROWS, :] = jnp.full((8, HEAD_DIM), total, jnp.float32)


def sum_kernel(parts_ref, out_ref):
    parts = parts_ref[...]
    pooled = parts[:, 0:CHIP_BLOCKS, :].reshape(SHARES * CHIP_BLOCKS, HEAD_DIM)
    slope = parts[:, CHIP_BLOCKS:2 * CHIP_BLOCKS, :].reshape(SHARES * CHIP_BLOCKS, HEAD_DIM)
    out_ref[0:HEAD_DIM, :] = dot_f32(pooled, slope, ((0,), (0,)))
    out_ref[HEAD_DIM:, :] = jnp.sum(parts[:, 2 * CHIP_BLOCKS:, :], axis=0)


def swap(x, axis):
    return lax.ppermute(x, axis, [(0, 1), (1, 0)])


def whole(*shape):
    return pl.BlockSpec(shape, lambda i, *_: (0,) * len(shape))


def shaped(shape, dtype=jnp.float32):
    return jax.ShapeDtypeStruct(shape, dtype)


def near_call(core, slots, groups, q_own, q_other, k_own, k_other, wq, wk):
    half = ROWS * BLOCK
    outs = [
        shaped((CHIP_BLOCKS * KV_HERE, WIDTH, HEAD_DIM), jnp.bfloat16),
        shaped((CHIP_BLOCKS * KV_HERE, SLOT_ROWS, WIDTH)),
        shaped((CHIP_BLOCKS * KV_HERE, SLOT_ROWS, WIDTH)),
        shaped((KV_HERE, LANES, HEAD_DIM)),
        shaped((KV_HERE, LANES, HEAD_DIM)),
        shaped((KV_HERE, CHIP_BLOCKS, POOL)),
        shaped((KV_HERE, CHIP_BLOCKS, HEAD_DIM)),
    ]
    return pl.pallas_call(
        near_kernel,
        grid_spec=pltpu.PrefetchScalarGridSpec(
            num_scalar_prefetch=3,
            grid=(1,),
            in_specs=[
                pl.BlockSpec((half, Q_COLS), lambda i, c, *_: (0, c[0])),
                whole(half, Q_COLS),
                pl.BlockSpec((half, K_COLS), lambda i, c, *_: (0, c[0])),
                whole(half, K_COLS),
                whole(HEADS_HERE, HEAD_DIM, HEAD_DIM),
                whole(KV_HERE, POOL, HEAD_DIM),
            ],
            out_specs=[whole(*o.shape) for o in outs],
            scratch_shapes=[
                pltpu.VMEM((CHIP_BLOCKS * BLOCK, K_COLS), jnp.bfloat16),
                pltpu.SMEM((CHIP_BLOCKS * 6 + 8,), jnp.int32),
            ],
        ),
        out_shape=outs,
        compiler_params=pltpu.CompilerParams(vmem_limit_bytes=40 * 1024 * 1024),
        cost_estimate=pl.CostEstimate(
            flops=2_000_000_000, bytes_accessed=8_000_000, transcendentals=8_000_000
        ),
        name="near",
    )(core, slots, groups, q_own, q_other, k_own, k_other, wq, wk)


def far_call(core, slots, groups, k_prev_own, k_prev_other, k_far, near, hit, wk):
    half = ROWS * BLOCK
    queries, slot_max, slot_sum, pooled_query, gate_query, near_key, near_gate_key = near
    args = (
        k_prev_own, k_prev_other, k_far, queries, slot_max, slot_sum, pooled_query, gate_query,
        near_key, near_gate_key, hit, wk,
    )
    return pl.pallas_call(
        far_kernel,
        grid_spec=pltpu.PrefetchScalarGridSpec(
            num_scalar_prefetch=3,
            grid=(1,),
            in_specs=[whole(*a.shape) for a in args],
            out_specs=whole(SHARES, PART_ROWS, HEAD_DIM),
            scratch_shapes=[
                pltpu.VMEM((SPAN * BLOCK, K_COLS), jnp.bfloat16),
                pltpu.VMEM((CHIP_BLOCKS * KV_HERE, SLOT_ROWS, WIDTH), jnp.float32),
                pltpu.VMEM((CHIP_BLOCKS * KV_HERE, SLOT_ROWS, WIDTH), jnp.float32),
                pltpu.VMEM((KV_HERE, SPAN + CHIP_BLOCKS, POOL), jnp.float32),
                pltpu.VMEM((KV_HERE, PADDED, LANES), jnp.float32),
                pltpu.SMEM((CHIP_BLOCKS * 6 + 8,), jnp.int32),
            ],
        ),
        out_shape=shaped((SHARES, PART_ROWS, HEAD_DIM)),
        compiler_params=pltpu.CompilerParams(vmem_limit_bytes=40 * 1024 * 1024),
        cost_estimate=pl.CostEstimate(
            flops=2_000_000_000, bytes_accessed=8_000_000, transcendentals=8_000_000
        ),
        name="far",
    )(core, slots, groups, *args)


def pack_slots(picked, rho):
    slot = jnp.arange(CAND, dtype=jnp.int32)
    before = jnp.sum(
        jnp.where(picked[:, None, :] & (slot[None, None, :] < slot[None, :, None]), 1, 0), axis=2
    )
    here = picked[:, None, :] & (before[:, None, :] == slot[None, :, None])
    count = jnp.sum(picked.astype(jnp.int32), axis=1)
    packed = jnp.sum(jnp.where(here, rho[:, None, :], 0), axis=2)
    packed = jnp.where(slot[None, :] < count[:, None], packed, DUMMY)
    return packed.reshape(-1), (count + 3) // 4


def plan(core, chip, offsets, counts):
    step = jnp.arange(CHIP_BLOCKS, dtype=jnp.int32)
    block = jnp.where(step < ROWS, core * ROWS + step, (1 - core) * ROWS + step - ROWS)[:, None]
    key_block = chip * CHIP_BLOCKS + block - offsets
    usable = (jnp.arange(CAND, dtype=jnp.int32)[None, :] < counts[:, None]) & (key_block >= 0)
    rho = SPAN - offsets
    near = pack_slots(usable & (offsets <= block), rho)
    far = pack_slots(usable & (offsets > block), rho)
    place = jnp.where(usable, block + rho, -1)
    row = jnp.arange(SPAN + CHIP_BLOCKS, dtype=jnp.int32)[:, None, None]
    hit = jnp.any(place[None, :, :] == row, axis=2)
    return near, far, jnp.tile(hit.astype(jnp.float32), (1, GROUP))


def body(
    teacher_queries, teacher_keys, query_projection, key_projection, block_offsets, valid_counts
):
    chips = ("z", "yh", "x")
    places = ("z", "yh", "x", "core")
    count = lax.axis_size(places)
    core = lax.axis_index("core")
    chip = lax.axis_index(chips)
    half = ROWS * BLOCK

    k_mine = lax.dynamic_slice_in_dim(teacher_keys, core * K_COLS, K_COLS, 1)
    k_prev_own = lax.ppermute(k_mine, places, [(i, i + 2) for i in range(count - 2)])
    k_give = lax.dynamic_slice_in_dim(teacher_keys, (1 - core) * K_COLS, K_COLS, 1)
    k_prev_other = lax.ppermute(
        k_give, places, [(i, (i ^ 1) + 2) for i in range(count - 2)]
    )
    note = jnp.concatenate(
        [block_offsets, valid_counts[:, None], jnp.zeros((ROWS, K_COLS - CAND - 1), jnp.int32)], axis=1
    ).astype(jnp.bfloat16)
    note = jnp.concatenate([note, jnp.zeros_like(note)], axis=0)
    k_other = swap(jnp.concatenate([k_give, note], axis=0), "core")
    note_other = k_other[half:half + ROWS, :CAND + 1].astype(jnp.int32)
    k_other = k_other[:half]
    k_far = lax.ppermute(
        jnp.where(core == 1, k_mine, k_other), places, [(i, i + 4) for i in range(count - 4)]
    )
    q_other = swap(
        lax.dynamic_slice_in_dim(teacher_queries, (1 - core) * Q_COLS, Q_COLS, 1), "core"
    )

    offsets = jnp.concatenate([block_offsets, note_other[:, :CAND]], axis=0)
    counts = jnp.concatenate([valid_counts, note_other[:, CAND]], axis=0)
    near, far, hit = plan(core, chip, offsets, counts)
    wq = lax.dynamic_slice_in_dim(query_projection, core * HEADS_HERE, HEADS_HERE, 0)
    wk = lax.dynamic_slice_in_dim(key_projection, core * KV_HERE, KV_HERE, 0)
    index = core.reshape(1).astype(jnp.int32)
    near_out = near_call(index, *near, teacher_queries, q_other, teacher_keys, k_other, wq, wk)
    parts = far_call(index, *far, k_prev_own, k_prev_other, k_far, near_out, hit, wk)

    got = lax.all_to_all(parts, ("yh", "x"), 0, 0)
    got = pl.pallas_call(sum_kernel, out_shape=shaped((SUM_ROWS + 8, HEAD_DIM)), name="sum")(got)
    for step in (1, 2, 4):
        got = got + lax.ppermute(got, "z", [(i, i ^ step) for i in range(8)])
    total = got[SUM_ROWS:SUM_ROWS + 1, :]
    total = total + swap(total, "head")
    total = total + swap(total, "core")
    spread = jnp.broadcast_to(got[:SUM_ROWS], (SHARES, SUM_ROWS, HEAD_DIM))
    mine = lax.all_to_all(spread, ("yh", "x"), 0, 0)
    other = swap(mine, "core")
    first = jnp.where(core == 0, mine, other)
    second = jnp.where(core == 0, other, mine)
    both = jnp.concatenate([first, second], axis=0)
    query_gradient = both[:, :HEAD_DIM]
    key_gradient = both[:, HEAD_DIM:].reshape(2 * KV_HERE, POOL, HEAD_DIM)
    return query_gradient, key_gradient, total[0, 0] / (1024 * HEADS)


def solution(mesh):
    split = Mesh(mesh.devices.reshape(8, 2, 4, 2, 2), ("z", "yh", "x", "core", "head"))
    ctx = ("z", "yh", "x", "core")
    placed = (
        P(ctx, "head"),
        P(ctx, "head"),
        P("head", None, None),
        P("head", None, None),
        P(ctx, None),
        P(ctx),
    )
    return jax.shard_map(
        body,
        mesh=split,
        in_specs=placed,
        out_specs=(P("head", None, None), P("head", None, None), P()),
        check_vma=False,
    )
```

time: 1470 us -> 128 us (0.09)
  waiting for transfers between devices: 1180 us -> 9.47 us
  blocking collectives: 93.7 us -> 36.5 us
  other arithmetic: 61.9 us -> 15.9 us
  matrix products: 43 us -> 0 us
  local copies, waits for them, and re-layouts: 51.9 us -> 12.4 us
  starting transfers between devices: 13.4 us -> 35.2 us
  Pallas kernels: 0 us -> 16.1 us
    psum x1 -> x0, waiting for transfers between devices: 1170 us -> none  [body(): query_sum, key_sum = lax.psum((grads[0], grads[1]), 'ctx')]
    psum x1 -> x0, blocking collectives: 93.7 us -> none  [body(): kl_total = lax.psum(local_total, ('ctx', 'head'))]
    dot_general x15 -> x0, matrix products: 43 us -> none  [the longest x8 30.7 us: block_map(): jnp.einsum('tgrd,cugd->grtcu', query_block, cand_keys, preferred_element_...]
    all_to_all x0 -> x2, blocking collectives: none -> 36.5 us  [the longest x1 22.7 us: body(): got = lax.all_to_all(parts, ('yh', 'x'), 0, 0)]
    reduce_sum x20 -> x3, other arithmetic: 36.6 us -> 2.82 us  [the longest x1 1.26 us: pack_slots(): count = jnp.sum(picked.astype(jnp.int32), axis=1)]
    gather x9 -> x0, local copies, waits for them, and re-layouts: 26 us -> none  [the longest x8 25.1 us: one_block(): return block_map(query_block, window_blocks[index_row], offsets, usable_row)]
    ppermute x3 -> x11, starting transfers between devices: 13.4 us -> 35.2 us  [the longest x3 11.9 us: body(): got = got + lax.ppermute(got, 'z', [(i, i ^ step) for i in range(8)])]
    pallas_call x0 -> x3, Pallas kernels: none -> 16.1 us  [the longest x1 8.47 us: near_call(): pl.pallas_call(near_kernel, grid_spec=pltpu.PrefetchScalarGridSpec(num_sc...]
  transfers between devices with their start and end apart: 4 -> 11, of which waited for: 4 -> 5; matrix products, arithmetic and copies ran while one was open for 1% -> 16% of each run, Pallas kernels for 0% -> 7%
where the time goes in v2:
time: 128 us
  blocking collectives  36.5 us (29%)
  starting transfers between devices  35.2 us (28%)
  Pallas kernels  16.1 us (13%)
  other arithmetic  15.9 us (12%)
  local copies, waits for them, and re-layouts  12.4 us (10%)
  waiting for transfers between devices  9.47 us (7%)
  between operations  1.96 us (2%)
    all_to_all x1, blocking collectives, body(): got = lax.all_to_all(parts, ('yh', 'x'), 0, 0)  22.7 us
    all_to_all x1, blocking collectives, body(): mine = lax.all_to_all(spread, ('yh', 'x'), 0, 0)  13.8 us
    ppermute x3, starting transfers between devices, body(): got = got + lax.ppermute(got, 'z', [(i, i ^ step) for i in range(8)])  11.9 us
    ppermute x5, starting transfers between devices, swap(): return lax.ppermute(x, axis, [(0, 1), (1, 0)])  9.01 us
    pallas_call x1, Pallas kernels, near_call(): pl.pallas_call(near_kernel, grid_spec=pltpu.PrefetchScalarGridSpec(num_sc...  8.47 us
    ppermute x3, waiting for transfers between devices, body(): got = got + lax.ppermute(got, 'z', [(i, i ^ step) for i in range(8)])  7.53 us
    ppermute x1, starting transfers between devices, body(): lax.ppermute(jnp.where(core == 1, k_mine, k_other), places, [(i, i + 4) f...  5.99 us
    pallas_call x1, Pallas kernels, far_call(): pl.pallas_call(far_kernel, grid_spec=pltpu.PrefetchScalarGridSpec(num_sca...  5.65 us
  transfers between devices with their start and end apart: 11, of which 5 were waited for; matrix products, arithmetic and copies ran while one was open for 16% of the time, Pallas kernels for 7%

profile of v2, /device:TPU:1, one launch (start us, length us, event | category | flops | bytes accessed | tf_op | source)
XLA Modules:
  0.0 127.5 jit_solution(14292350102599150490)
XLA Ops:
  0.7 1.8 %constant_dynamic-slice_fusion.4 = bf16[512,256]{1,0:T(8,128)(2,1)} fusion(bf16[512,512]{1,0:T(8,128)(2,1)} %k_own_ref.1, s32[]{:T(128)S(6)} %select_n.90), kind=kLoop, calls=%fused_computation.42 | loop fusion | bytes 524292 | tf_op jit(solution)/shard_map/dynamic_slice | solution.py:387
  2.4 5.2 %collective-permute-start.2 = (bf16[512,256]{1,0:T(8,128)(2,1)}, bf16[512,256]{1,0:T(8,128)(2,1)}, u32[]{:S(2)}, u32[]{:S(2)}) collective-permute-start(bf16[512,256]{1,0:T(8,128)(2,1)} %constant_dynamic-slice_fusion.4), channel_id=1, source_target_pairs={{0,6},{2,4},{4,10},{6,8},{8,14},{10,12},{12,18},{14,16},{16,22},{1... | collective-permute-start | bytes 786440 | tf_op jit(solution)/shard_map/ppermute | solution.py:388
  9.1 1.8 %maximum_maximum_fusion = bf16[528,256]{1,0:T(8,128)(2,1)} fusion(bf16[8,231]{1,0:T(8,128)(2,1)S(1)} %broadcast_in_dim.69, bf16[8,1]{1,0:T(8,128)(2,1)S(1)} %copy.12, bf16[8,24]{1,0:T(8,128)(2,1)S(1)} %convert.9, bf16[512,256]{1,0:T(8,128)(2,1)} %constant_dynamic-slice_fusion.4, bf16[528]{0:T(1024)(128)(2,1)S(1)} %pad.10.clone), kind=kLoop, calls=%fused_computation.6 | loop fusion | flops 1351680 | bytes 537632 | tf_op jit(solution)/shard_map/concatenate | solution.py:395
  11.0 2.3 %constant_dynamic-slice_fusion.2 = bf16[512,1024]{1,0:T(8,128)(2,1)} fusion(bf16[512,2048]{1,0:T(8,128)(2,1)} %q_own_ref.1, s32[]{:T(128)S(6)} %select_n.105), kind=kLoop, calls=%fused_computation.40 | loop fusion | bytes 2097156 | tf_op jit(solution)/shard_map/dynamic_slice | solution.py:402
  17.4 1.3 convert_reduce_fusion.1
  20.4 2.0 %broadcast_select_fusion.2 = (bf16[512,256]{1,0:T(8,128)(2,1)}, bf16[512,256]{1,0:T(8,128)(2,1)}, bf16[512,256]{1,0:T(8,128)(2,1)}) fusion(pred[]{:T(512)S(6)} %eq.50, bf16[528,256]{1,0:T(8,128)(2,1)} %collective-permute-done, bf16[512,512]{1,0:T(8,128)(2,1)} %k_own_ref.1, s32[]{:T(128)S(6)} %select_n.97), kind=kLoop, calls=%fused_computation.7 | loop fusion | flops 131072 | bytes 1310725 | tf_op jit(solution)/shard_map/jit(_where)/select_n | solution.py:399
  22.3 3.1 %collective-permute-start.1 = (bf16[512,256]{1,0:T(8,128)(2,1)}, bf16[512,256]{1,0:T(8,128)(2,1)}, u32[]{:S(2)}, u32[]{:S(2)}) collective-permute-start(bf16[512,256]{1,0:T(8,128)(2,1)} %get-tuple-element.24), channel_id=1, source_target_pairs={{0,4},{2,6},{4,8},{6,10},{8,12},{10,14},{12,16},{14,18},{16,20},{1... | collective-permute-start | bytes 786440 | tf_op jit(solution)/shard_map/ppermute | solution.py:386
  25.4 6.0 %collective-permute-start.3 = (bf16[512,256]{1,0:T(8,128)(2,1)}, bf16[512,256]{1,0:T(8,128)(2,1)}, u32[]{:S(2)}, u32[]{:S(2)}) collective-permute-start(bf16[512,256]{1,0:T(8,128)(2,1)} %get-tuple-element.23), channel_id=1, source_target_pairs={{0,8},{2,10},{4,12},{6,14},{8,16},{10,18},{12,20},{14,22},{16,24},... | collective-permute-start | bytes 786440 | tf_op jit(solution)/shard_map/ppermute | solution.py:398
  31.4 1.4 %fusion.6 = s32[16,24]{1,0:T(8,128)} fusion(s32[16,24]{1,0:T(8,128)} %get-tuple-element.17, s32[16]{0:T(128)} %get-tuple-element.33), kind=kLoop, calls=%fused_computation.29 | loop fusion | flops 768 | bytes 3136 | tf_op jit(solution)/shard_map/jit(_where)/select_n | solution.py:357
  36.2 1.4 %copy.13.usable_ref = f32[40,64]{1,0:T(8,128)} copy(f32[40,64]{0,1:T(8,128)} %bitcast.9) | data formatting | bytes 20480 | tf_op jit(solution)/shard_map/tile | solution.py:372
  40.7 8.5 %near.1 = (bf16[32,256,128]{2,1,0:T(8,128)(2,1)S(1)}, f32[32,32,256]{2,1,0:T(8,128)S(1)}, f32[32,32,256]{2,1,0:T(8,128)S(1)}, f32[2,64,128]{2,1,0:T(8,128)S(1)},...) custom-call(s32[1]{0:T(128)} %bitcast.core_ref, s32[384]{0:T(512)S(1)} %select_n.103.list_ref, ...), custom_call_target="tpu_custom_call" | custom-call | flops 2000000000 | bytes 8000000 | tf_op jit(solution)/shard_map/near/pallas_call | solution.py:289
  49.2 5.7 %far.1 = f32[8,136,128]{2,1,0:T(8,128)S(1)} custom-call(s32[1]{0:T(128)} %bitcast.core_ref, s32[384]{0:T(512)S(1)} %select_n.95.list_ref, s32[16]{0:T(128)S(1)} %and_select_fusion.1.groups_ref, bf16[512,256]{1,0:T(8,128)(2,1)} %collective-permute-done.1.k_prev_own_ref, bf16[512,256]{1,0:T(8,128)(2,1)} %collective-permute-done.2.k_prev_other_ref, ...), custom_call_target="tpu_custom_call" | custom-call | flops 2000000000 | bytes 8000000 | tf_op jit(solution)/shard_map/far/pallas_call | solution.py:324
  54.8 22.7 %all_to_all.10.parts_ref = f32[8,136,128]{2,1,0:T(8,128)} all-to-all(f32[8,136,128]{2,1,0:T(8,128)S(1)} %far.1), channel_id=1, replica_groups=mesh['z'=8,'yh'=2,'x'=4,'core'=2,'head'=2] {'yh','x'}, dimensions={0} | all-to-all | bytes 1114112 | tf_op jit(solution)/shard_map/all_to_all | solution.py:414
  77.6 2.0 %sum.1 = f32[232,128]{1,0:T(8,128)} custom-call(f32[8,136,128]{2,1,0:T(8,128)} %all_to_all.10.parts_ref), custom_call_target="tpu_custom_call" | custom-call | tf_op jit(solution)/shard_map/sum/pallas_call | solution.py:415
  79.6 1.5 %collective-permute-start.5 = (f32[232,128]{1,0:T(8,128)}, f32[232,128]{1,0:T(8,128)S(1)}, u32[]{:S(2)}, u32[]{:S(2)}) collective-permute-start(f32[232,128]{1,0:T(8,128)} %sum.1), channel_id=1, source_target_pairs={{0,32},{32,0},{64,96},{96,64},{128,160},{160,128},{192,224},{224,1... | collective-permute-start | bytes 356360 | tf_op jit(solution)/shard_map/ppermute | solution.py:417
  81.1 2.4 %collective-permute-done.5 = f32[232,128]{1,0:T(8,128)S(1)} collective-permute-done((f32[232,128]{1,0:T(8,128)}, f32[232,128]{1,0:T(8,128)S(1)}, u32[]{:S(2)}, u32[]{:S(2)}) %collective-permute-start.5) | collective-permute-done | bytes 118816 | tf_op jit(solution)/shard_map/ppermute | solution.py:417
  84.4 5.0 %collective-permute-start.6 = (f32[232,128]{1,0:T(8,128)S(1)}, f32[232,128]{1,0:T(8,128)S(1)}, u32[]{:S(2)}, u32[]{:S(2)}) collective-permute-start(f32[232,128]{1,0:T(8,128)S(1)} %add.115), channel_id=1, source_target_pairs={{0,64},{32,96},{64,0},{96,32},{128,192},{160,224},{192,128},{224,1... | collective-permute-start | bytes 356360 | tf_op jit(solution)/shard_map/ppermute | solution.py:417
  89.4 2.2 %collective-permute-done.6 = f32[232,128]{1,0:T(8,128)S(1)} collective-permute-done((f32[232,128]{1,0:T(8,128)S(1)}, f32[232,128]{1,0:T(8,128)S(1)}, u32[]{:S(2)}, u32[]{:S(2)}) %collective-permute-start.6) | collective-permute-done | bytes 118816 | tf_op jit(solution)/shard_map/ppermute | solution.py:417
  91.7 5.4 %collective-permute-start.7 = (f32[232,128]{1,0:T(8,128)S(1)}, f32[232,128]{1,0:T(8,128)S(1)}, u32[]{:S(2)}, u32[]{:S(2)}) collective-permute-start(f32[232,128]{1,0:T(8,128)S(1)} %add.116), channel_id=1, source_target_pairs={{0,128},{32,160},{64,192},{96,224},{128,0},{160,32},{192,64},{224,... | collective-permute-start | bytes 356360 | tf_op jit(solution)/shard_map/ppermute | solution.py:417
  97.1 2.9 %collective-permute-done.7 = f32[232,128]{1,0:T(8,128)S(1)} collective-permute-done((f32[232,128]{1,0:T(8,128)S(1)}, f32[232,128]{1,0:T(8,128)S(1)}, u32[]{:S(2)}, u32[]{:S(2)}) %collective-permute-start.7) | collective-permute-done | bytes 118816 | tf_op jit(solution)/shard_map/ppermute | solution.py:417
  100.0 13.8 %all_to_all.11 = f32[8,224,128]{2,1,0:T(8,128)S(1)} all-to-all(f32[8,224,128]{2,1,0:T(8,128)S(1)} %broadcast_in_dim.76), channel_id=1, replica_groups=mesh['z'=8,'yh'=2,'x'=4,'core'=2,'head'=2] {'yh','x'}, dimensions={0} | all-to-all | bytes 1835008 | tf_op jit(solution)/shard_map/all_to_all | solution.py:422
  113.8 6.0 %collective-permute-start.8 = (f32[8,224,128]{2,1,0:T(8,128)S(1)}, f32[8,224,128]{2,1,0:T(8,128)S(1)}, u32[]{:S(2)}, u32[]{:S(2)}) collective-permute-start(f32[8,224,128]{2,1,0:T(8,128)S(1)} %all_to_all.11), channel_id=1, source_target_pairs={{0,2},{2,0},{1,3},{3,1},{4,6},{6,4},{5,7},{7,5},{8,10},{10,8},{9,1... | collective-permute-start | bytes 2752520 | tf_op jit(solution)/shard_map/ppermute | solution.py:267
  119.9 1.3 %collective-permute-start.9 = (f32[1,128]{1,0:T(1,128)S(1)}, f32[1,128]{1,0:T(1,128)S(1)}, u32[]{:S(2)}, u32[]{:S(2)}) collective-permute-start(f32[1,128]{1,0:T(1,128)S(1)} %slice.41), channel_id=1, source_target_pairs={{0,1},{1,0},{2,3},{3,2},{4,5},{5,4},{6,7},{7,6},{8,9},{9,8},{10,11... | collective-permute-start | bytes 1544 | tf_op jit(solution)/shard_map/ppermute | solution.py:267
  122.2 1.2 collective-permute-start.10
  (60 shorter events, 18.9 us)
Async XLA Ops:
  0.6 14.3 %copy-start = (f32[16,128,128]{2,1,0:T(8,128)S(1)}, f32[16,128,128]{2,1,0:T(8,128)}, u32[]{:S(2)}) copy-start(f32[16,128,128]{2,1,0:T(8,128)} %param.8) | copy-start | bytes 3145732
  2.4 46.7 %collective-permute-start.2 = (bf16[512,256]{1,0:T(8,128)(2,1)}, bf16[512,256]{1,0:T(8,128)(2,1)}, u32[]{:S(2)}, u32[]{:S(2)}) collective-permute-start(bf16[512,256]{1,0:T(8,128)(2,1)} %constant_dynamic-slice_fusion.4), channel_id=1, source_target_pairs={{0,6},{2,4},{4,10},{6,8},{8,14},{10,12},{12,18},{14,16},{16,22},{1... | collective-permute-start | bytes 786440 | tf_op jit(solution)/shard_map/ppermute | solution.py:388
  11.0 6.4 %copy-start.6 = (s32[8,24]{1,0:T(8,128)S(1)}, s32[8,24]{1,0:T(8,128)}, u32[]{:S(2)}) copy-start(s32[8,24]{1,0:T(8,128)} %param.10) | copy-start | bytes 2308
  11.0 4.8 %collective-permute-start = (bf16[528,256]{1,0:T(8,128)(2,1)}, bf16[528,256]{1,0:T(8,128)(2,1)}, u32[]{:S(2)}, u32[]{:S(2)}) collective-permute-start(bf16[528,256]{1,0:T(8,128)(2,1)} %maximum_maximum_fusion), channel_id=1, source_target_pairs={{0,2},{2,0},{1,3},{3,1},{4,6},{6,4},{5,7},{7,5},{8,10},{10,8},{9,1... | collective-permute-start | bytes 811016 | tf_op jit(solution)/shard_map/ppermute | solution.py:267
  13.3 24.4 %copy-start.1 = (bf16[512,2048]{1,0:T(8,128)(2,1)S(1)}, bf16[512,2048]{1,0:T(8,128)(2,1)}, u32[]{:S(2)}) copy-start(bf16[512,2048]{1,0:T(8,128)(2,1)} %q_own_ref.1) | copy-start | bytes 6291460
  13.3 24.4 %collective-permute-start.4 = (bf16[512,1024]{1,0:T(8,128)(2,1)}, bf16[512,1024]{1,0:T(8,128)(2,1)}, u32[]{:S(2)}, u32[]{:S(2)}) collective-permute-start(bf16[512,1024]{1,0:T(8,128)(2,1)} %constant_dynamic-slice_fusion.2), channel_id=1, source_target_pairs={{0,2},{2,0},{1,3},{3,1},{4,6},{6,4},{5,7},{7,5},{8,10},{10,8},{9,1... | collective-permute-start | bytes 3145736 | tf_op jit(solution)/shard_map/ppermute | solution.py:267
  18.6 1.6 %copy-start.7 = (s32[16]{0:T(128)}, s32[16]{0:T(128)S(1)}, u32[]{:S(2)}) copy-start(s32[16]{0:T(128)S(1)} %get-tuple-element.25) | copy-start | bytes 196
  22.3 26.8 %collective-permute-start.1 = (bf16[512,256]{1,0:T(8,128)(2,1)}, bf16[512,256]{1,0:T(8,128)(2,1)}, u32[]{:S(2)}, u32[]{:S(2)}) collective-permute-start(bf16[512,256]{1,0:T(8,128)(2,1)} %get-tuple-element.24), channel_id=1, source_target_pairs={{0,4},{2,6},{4,8},{6,10},{8,12},{10,14},{12,16},{14,18},{16,20},{1... | collective-permute-start | bytes 786440 | tf_op jit(solution)/shard_map/ppermute | solution.py:386
  25.4 23.7 %collective-permute-start.3 = (bf16[512,256]{1,0:T(8,128)(2,1)}, bf16[512,256]{1,0:T(8,128)(2,1)}, u32[]{:S(2)}, u32[]{:S(2)}) collective-permute-start(bf16[512,256]{1,0:T(8,128)(2,1)} %get-tuple-element.23), channel_id=1, source_target_pairs={{0,8},{2,10},{4,12},{6,14},{8,16},{10,18},{12,20},{14,22},{16,24},... | collective-permute-start | bytes 786440 | tf_op jit(solution)/shard_map/ppermute | solution.py:398
  37.6 1.0 copy-start.2
  38.7 1.0 copy-start.3
  39.7 0.9 copy-start.4
  40.7 8.5 %copy-start.5 = (f32[40,64]{1,0:T(8,128)S(1)}, f32[40,64]{1,0:T(8,128)}, u32[]{:S(2)}) copy-start(f32[40,64]{1,0:T(8,128)} %copy.13.usable_ref) | copy-start | bytes 30724
  79.6 4.0 %collective-permute-start.5 = (f32[232,128]{1,0:T(8,128)}, f32[232,128]{1,0:T(8,128)S(1)}, u32[]{:S(2)}, u32[]{:S(2)}) collective-permute-start(f32[232,128]{1,0:T(8,128)} %sum.1), channel_id=1, source_target_pairs={{0,32},{32,0},{64,96},{96,64},{128,160},{160,128},{192,224},{224,1... | collective-permute-start | bytes 356360 | tf_op jit(solution)/shard_map/ppermute | solution.py:417
  84.4 7.2 %collective-permute-start.6 = (f32[232,128]{1,0:T(8,128)S(1)}, f32[232,128]{1,0:T(8,128)S(1)}, u32[]{:S(2)}, u32[]{:S(2)}) collective-permute-start(f32[232,128]{1,0:T(8,128)S(1)} %add.115), channel_id=1, source_target_pairs={{0,64},{32,96},{64,0},{96,32},{128,192},{160,224},{192,128},{224,1... | collective-permute-start | bytes 356360 | tf_op jit(solution)/shard_map/ppermute | solution.py:417
  91.7 8.3 %collective-permute-start.7 = (f32[232,128]{1,0:T(8,128)S(1)}, f32[232,128]{1,0:T(8,128)S(1)}, u32[]{:S(2)}, u32[]{:S(2)}) collective-permute-start(f32[232,128]{1,0:T(8,128)S(1)} %add.116), channel_id=1, source_target_pairs={{0,128},{32,160},{64,192},{96,224},{128,0},{160,32},{192,64},{224,... | collective-permute-start | bytes 356360 | tf_op jit(solution)/shard_map/ppermute | solution.py:417
  113.8 10.5 %collective-permute-start.8 = (f32[8,224,128]{2,1,0:T(8,128)S(1)}, f32[8,224,128]{2,1,0:T(8,128)S(1)}, u32[]{:S(2)}, u32[]{:S(2)}) collective-permute-start(f32[8,224,128]{2,1,0:T(8,128)S(1)} %all_to_all.11), channel_id=1, source_target_pairs={{0,2},{2,0},{1,3},{3,1},{4,6},{6,4},{5,7},{7,5},{8,10},{10,8},{9,1... | collective-permute-start | bytes 2752520 | tf_op jit(solution)/shard_map/ppermute | solution.py:267
  119.9 2.4 %collective-permute-start.9 = (f32[1,128]{1,0:T(1,128)S(1)}, f32[1,128]{1,0:T(1,128)S(1)}, u32[]{:S(2)}, u32[]{:S(2)}) collective-permute-start(f32[1,128]{1,0:T(1,128)S(1)} %slice.41), channel_id=1, source_target_pairs={{0,1},{1,0},{2,3},{3,2},{4,5},{5,4},{6,7},{7,6},{8,9},{9,8},{10,11... | collective-permute-start | bytes 1544 | tf_op jit(solution)/shard_map/ppermute | solution.py:267
  122.2 2.0 %collective-permute-start.10 = (f32[1,128]{1,0:T(1,128)S(1)}, f32[1,128]{1,0:T(1,128)S(1)}, u32[]{:S(2)}, u32[]{:S(2)}) collective-permute-start(f32[1,128]{1,0:T(1,128)S(1)} %slice_add_fusion), channel_id=1, source_target_pairs={{0,2},{2,0},{1,3},{3,1},{4,6},{6,4},{5,7},{7,5},{8,10},{10,8},{9,1... | collective-permute-start | bytes 1544 | tf_op jit(solution)/shard_map/ppermute | solution.py:267

commit v3 on v2

--- a/solution.py
+++ b/solution.py
@@ -28,11 +28,15 @@
 DUMMY = 31
 SLOT_ROWS = 32
 LANES = GROUP * CHIP_BLOCKS
-SHARES = 8
+SHARES = 16
 KEY_ROWS = KV_HERE * POOL // SHARES
-PART_ROWS = 2 * CHIP_BLOCKS + KEY_ROWS + 8
-SUM_ROWS = HEAD_DIM + KEY_ROWS
+HALF_HEAD = HEAD_DIM // 2
+PART_ROWS = CHIP_BLOCKS + ROWS + KEY_ROWS + 8
+SUM_ROWS = HALF_HEAD + KEY_ROWS
+VMEM_BYTES = 56 * 1024 * 1024
 UNROLL = 3
+LIST_SIZE = CHIP_BLOCKS * CAND + 8
+WORK_SIZE = CHIP_BLOCKS * CAND // 4 + 8
 LOW = -1e30
 EXP_SCALE = math.log2(math.e) / math.sqrt(HEAD_DIM)
 HIGH = lax.Precision.HIGHEST
@@ -57,17 +61,45 @@
     ]
 
 
-def enlist(groups_ref, work):
-    def per_block(s, filled):
-        def one(i, filled):
-            work[filled] = s * CAND + i * 4
-            return filled + 1
-        return lax.fori_loop(0, groups_ref[s], one, filled)
-
-    filled = lax.fori_loop(0, CHIP_BLOCKS, per_block, 0)
-    spare = work[jnp.maximum(filled - 1, 0)]
-    for extra in range(UNROLL - 1):
-        work[filled + extra] = spare
+def make_lists(core, chip, tables, near_list, near_work, far_list, far_work):
+    limit_base = chip * CHIP_BLOCKS
+    filled = (jnp.int32(0), jnp.int32(0))
+    for source, (offsets_ref, counts_ref) in enumerate(tables):
+        first = ROWS * core if source == 0 else ROWS * (1 - core)
+
+        def per_block(j, filled):
+            block = first + j
+            base = (source * ROWS + j) * CAND
+
+            def per_slot(c, ends):
+                near_end, far_end = ends
+                offset = offsets_ref[j, c]
+                near = offset <= block
+                far = (offset > block) & (offset <= limit_base + block)
+                near_list[near_end] = SPAN - offset
+                far_list[far_end] = SPAN - offset
+                return near_end + near.astype(jnp.int32), far_end + far.astype(jnp.int32)
+
+            ends = lax.fori_loop(0, counts_ref[j], per_slot, (base, base))
+            out = []
+            for end, slots, work, total in zip(
+                ends, (near_list, far_list), (near_work, far_work), filled
+            ):
+                for extra in range(3):
+                    slots[end + extra] = DUMMY
+
+                def add(i, total):
+                    work[total] = base + i * 4
+                    return total + 1
+
+                out.append(lax.fori_loop(0, (end - base + 3) // 4, add, total))
+            return tuple(out)
+
+        filled = lax.fori_loop(0, ROWS, per_block, filled)
+    for work, total in zip((near_work, far_work), filled):
+        spare = work[jnp.maximum(total - 1, 0)]
+        for extra in range(UNROLL - 1):
+            work[total + extra] = spare
     return filled
 
 
@@ -112,11 +144,13 @@
 
 
 def near_kernel(
-    core_ref, list_ref, groups_ref,
+    place_ref, offsets_own_ref, counts_own_ref, offsets_other_ref, counts_other_ref,
     q_own_ref, q_other_ref, k_own_ref, k_other_ref, wq_ref, wk_ref,
     queries, slot_max, slot_sum, pooled_query, gate_query, pooled_key, gate_key,
-    keys, work,
+    far_list, far_work, far_filled,
+    keys, near_list, near_work,
 ):
+    core_ref = place_ref
     core = core_ref[0]
     half = ROWS * BLOCK
     for source, ref in ((core, k_own_ref), (1 - core, k_other_ref)):
@@ -144,9 +178,14 @@
 
     slot_max[...] = jnp.full_like(slot_max, LOW)
     slot_sum[...] = jnp.zeros_like(slot_sum)
-    filled = enlist(groups_ref, work)
+    filled, filled_far = make_lists(
+        core, place_ref[1],
+        ((offsets_own_ref, counts_own_ref), (offsets_other_ref, counts_other_ref)),
+        near_list, near_work, far_list, far_work,
+    )
+    far_filled[0] = filled_far
     slot_loop(
-        filled, work, list_ref,
+        filled, near_work, near_list,
         lambda s, row: position(core, s) + jnp.minimum(row, SPAN) - SPAN,
         keys, queries, slot_max, slot_sum, True,
     )
@@ -160,11 +199,11 @@
 
 
 def far_kernel(
-    core_ref, list_ref, groups_ref,
+    core_ref, far_list, far_work, far_filled,
     k_prev_own_ref, k_prev_other_ref, k_far_ref, queries,
-    max_ref, sum_ref, pooled_query, gate_query, near_key, near_gate_key, usable_ref, wk_ref,
+    max_ref, sum_ref, pooled_query, gate_query, near_key, near_gate_key, wk_ref,
     out_ref,
-    keys, slot_max, slot_sum, pooled_key, shares, work,
+    keys, slot_max, slot_sum, pooled_key, shares, hits,
 ):
     core = core_ref[0]
     half = ROWS * BLOCK
@@ -180,10 +219,9 @@
     slot_max[...] = max_ref[...]
     slot_sum[...] = sum_ref[...]
     shares[...] = jnp.zeros_like(shares)
-
-    filled = enlist(groups_ref, work)
+    hits[...] = jnp.zeros_like(hits)
     slot_loop(
-        filled, work, list_ref,
+        far_filled[0], far_work, far_list,
         lambda s, row: jnp.where(row <= SPAN, position(core, s) + row, 0),
         keys, queries, slot_max, slot_sum, False,
     )
@@ -214,15 +252,19 @@
                     jnp.dot(coarse, spread, preferred_element_type=jnp.float32)
                     + jnp.dot(fine, spread, preferred_element_type=jnp.float32)
                 )
-                found.append((g, position(core, s), jnp.where(lane_block == s, mean, 0.0)))
-        for g, block, mine in found:
-            shares[g, pl.ds(block, SLOT_ROWS), :] += mine
+                found.append((shares.at[g], position(core, s), jnp.where(lane_block == s, mean, 0.0)))
+                if g == 0:
+                    filled = jnp.where(tops > 0.5 * LOW, 1.0, 0.0).astype(jnp.bfloat16)
+                    hit = jnp.dot(filled, spread, preferred_element_type=jnp.float32)
+                    found.append((hits, position(core, s), jnp.where(lane_block == s, hit, 0.0)))
+        for table, block, mine in found:
+            table[pl.ds(block, SLOT_ROWS), :] += mine
 
     scale = 1.0 / math.sqrt(HEAD_DIM)
     window = SPAN + CHIP_BLOCKS
-    usable = usable_ref[...] > 0.0
+    usable = hits[0:window, :] > 0.5
     divergence = jnp.zeros((1, LANES), jnp.float32)
-    key_base = 2 * CHIP_BLOCKS
+    key_base = CHIP_BLOCKS + ROWS
     for g in range(KV_HERE):
         far_gate_key = dot_f32(pooled_key[g, 0:SPAN, :], wk_ref[g], ((1,), (0,)))
         gate_key = jnp.concatenate([far_gate_key, near_gate_key[g]], axis=0)
@@ -242,9 +284,15 @@
         d_query = dot_f32(slope, gate_key, ((0,), (0,)))
         d_key = dot_f32(slope, gate_query[g], ((1,), (0,)))
         for r in range(GROUP):
-            picked = slice(r * CHIP_BLOCKS, (r + 1) * CHIP_BLOCKS)
-            out_ref[g * GROUP + r, 0:CHIP_BLOCKS, :] = pooled_query[g, picked, :]
-            out_ref[g * GROUP + r, CHIP_BLOCKS:key_base, :] = d_query[picked, :]
+            at = r * CHIP_BLOCKS
+            pooled = pooled_query[g, at:at + CHIP_BLOCKS, :]
+            for part in range(2):
+                share = (g * GROUP + r) * 2 + part
+                cols = slice(part * HALF_HEAD, (part + 1) * HALF_HEAD)
+                out_ref[share, 0:CHIP_BLOCKS, :] = d_query[at:at + CHIP_BLOCKS, :]
+                out_ref[share, CHIP_BLOCKS:key_base, :] = jnp.concatenate(
+                    [pooled[0:ROWS, cols], pooled[ROWS:CHIP_BLOCKS, cols]], axis=1
+                )
         key_part = dot_f32(pooled_key[g], d_key, ((0,), (0,)))
         for i in range(SHARES // KV_HERE):
             out_ref[g * (SHARES // KV_HERE) + i, key_base:key_base + KEY_ROWS, :] = (
@@ -257,10 +305,47 @@
 
 def sum_kernel(parts_ref, out_ref):
     parts = parts_ref[...]
-    pooled = parts[:, 0:CHIP_BLOCKS, :].reshape(SHARES * CHIP_BLOCKS, HEAD_DIM)
-    slope = parts[:, CHIP_BLOCKS:2 * CHIP_BLOCKS, :].reshape(SHARES * CHIP_BLOCKS, HEAD_DIM)
-    out_ref[0:HEAD_DIM, :] = dot_f32(pooled, slope, ((0,), (0,)))
-    out_ref[HEAD_DIM:, :] = jnp.sum(parts[:, 2 * CHIP_BLOCKS:, :], axis=0)
+    pooled = parts[:, CHIP_BLOCKS:CHIP_BLOCKS + ROWS, :].reshape(SHARES * ROWS, HEAD_DIM)
+    early = parts[:, 0:ROWS, :].reshape(SHARES * ROWS, HEAD_DIM)
+    late = parts[:, ROWS:CHIP_BLOCKS, :].reshape(SHARES * ROWS, HEAD_DIM)
+    out_ref[0:HALF_HEAD, :] = (
+        dot_f32(pooled[:, :HALF_HEAD], early, ((0,), (0,)))
+        + dot_f32(pooled[:, HALF_HEAD:], late, ((0,), (0,)))
+    )
+    out_ref[HALF_HEAD:, :] = jnp.sum(parts[:, CHIP_BLOCKS + ROWS:, :], axis=0)
+
+
+def cut_keys_kernel(core_ref, keys_ref, mine_ref, give_ref, sems):
+    at = pl.multiple_of(core_ref[0] * K_COLS, K_COLS)
+    other = pl.multiple_of((1 - core_ref[0]) * K_COLS, K_COLS)
+    mine = pltpu.make_async_copy(keys_ref.at[:, pl.ds(at, K_COLS)], mine_ref, sems.at[0])
+    give = pltpu.make_async_copy(keys_ref.at[:, pl.ds(other, K_COLS)], give_ref, sems.at[1])
+    mine.start()
+    give.start()
+    mine.wait()
+    give.wait()
+
+
+def cut_queries_kernel(core_ref, queries_ref, give_ref, sems):
+    other = pl.multiple_of((1 - core_ref[0]) * Q_COLS, Q_COLS)
+    give = pltpu.make_async_copy(queries_ref.at[:, pl.ds(other, Q_COLS)], give_ref, sems.at[0])
+    give.start()
+    give.wait()
+
+
+def cut(kernel, core, whole_array, outs, name):
+    return pl.pallas_call(
+        kernel,
+        grid_spec=pltpu.PrefetchScalarGridSpec(
+            num_scalar_prefetch=1,
+            grid=(1,),
+            in_specs=[pl.BlockSpec(memory_space=pl.ANY)],
+            out_specs=[pl.BlockSpec(memory_space=pl.ANY)] * len(outs),
+            scratch_shapes=[pltpu.SemaphoreType.DMA((2,))],
+        ),
+        out_shape=outs,
+        name=name,
+    )(core, whole_array)
 
 
 def swap(x, axis):
@@ -275,7 +360,11 @@
     return jax.ShapeDtypeStruct(shape, dtype)
 
 
-def near_call(core, slots, groups, q_own, q_other, k_own, k_other, wq, wk):
+def smem():
+    return pl.BlockSpec(memory_space=pltpu.SMEM)
+
+
+def near_call(place, tables, q_own, q_other, k_mine, k_other, wq, wk):
     half = ROWS * BLOCK
     outs = [
         shaped((CHIP_BLOCKS * KV_HERE, WIDTH, HEAD_DIM), jnp.bfloat16),
@@ -286,47 +375,46 @@
         shaped((KV_HERE, CHIP_BLOCKS, POOL)),
         shaped((KV_HERE, CHIP_BLOCKS, HEAD_DIM)),
     ]
+    lists = [LIST_SIZE, WORK_SIZE, 1]
     return pl.pallas_call(
         near_kernel,
         grid_spec=pltpu.PrefetchScalarGridSpec(
-            num_scalar_prefetch=3,
+            num_scalar_prefetch=1,
             grid=(1,),
-            in_specs=[
-                pl.BlockSpec((half, Q_COLS), lambda i, c, *_: (0, c[0])),
+            in_specs=[smem()] * 4 + [
+                pl.BlockSpec((half, Q_COLS), lambda i, c: (0, c[0])),
                 whole(half, Q_COLS),
-                pl.BlockSpec((half, K_COLS), lambda i, c, *_: (0, c[0])),
                 whole(half, K_COLS),
-                whole(HEADS_HERE, HEAD_DIM, HEAD_DIM),
-                whole(KV_HERE, POOL, HEAD_DIM),
+                whole(half, K_COLS),
+                pl.BlockSpec((HEADS_HERE, HEAD_DIM, HEAD_DIM), lambda i, c: (c[0], 0, 0)),
+                pl.BlockSpec((KV_HERE, POOL, HEAD_DIM), lambda i, c: (c[0], 0, 0)),
             ],
-            out_specs=[whole(*o.shape) for o in outs],
+            out_specs=[whole(*o.shape) for o in outs] + [smem()] * 3,
             scratch_shapes=[
                 pltpu.VMEM((CHIP_BLOCKS * BLOCK, K_COLS), jnp.bfloat16),
-                pltpu.SMEM((CHIP_BLOCKS * 6 + 8,), jnp.int32),
+                pltpu.SMEM((LIST_SIZE,), jnp.int32),
+                pltpu.SMEM((WORK_SIZE,), jnp.int32),
             ],
         ),
-        out_shape=outs,
-        compiler_params=pltpu.CompilerParams(vmem_limit_bytes=40 * 1024 * 1024),
+        out_shape=outs + [shaped((n,), jnp.int32) for n in lists],
+        compiler_params=pltpu.CompilerParams(vmem_limit_bytes=VMEM_BYTES),
         cost_estimate=pl.CostEstimate(
             flops=2_000_000_000, bytes_accessed=8_000_000, transcendentals=8_000_000
         ),
         name="near",
-    )(core, slots, groups, q_own, q_other, k_own, k_other, wq, wk)
-
-
-def far_call(core, slots, groups, k_prev_own, k_prev_other, k_far, near, hit, wk):
-    half = ROWS * BLOCK
-    queries, slot_max, slot_sum, pooled_query, gate_query, near_key, near_gate_key = near
-    args = (
-        k_prev_own, k_prev_other, k_far, queries, slot_max, slot_sum, pooled_query, gate_query,
-        near_key, near_gate_key, hit, wk,
-    )
+    )(place, *tables, q_own, q_other, k_mine, k_other, wq, wk)
+
+
+def far_call(place, k_prev_own, k_prev_other, k_far, near, wk):
+    args = (k_prev_own, k_prev_other, k_far, *near[:-3])
     return pl.pallas_call(
         far_kernel,
         grid_spec=pltpu.PrefetchScalarGridSpec(
-            num_scalar_prefetch=3,
+            num_scalar_prefetch=1,
             grid=(1,),
-            in_specs=[whole(*a.shape) for a in args],
+            in_specs=[smem()] * 3 + [whole(*a.shape) for a in args] + [
+                pl.BlockSpec((KV_HERE, POOL, HEAD_DIM), lambda i, c: (c[0], 0, 0)),
+            ],
             out_specs=whole(SHARES, PART_ROWS, HEAD_DIM),
             scratch_shapes=[
                 pltpu.VMEM((SPAN * BLOCK, K_COLS), jnp.bfloat16),
@@ -334,104 +422,73 @@
                 pltpu.VMEM((CHIP_BLOCKS * KV_HERE, SLOT_ROWS, WIDTH), jnp.float32),
                 pltpu.VMEM((KV_HERE, SPAN + CHIP_BLOCKS, POOL), jnp.float32),
                 pltpu.VMEM((KV_HERE, PADDED, LANES), jnp.float32),
-                pltpu.SMEM((CHIP_BLOCKS * 6 + 8,), jnp.int32),
+                pltpu.VMEM((PADDED, LANES), jnp.float32),
             ],
         ),
         out_shape=shaped((SHARES, PART_ROWS, HEAD_DIM)),
-        compiler_params=pltpu.CompilerParams(vmem_limit_bytes=40 * 1024 * 1024),
+        compiler_params=pltpu.CompilerParams(vmem_limit_bytes=VMEM_BYTES),
         cost_estimate=pl.CostEstimate(
             flops=2_000_000_000, bytes_accessed=8_000_000, transcendentals=8_000_000
         ),
         name="far",
-    )(core, slots, groups, *args)
-
-
-def pack_slots(picked, rho):
-    slot = jnp.arange(CAND, dtype=jnp.int32)
-    before = jnp.sum(
-        jnp.where(picked[:, None, :] & (slot[None, None, :] < slot[None, :, None]), 1, 0), axis=2
-    )
-    here = picked[:, None, :] & (before[:, None, :] == slot[None, :, None])
-    count = jnp.sum(picked.astype(jnp.int32), axis=1)
-    packed = jnp.sum(jnp.where(here, rho[:, None, :], 0), axis=2)
-    packed = jnp.where(slot[None, :] < count[:, None], packed, DUMMY)
-    return packed.reshape(-1), (count + 3) // 4
-
-
-def plan(core, chip, offsets, counts):
-    step = jnp.arange(CHIP_BLOCKS, dtype=jnp.int32)
-    block = jnp.where(step < ROWS, core * ROWS + step, (1 - core) * ROWS + step - ROWS)[:, None]
-    key_block = chip * CHIP_BLOCKS + block - offsets
-    usable = (jnp.arange(CAND, dtype=jnp.int32)[None, :] < counts[:, None]) & (key_block >= 0)
-    rho = SPAN - offsets
-    near = pack_slots(usable & (offsets <= block), rho)
-    far = pack_slots(usable & (offsets > block), rho)
-    place = jnp.where(usable, block + rho, -1)
-    row = jnp.arange(SPAN + CHIP_BLOCKS, dtype=jnp.int32)[:, None, None]
-    hit = jnp.any(place[None, :, :] == row, axis=2)
-    return near, far, jnp.tile(hit.astype(jnp.float32), (1, GROUP))
+    )(place, *near[-3:], *args, wk)
 
 
 def body(
     teacher_queries, teacher_keys, query_projection, key_projection, block_offsets, valid_counts
 ):
-    chips = ("z", "yh", "x")
-    places = ("z", "yh", "x", "core")
+    chips = ("za", "zb", "yh", "x")
+    places = chips + ("core",)
     count = lax.axis_size(places)
     core = lax.axis_index("core")
-    chip = lax.axis_index(chips)
+    place = jnp.stack([core, lax.axis_index(chips)]).astype(jnp.int32)
     half = ROWS * BLOCK
 
-    k_mine = lax.dynamic_slice_in_dim(teacher_keys, core * K_COLS, K_COLS, 1)
+    k_mine, k_give = cut(
+        cut_keys_kernel, place, teacher_keys, [shaped((half, K_COLS), jnp.bfloat16)] * 2, "cut_keys"
+    )
     k_prev_own = lax.ppermute(k_mine, places, [(i, i + 2) for i in range(count - 2)])
-    k_give = lax.dynamic_slice_in_dim(teacher_keys, (1 - core) * K_COLS, K_COLS, 1)
     k_prev_other = lax.ppermute(
         k_give, places, [(i, (i ^ 1) + 2) for i in range(count - 2)]
     )
-    note = jnp.concatenate(
-        [block_offsets, valid_counts[:, None], jnp.zeros((ROWS, K_COLS - CAND - 1), jnp.int32)], axis=1
-    ).astype(jnp.bfloat16)
-    note = jnp.concatenate([note, jnp.zeros_like(note)], axis=0)
-    k_other = swap(jnp.concatenate([k_give, note], axis=0), "core")
-    note_other = k_other[half:half + ROWS, :CAND + 1].astype(jnp.int32)
-    k_other = k_other[:half]
+    k_other = swap(k_give, "core")
+    (q_give,) = cut(
+        cut_queries_kernel, place, teacher_queries, [shaped((half, Q_COLS), jnp.bfloat16)], "cut_queries"
+    )
+    q_other = swap(q_give, "core")
+    tables = (block_offsets, valid_counts, swap(block_offsets, "core"), swap(valid_counts, "core"))
     k_far = lax.ppermute(
         jnp.where(core == 1, k_mine, k_other), places, [(i, i + 4) for i in range(count - 4)]
     )
-    q_other = swap(
-        lax.dynamic_slice_in_dim(teacher_queries, (1 - core) * Q_COLS, Q_COLS, 1), "core"
-    )
-
-    offsets = jnp.concatenate([block_offsets, note_other[:, :CAND]], axis=0)
-    counts = jnp.concatenate([valid_counts, note_other[:, CAND]], axis=0)
-    near, far, hit = plan(core, chip, offsets, counts)
-    wq = lax.dynamic_slice_in_dim(query_projection, core * HEADS_HERE, HEADS_HERE, 0)
-    wk = lax.dynamic_slice_in_dim(key_projection, core * KV_HERE, KV_HERE, 0)
-    index = core.reshape(1).astype(jnp.int32)
-    near_out = near_call(index, *near, teacher_queries, q_other, teacher_keys, k_other, wq, wk)
-    parts = far_call(index, *far, k_prev_own, k_prev_other, k_far, near_out, hit, wk)
-
-    got = lax.all_to_all(parts, ("yh", "x"), 0, 0)
+    near = near_call(
+        place, tables, teacher_queries, q_other, k_mine, k_other, query_projection, key_projection
+    )
+    parts = far_call(place, k_prev_own, k_prev_other, k_far, near, key_projection)
+
+    group = ("zb", "yh", "x")
+    got = lax.all_to_all(parts, group, 0, 0)
     got = pl.pallas_call(sum_kernel, out_shape=shaped((SUM_ROWS + 8, HEAD_DIM)), name="sum")(got)
-    for step in (1, 2, 4):
-        got = got + lax.ppermute(got, "z", [(i, i ^ step) for i in range(8)])
+    one, two, three = (
+        lax.ppermute(got, "za", [(i, i ^ step) for i in range(4)]) for step in (1, 2, 3)
+    )
+    got = (got + one) + (two + three)
     total = got[SUM_ROWS:SUM_ROWS + 1, :]
     total = total + swap(total, "head")
     total = total + swap(total, "core")
     spread = jnp.broadcast_to(got[:SUM_ROWS], (SHARES, SUM_ROWS, HEAD_DIM))
-    mine = lax.all_to_all(spread, ("yh", "x"), 0, 0)
+    mine = lax.all_to_all(spread, group, 0, 0)
     other = swap(mine, "core")
     first = jnp.where(core == 0, mine, other)
     second = jnp.where(core == 0, other, mine)
     both = jnp.concatenate([first, second], axis=0)
-    query_gradient = both[:, :HEAD_DIM]
-    key_gradient = both[:, HEAD_DIM:].reshape(2 * KV_HERE, POOL, HEAD_DIM)
+    query_gradient = both[:, :HALF_HEAD].reshape(2 * HEADS_HERE, HEAD_DIM, HEAD_DIM)
+    key_gradient = both[:, HALF_HEAD:].reshape(2 * KV_HERE, POOL, HEAD_DIM)
     return query_gradient, key_gradient, total[0, 0] / (1024 * HEADS)
 
 
 def solution(mesh):
-    split = Mesh(mesh.devices.reshape(8, 2, 4, 2, 2), ("z", "yh", "x", "core", "head"))
-    ctx = ("z", "yh", "x", "core")
+    split = Mesh(mesh.devices.reshape(4, 2, 2, 4, 2, 2), ("za", "zb", "yh", "x", "core", "head"))
+    ctx = ("za", "zb", "yh", "x", "core")
     placed = (
         P(ctx, "head"),
         P(ctx, "head"),

time: 128 us -> 170 us (1.33); the launches traced: 128 us -> 167 us
  Pallas kernels: 16.1 us -> 75.6 us
  other arithmetic: 15.9 us -> 4.67 us
  local copies, waits for them, and re-layouts: 12.4 us -> 2.48 us
  blocking collectives: 36.5 us -> 44.9 us
  starting transfers between devices: 35.2 us -> 28.1 us
    pallas_call x0 -> x2, Pallas kernels: none -> 51.3 us  [cut(): pl.pallas_call(kernel, grid_spec=pltpu.PrefetchScalarGridSpec(num_scalar_...]
    all_to_all x2, blocking collectives: 36.5 us -> 44.9 us  [the longest x1 27.8 us: body(): got = lax.all_to_all(parts, group, 0, 0)]
    dynamic_slice x4 -> x0, local copies, waits for them, and re-layouts: 6.01 us -> none  [the longest x1 2.26 us: body(): lax.dynamic_slice_in_dim(teacher_queries, (1 - core) * Q_COLS, Q_COLS, 1)]
    pallas_call x1, Pallas kernels: 8.47 us -> 13.7 us  [near_call(): pl.pallas_call(near_kernel, grid_spec=pltpu.PrefetchScalarGridSpec(num_sc...]
    ppermute x3, starting transfers between devices: 11.9 us -> 7.1 us  [body(): lax.ppermute(got, 'za', [(i, i ^ step) for i in range(4)])]
    ppermute x1, starting transfers between devices: 5.2 us -> 1.76 us  [body(): lax.ppermute(k_give, places, [(i, (i ^ 1) + 2) for i in range(count - 2)])]
    pallas_call x1, Pallas kernels: 5.65 us -> 8.54 us  [far_call(): pl.pallas_call(far_kernel, grid_spec=pltpu.PrefetchScalarGridSpec(num_sca...]
    reduce_sum x3 -> x0, other arithmetic: 2.82 us -> none  [the longest x1 1.26 us: pack_slots(): count = jnp.sum(picked.astype(jnp.int32), axis=1)]
  transfers between devices with their start and end apart: 11 -> 13, of which waited for: 5 -> 6; matrix products, arithmetic and copies ran while one was open for 16% -> 1% of each run, Pallas kernels for 7% -> 19%
where the time goes in v3:
time: 170 us; the launch traced here: 167 us
  Pallas kernels  75.6 us (44%)
  blocking collectives  44.9 us (26%)
  starting transfers between devices  28.1 us (17%)
  waiting for transfers between devices  9.62 us (6%)
  other arithmetic  4.67 us (3%)
  local copies, waits for them, and re-layouts  2.48 us (1%)
  between operations  2.01 us (1%)
    pallas_call x2, Pallas kernels, cut(): pl.pallas_call(kernel, grid_spec=pltpu.PrefetchScalarGridSpec(num_scalar_...  51.3 us
    all_to_all x1, blocking collectives, body(): got = lax.all_to_all(parts, group, 0, 0)  27.8 us
    all_to_all x1, blocking collectives, body(): mine = lax.all_to_all(spread, group, 0, 0)  17.1 us
    pallas_call x1, Pallas kernels, near_call(): pl.pallas_call(near_kernel, grid_spec=pltpu.PrefetchScalarGridSpec(num_sc...  13.7 us
    ppermute x7, starting transfers between devices, swap(): return lax.ppermute(x, axis, [(0, 1), (1, 0)])  10.1 us
    pallas_call x1, Pallas kernels, far_call(): pl.pallas_call(far_kernel, grid_spec=pltpu.PrefetchScalarGridSpec(num_sca...  8.54 us
    ppermute x3, starting transfers between devices, body(): lax.ppermute(got, 'za', [(i, i ^ step) for i in range(4)])  7.1 us
    ppermute x1, starting transfers between devices, body(): lax.ppermute(jnp.where(core == 1, k_mine, k_other), places, [(i, i + 4) f...  5.98 us
  transfers between devices with their start and end apart: 13, of which 6 were waited for; matrix products, arithmetic and copies ran while one was open for 1% of the time, Pallas kernels for 19%

profile of v3, /device:TPU:1, one launch (start us, length us, event | category | flops | bytes accessed | tf_op | source)
XLA Modules:
  0.0 167.4 jit_solution(2589329665992095981)
XLA Ops:
  1.2 33.7 %cut_queries.1 = bf16[512,1024]{1,0:T(8,128)(2,1)} custom-call(s32[2]{0:T(128)} %pad_add_fusion.core_ref.place_ref, bf16[512,2048]{1,0:T(8,128)(2,1)} %q_own_ref.1), custom_call_target="tpu_custom_call" | custom-call | tf_op jit(solution)/shard_map/cut_queries/pallas_call | solution.py:337
  34.9 3.3 %collective-permute-start.2 = (bf16[512,1024]{1,0:T(8,128)(2,1)}, bf16[512,1024]{1,0:T(8,128)(2,1)S(1)}, u32[]{:S(2)}, u32[]{:S(2)}) collective-permute-start(bf16[512,1024]{1,0:T(8,128)(2,1)} %cut_queries.1), channel_id=1, source_target_pairs={{0,2},{2,0},{1,3},{3,1},{4,6},{6,4},{5,7},{7,5},{8,10},{10,8},{9,1... | collective-permute-start | bytes 3145736 | tf_op jit(solution)/shard_map/ppermute | solution.py:352
  38.3 17.7 %cut_keys.1 = (bf16[512,256]{1,0:T(8,128)(2,1)}, bf16[512,256]{1,0:T(8,128)(2,1)}) custom-call(s32[2]{0:T(128)} %pad_add_fusion.core_ref.place_ref, bf16[512,512]{1,0:T(8,128)(2,1)} %keys_ref.1), custom_call_target="tpu_custom_call" | custom-call | tf_op jit(solution)/shard_map/cut_keys/pallas_call | solution.py:337
  56.0 1.8 %collective-permute-start.5 = (bf16[512,256]{1,0:T(8,128)(2,1)}, bf16[512,256]{1,0:T(8,128)(2,1)S(1)}, u32[]{:S(2)}, u32[]{:S(2)}) collective-permute-start(bf16[512,256]{1,0:T(8,128)(2,1)} %get-tuple-element.16), channel_id=1, source_target_pairs={{0,6},{2,4},{4,10},{6,8},{8,14},{10,12},{12,18},{14,16},{16,22},{1... | collective-permute-start | bytes 786440 | tf_op jit(solution)/shard_map/ppermute | solution.py:451
  57.8 3.1 %collective-permute-start.4 = (bf16[512,256]{1,0:T(8,128)(2,1)}, bf16[512,256]{1,0:T(8,128)(2,1)S(1)}, u32[]{:S(2)}, u32[]{:S(2)}) collective-permute-start(bf16[512,256]{1,0:T(8,128)(2,1)} %get-tuple-element.15.k_own_ref), channel_id=1, source_target_pairs={{0,4},{2,6},{4,8},{6,10},{8,12},{10,14},{12,16},{14,18},{16,20},{1... | collective-permute-start | bytes 786440 | tf_op jit(solution)/shard_map/ppermute | solution.py:450
  60.9 1.1 broadcast_select_fusion.2
  62.0 6.0 %collective-permute-start.6 = (bf16[512,256]{1,0:T(8,128)(2,1)S(1)}, bf16[512,256]{1,0:T(8,128)(2,1)S(1)}, u32[]{:S(2)}, u32[]{:S(2)}) collective-permute-start(bf16[512,256]{1,0:T(8,128)(2,1)S(1)} %broadcast_select_fusion.2), channel_id=1, source_target_pairs={{0,8},{2,10},{4,12},{6,14},{8,16},{10,18},{12,20},{14,22},{16,24},... | collective-permute-start | bytes 786440 | tf_op jit(solution)/shard_map/ppermute | solution.py:460
  68.1 1.1 collective-permute-done.1.counts_other_ref
  69.4 1.0 collective-permute-done.offsets_other_ref
  71.0 1.0 copy-done.1
  72.0 13.7 %near.1 = (bf16[32,256,128]{2,1,0:T(8,128)(2,1)}, f32[32,32,256]{2,1,0:T(8,128)}, f32[32,32,256]{2,1,0:T(8,128)}, f32[2,64,128]{2,1,0:T(8,128)}, f32[2,64,128]{2...) custom-call(s32[2]{0:T(128)} %pad_add_fusion.core_ref.place_ref, ...), custom_call_target="tpu_custom_call" | custom-call | flops 2000000000 | bytes 8000000 | tf_op jit(solution)/shard_map/near/pallas_call | solution.py:379
  86.5 8.5 %far.1 = f32[16,80,128]{2,1,0:T(8,128)} custom-call(s32[2]{0:T(128)} %pad_add_fusion.core_ref.place_ref, s32[392]{0:T(512)} %get-tuple-element.17.far_list, s32[104]{0:T(128)} %get-tuple-element.18.far_work, s32[1]{0:T(128)} %get-tuple-element.19.far_filled, bf16[512,256]{1,0:T(8,128)(2,1)} %copy-done.3, bf16[512,256]{1,0:T(8,128)(2,1)} %copy-done.2, ...), custom_call_target="tpu_custom_call" | custom-call | flops 2000000000 | bytes 8000000 | tf_op jit(solution)/shard_map/far/pallas_call | solution.py:410
  95.1 27.8 %all_to_all.10.parts_ref = f32[16,80,128]{2,1,0:T(8,128)} all-to-all(f32[16,80,128]{2,1,0:T(8,128)} %far.1), channel_id=1, replica_groups=mesh['za'=4,'zb'=2,'yh'=2,'x'=4,'core'=2,'head'=2] {'zb','yh','x'}, dimensions={0} | all-to-all | bytes 1310720 | tf_op jit(solution)/shard_map/all_to_all | solution.py:469
  122.9 2.1 %sum.1 = f32[120,128]{1,0:T(8,128)} custom-call(f32[16,80,128]{2,1,0:T(8,128)} %all_to_all.10.parts_ref), custom_call_target="tpu_custom_call" | custom-call | tf_op jit(solution)/shard_map/sum/pallas_call | solution.py:470
  125.0 3.4 %collective-permute-start.7 = (f32[120,128]{1,0:T(8,128)}, f32[120,128]{1,0:T(8,128)S(1)}, u32[]{:S(2)}, u32[]{:S(2)}) collective-permute-start(f32[120,128]{1,0:T(8,128)} %sum.1), channel_id=1, source_target_pairs={{0,64},{64,0},{128,192},{192,128},{1,65},{65,1},{129,193},{193,129... | collective-permute-start | bytes 184328 | tf_op jit(solution)/shard_map/ppermute | solution.py:472
  128.3 3.7 %collective-permute-start.8 = (f32[120,128]{1,0:T(8,128)}, f32[120,128]{1,0:T(8,128)S(1)}, u32[]{:S(2)}, u32[]{:S(2)}) collective-permute-start(f32[120,128]{1,0:T(8,128)} %sum.1), channel_id=1, source_target_pairs={{0,128},{64,192},{128,0},{192,64},{1,129},{65,193},{129,1},{193,65... | collective-permute-start | bytes 184328 | tf_op jit(solution)/shard_map/ppermute | solution.py:472
  132.1 4.1 %collective-permute-done.8 = f32[120,128]{1,0:T(8,128)S(1)} collective-permute-done((f32[120,128]{1,0:T(8,128)}, f32[120,128]{1,0:T(8,128)S(1)}, u32[]{:S(2)}, u32[]{:S(2)}) %collective-permute-start.8) | collective-permute-done | bytes 61472 | tf_op jit(solution)/shard_map/ppermute | solution.py:472
  136.2 1.7 collective-permute-done.9
  138.8 17.1 %all_to_all.11 = f32[16,112,128]{2,1,0:T(8,128)S(1)} all-to-all(f32[16,112,128]{2,1,0:T(8,128)S(1)} %broadcast_in_dim.3), channel_id=1, replica_groups=mesh['za'=4,'zb'=2,'yh'=2,'x'=4,'core'=2,'head'=2] {'zb','yh','x'}, dimensions={0} | all-to-all | bytes 1835008 | tf_op jit(solution)/shard_map/all_to_all | solution.py:479
  155.9 3.8 %collective-permute-start.10 = (f32[16,112,128]{2,1,0:T(8,128)S(1)}, f32[16,112,128]{2,1,0:T(8,128)S(1)}, u32[]{:S(2)}, u32[]{:S(2)}) collective-permute-start(f32[16,112,128]{2,1,0:T(8,128)S(1)} %all_to_all.11), channel_id=1, source_target_pairs={{0,2},{2,0},{1,3},{3,1},{4,6},{6,4},{5,7},{7,5},{8,10},{10,8},{9,1... | collective-permute-start | bytes 2752520 | tf_op jit(solution)/shard_map/ppermute | solution.py:352
  159.7 1.5 collective-permute-start.11
  162.2 1.1 collective-permute-start.12
  164.3 0.9 pad_maximum_fusion
  165.2 1.1 fusion
  (38 shorter events, 5.2 us)
Async XLA Ops:
  1.2 66.8 %copy-start.7 = (s32[8]{0:T(128)S(1)}, s32[8]{0:T(128)}, u32[]{:S(2)}) copy-start(s32[8]{0:T(128)} %counts_own_ref.1) | copy-start | bytes 100
  1.2 68.0 %copy-start.5 = (s32[8,24]{1,0:T(8,128)S(1)}, s32[8,24]{1,0:T(8,128)}, u32[]{:S(2)}) copy-start(s32[8,24]{1,0:T(8,128)} %offsets_own_ref.1) | copy-start | bytes 2308
  34.9 35.5 %collective-permute-start.2 = (bf16[512,1024]{1,0:T(8,128)(2,1)}, bf16[512,1024]{1,0:T(8,128)(2,1)S(1)}, u32[]{:S(2)}, u32[]{:S(2)}) collective-permute-start(bf16[512,1024]{1,0:T(8,128)(2,1)} %cut_queries.1), channel_id=1, source_target_pairs={{0,2},{2,0},{1,3},{3,1},{4,6},{6,4},{5,7},{7,5},{8,10},{10,8},{9,1... | collective-permute-start | bytes 3145736 | tf_op jit(solution)/shard_map/ppermute | solution.py:352
  55.9 5.0 %collective-permute-start.3 = (bf16[512,256]{1,0:T(8,128)(2,1)}, bf16[512,256]{1,0:T(8,128)(2,1)S(1)}, u32[]{:S(2)}, u32[]{:S(2)}) collective-permute-start(bf16[512,256]{1,0:T(8,128)(2,1)} %get-tuple-element.16), channel_id=1, source_target_pairs={{0,2},{2,0},{1,3},{3,1},{4,6},{6,4},{5,7},{7,5},{8,10},{10,8},{9,1... | collective-permute-start | bytes 786440 | tf_op jit(solution)/shard_map/ppermute | solution.py:352
  56.0 29.6 %collective-permute-start.5 = (bf16[512,256]{1,0:T(8,128)(2,1)}, bf16[512,256]{1,0:T(8,128)(2,1)S(1)}, u32[]{:S(2)}, u32[]{:S(2)}) collective-permute-start(bf16[512,256]{1,0:T(8,128)(2,1)} %get-tuple-element.16), channel_id=1, source_target_pairs={{0,6},{2,4},{4,10},{6,8},{8,14},{10,12},{12,18},{14,16},{16,22},{1... | collective-permute-start | bytes 786440 | tf_op jit(solution)/shard_map/ppermute | solution.py:451
  57.8 27.8 %collective-permute-start.4 = (bf16[512,256]{1,0:T(8,128)(2,1)}, bf16[512,256]{1,0:T(8,128)(2,1)S(1)}, u32[]{:S(2)}, u32[]{:S(2)}) collective-permute-start(bf16[512,256]{1,0:T(8,128)(2,1)} %get-tuple-element.15.k_own_ref), channel_id=1, source_target_pairs={{0,4},{2,6},{4,8},{6,10},{8,12},{10,14},{12,16},{14,18},{16,20},{1... | collective-permute-start | bytes 786440 | tf_op jit(solution)/shard_map/ppermute | solution.py:450
  60.9 9.5 %copy-start = (bf16[512,256]{1,0:T(8,128)(2,1)}, bf16[512,256]{1,0:T(8,128)(2,1)S(1)}, u32[]{:S(2)}) copy-start(bf16[512,256]{1,0:T(8,128)(2,1)S(1)} %collective-permute-done.3.k_other_ref) | copy-start | bytes 786436
  62.0 23.7 %collective-permute-start.6 = (bf16[512,256]{1,0:T(8,128)(2,1)S(1)}, bf16[512,256]{1,0:T(8,128)(2,1)S(1)}, u32[]{:S(2)}, u32[]{:S(2)}) collective-permute-start(bf16[512,256]{1,0:T(8,128)(2,1)S(1)} %broadcast_select_fusion.2), channel_id=1, source_target_pairs={{0,8},{2,10},{4,12},{6,14},{8,16},{10,18},{12,20},{14,22},{16,24},... | collective-permute-start | bytes 786440 | tf_op jit(solution)/shard_map/ppermute | solution.py:460
  68.0 1.2 collective-permute-start.1
  69.2 1.2 copy-start.8
  69.2 1.2 collective-permute-start
  70.4 0.6 copy-start.6
  71.0 1.0 copy-start.1
  85.7 0.7 copy-start.3
  85.7 0.8 copy-start.2
  85.7 0.9 copy-start.4
  125.0 7.1 %collective-permute-start.7 = (f32[120,128]{1,0:T(8,128)}, f32[120,128]{1,0:T(8,128)S(1)}, u32[]{:S(2)}, u32[]{:S(2)}) collective-permute-start(f32[120,128]{1,0:T(8,128)} %sum.1), channel_id=1, source_target_pairs={{0,64},{64,0},{128,192},{192,128},{1,65},{65,1},{129,193},{193,129... | collective-permute-start | bytes 184328 | tf_op jit(solution)/shard_map/ppermute | solution.py:472
  128.3 7.8 %collective-permute-start.8 = (f32[120,128]{1,0:T(8,128)}, f32[120,128]{1,0:T(8,128)S(1)}, u32[]{:S(2)}, u32[]{:S(2)}) collective-permute-start(f32[120,128]{1,0:T(8,128)} %sum.1), channel_id=1, source_target_pairs={{0,128},{64,192},{128,0},{192,64},{1,129},{65,193},{129,1},{193,65... | collective-permute-start | bytes 184328 | tf_op jit(solution)/shard_map/ppermute | solution.py:472
  132.1 5.8 %collective-permute-start.9 = (f32[120,128]{1,0:T(8,128)}, f32[120,128]{1,0:T(8,128)S(1)}, u32[]{:S(2)}, u32[]{:S(2)}) collective-permute-start(f32[120,128]{1,0:T(8,128)} %sum.1), channel_id=1, source_target_pairs={{0,192},{64,128},{128,64},{192,0},{1,193},{65,129},{129,65},{193,1... | collective-permute-start | bytes 184328 | tf_op jit(solution)/shard_map/ppermute | solution.py:472
  155.9 8.2 %collective-permute-start.10 = (f32[16,112,128]{2,1,0:T(8,128)S(1)}, f32[16,112,128]{2,1,0:T(8,128)S(1)}, u32[]{:S(2)}, u32[]{:S(2)}) collective-permute-start(f32[16,112,128]{2,1,0:T(8,128)S(1)} %all_to_all.11), channel_id=1, source_target_pairs={{0,2},{2,0},{1,3},{3,1},{4,6},{6,4},{5,7},{7,5},{8,10},{10,8},{9,1... | collective-permute-start | bytes 2752520 | tf_op jit(solution)/shard_map/ppermute | solution.py:352
  159.7 2.5 %collective-permute-start.11 = (f32[1,128]{1,0:T(1,128)S(1)}, f32[1,128]{1,0:T(1,128)S(1)}, u32[]{:S(2)}, u32[]{:S(2)}) collective-permute-start(f32[1,128]{1,0:T(1,128)S(1)} %slice.23), channel_id=1, source_target_pairs={{0,1},{1,0},{2,3},{3,2},{4,5},{5,4},{6,7},{7,6},{8,9},{9,8},{10,11... | collective-permute-start | bytes 1544 | tf_op jit(solution)/shard_map/ppermute | solution.py:352
  162.2 1.9 %collective-permute-start.12 = (f32[1,128]{1,0:T(1,128)S(1)}, f32[1,128]{1,0:T(1,128)S(1)}, u32[]{:S(2)}, u32[]{:S(2)}) collective-permute-start(f32[1,128]{1,0:T(1,128)S(1)} %slice_add_fusion), channel_id=1, source_target_pairs={{0,2},{2,0},{1,3},{3,1},{4,6},{6,4},{5,7},{7,5},{8,10},{10,8},{9,1... | collective-permute-start | bytes 1544 | tf_op jit(solution)/shard_map/ppermute | solution.py:352

commit v4 on v3

--- a/solution.py
+++ b/solution.py
@@ -33,8 +33,9 @@
 HALF_HEAD = HEAD_DIM // 2
 PART_ROWS = CHIP_BLOCKS + ROWS + KEY_ROWS + 8
 SUM_ROWS = HALF_HEAD + KEY_ROWS
-VMEM_BYTES = 56 * 1024 * 1024
+VMEM_BYTES = 40 * 1024 * 1024
 UNROLL = 3
+NOTE_ROWS = 16
 LIST_SIZE = CHIP_BLOCKS * CAND + 8
 WORK_SIZE = CHIP_BLOCKS * CAND // 4 + 8
 LOW = -1e30
@@ -62,42 +63,40 @@
 
 
 def make_lists(core, chip, tables, near_list, near_work, far_list, far_work):
-    limit_base = chip * CHIP_BLOCKS
     filled = (jnp.int32(0), jnp.int32(0))
-    for source, (offsets_ref, counts_ref) in enumerate(tables):
+    for source, table in enumerate(tables):
         first = ROWS * core if source == 0 else ROWS * (1 - core)
 
         def per_block(j, filled):
             block = first + j
+            limit = chip * CHIP_BLOCKS + block
+            count = table(j, CAND)
             base = (source * ROWS + j) * CAND
-
-            def per_slot(c, ends):
-                near_end, far_end = ends
-                offset = offsets_ref[j, c]
-                near = offset <= block
-                far = (offset > block) & (offset <= limit_base + block)
+            near_end = far_end = base
+            for c in range(CAND):
+                offset = table(j, c)
+                here = (c < count) & (offset <= limit)
+                near = jnp.where(here & (offset <= block), 1, 0)
+                far = jnp.where(here & (offset > block), 1, 0)
                 near_list[near_end] = SPAN - offset
                 far_list[far_end] = SPAN - offset
-                return near_end + near.astype(jnp.int32), far_end + far.astype(jnp.int32)
-
-            ends = lax.fori_loop(0, counts_ref[j], per_slot, (base, base))
+                near_end += near
+                far_end += far
             out = []
             for end, slots, work, total in zip(
-                ends, (near_list, far_list), (near_work, far_work), filled
+                (near_end, far_end), (near_list, far_list), (near_work, far_work), filled
             ):
                 for extra in range(3):
                     slots[end + extra] = DUMMY
-
-                def add(i, total):
+                for i in range(CAND // 4):
                     work[total] = base + i * 4
-                    return total + 1
-
-                out.append(lax.fori_loop(0, (end - base + 3) // 4, add, total))
+                    total += jnp.where(i * 4 < end - base, 1, 0)
+                out.append(total)
             return tuple(out)
 
         filled = lax.fori_loop(0, ROWS, per_block, filled)
     for work, total in zip((near_work, far_work), filled):
-        spare = work[jnp.maximum(total - 1, 0)]
+        spare = jnp.where(total > 0, work[jnp.maximum(total - 1, 0)], 0)
         for extra in range(UNROLL - 1):
             work[total + extra] = spare
     return filled
@@ -144,13 +143,16 @@
 
 
 def near_kernel(
-    place_ref, offsets_own_ref, counts_own_ref, offsets_other_ref, counts_other_ref,
+    place_ref, offsets_ref, counts_ref,
     q_own_ref, q_other_ref, k_own_ref, k_other_ref, wq_ref, wk_ref,
     queries, slot_max, slot_sum, pooled_query, gate_query, pooled_key, gate_key,
     far_list, far_work, far_filled,
-    keys, near_list, near_work,
+    keys, near_list, near_work, note_vector, note_scalar, sems,
 ):
     core_ref = place_ref
+    note_vector[...] = q_other_ref[ROWS * BLOCK:, 0:HEAD_DIM].astype(jnp.float32).astype(jnp.int32)
+    note_copy = pltpu.make_async_copy(note_vector, note_scalar, sems.at[0])
+    note_copy.start()
     core = core_ref[0]
     half = ROWS * BLOCK
     for source, ref in ((core, k_own_ref), (1 - core, k_other_ref)):
@@ -178,9 +180,13 @@
 
     slot_max[...] = jnp.full_like(slot_max, LOW)
     slot_sum[...] = jnp.zeros_like(slot_sum)
+    note_copy.wait()
     filled, filled_far = make_lists(
         core, place_ref[1],
-        ((offsets_own_ref, counts_own_ref), (offsets_other_ref, counts_other_ref)),
+        (
+            lambda j, c: counts_ref[j] if c == CAND else offsets_ref[j, c],
+            lambda j, c: note_scalar[j, c],
+        ),
         near_list, near_work, far_list, far_work,
     )
     far_filled[0] = filled_far
@@ -315,53 +321,77 @@
     out_ref[HALF_HEAD:, :] = jnp.sum(parts[:, CHIP_BLOCKS + ROWS:, :], axis=0)
 
 
-def cut_keys_kernel(core_ref, keys_ref, mine_ref, give_ref, sems):
-    at = pl.multiple_of(core_ref[0] * K_COLS, K_COLS)
-    other = pl.multiple_of((1 - core_ref[0]) * K_COLS, K_COLS)
-    mine = pltpu.make_async_copy(keys_ref.at[:, pl.ds(at, K_COLS)], mine_ref, sems.at[0])
-    give = pltpu.make_async_copy(keys_ref.at[:, pl.ds(other, K_COLS)], give_ref, sems.at[1])
-    mine.start()
-    give.start()
-    mine.wait()
-    give.wait()
-
-
-def cut_queries_kernel(core_ref, queries_ref, give_ref, sems):
-    other = pl.multiple_of((1 - core_ref[0]) * Q_COLS, Q_COLS)
-    give = pltpu.make_async_copy(queries_ref.at[:, pl.ds(other, Q_COLS)], give_ref, sems.at[0])
-    give.start()
-    give.wait()
-
-
-def cut(kernel, core, whole_array, outs, name):
+def cut_keys_kernel(place_ref, mine_in, give_in, mine_ref, give_ref):
+    mine_ref[...] = mine_in[...]
+    give_ref[...] = give_in[...]
+
+
+def cut_queries_kernel(place_ref, counts_ref, offsets_ref, give_in, give_ref):
+    half = ROWS * BLOCK
+    give_ref[0:half, :] = give_in[...]
+    row = lax.broadcasted_iota(jnp.int32, (ROWS, HEAD_DIM), 0)
+    lane = lax.broadcasted_iota(jnp.int32, (ROWS, HEAD_DIM), 1)
+    note = jnp.concatenate(
+        [offsets_ref[...], jnp.zeros((ROWS, HEAD_DIM - CAND), jnp.int32)], axis=1
+    )
+    for j in range(ROWS):
+        note = jnp.where((lane == CAND) & (row == j), counts_ref[j], note)
+    note = note.astype(jnp.float32).astype(jnp.bfloat16)
+    give_ref[half:, :] = jnp.zeros((NOTE_ROWS, Q_COLS), jnp.bfloat16)
+    give_ref[half:, 0:HEAD_DIM] = jnp.concatenate([note, jnp.zeros_like(note)], axis=0)
+
+
+def swap(x, axis):
+    return lax.ppermute(x, axis, [(0, 1), (1, 0)])
+
+
+def whole(*shape):
+    return pl.BlockSpec(shape, lambda i, *_: (0,) * len(shape))
+
+
+def shaped(shape, dtype=jnp.float32):
+    return jax.ShapeDtypeStruct(shape, dtype)
+
+
+def smem():
+    return pl.BlockSpec(memory_space=pltpu.SMEM)
+
+
+def cut_keys(place, keys):
+    half = ROWS * BLOCK
     return pl.pallas_call(
-        kernel,
+        cut_keys_kernel,
         grid_spec=pltpu.PrefetchScalarGridSpec(
             num_scalar_prefetch=1,
             grid=(1,),
-            in_specs=[pl.BlockSpec(memory_space=pl.ANY)],
-            out_specs=[pl.BlockSpec(memory_space=pl.ANY)] * len(outs),
-            scratch_shapes=[pltpu.SemaphoreType.DMA((2,))],
-        ),
-        out_shape=outs,
-        name=name,
-    )(core, whole_array)
-
-
-def swap(x, axis):
-    return lax.ppermute(x, axis, [(0, 1), (1, 0)])
-
-
-def whole(*shape):
-    return pl.BlockSpec(shape, lambda i, *_: (0,) * len(shape))
-
-
-def shaped(shape, dtype=jnp.float32):
-    return jax.ShapeDtypeStruct(shape, dtype)
-
-
-def smem():
-    return pl.BlockSpec(memory_space=pltpu.SMEM)
+            in_specs=[
+                pl.BlockSpec((half, K_COLS), lambda i, c: (0, c[0])),
+                pl.BlockSpec((half, K_COLS), lambda i, c: (0, 1 - c[0])),
+            ],
+            out_specs=[whole(half, K_COLS)] * 2,
+        ),
+        out_shape=[shaped((half, K_COLS), jnp.bfloat16)] * 2,
+        name="cut_keys",
+    )(place, keys, keys)
+
+
+def cut_queries(place, queries, offsets, counts):
+    half = ROWS * BLOCK
+    return pl.pallas_call(
+        cut_queries_kernel,
+        grid_spec=pltpu.PrefetchScalarGridSpec(
+            num_scalar_prefetch=1,
+            grid=(1,),
+            in_specs=[
+                smem(),
+                whole(ROWS, CAND),
+                pl.BlockSpec((half, Q_COLS), lambda i, c: (0, 1 - c[0])),
+            ],
+            out_specs=whole(half + NOTE_ROWS, Q_COLS),
+        ),
+        out_shape=shaped((half + NOTE_ROWS, Q_COLS), jnp.bfloat16),
+        name="cut_queries",
+    )(place, counts, offsets, queries)
 
 
 def near_call(place, tables, q_own, q_other, k_mine, k_other, wq, wk):
@@ -381,9 +411,9 @@
         grid_spec=pltpu.PrefetchScalarGridSpec(
             num_scalar_prefetch=1,
             grid=(1,),
-            in_specs=[smem()] * 4 + [
+            in_specs=[smem()] * 2 + [
                 pl.BlockSpec((half, Q_COLS), lambda i, c: (0, c[0])),
-                whole(half, Q_COLS),
+                whole(half + NOTE_ROWS, Q_COLS),
                 whole(half, K_COLS),
                 whole(half, K_COLS),
                 pl.BlockSpec((HEADS_HERE, HEAD_DIM, HEAD_DIM), lambda i, c: (c[0], 0, 0)),
@@ -394,6 +424,9 @@
                 pltpu.VMEM((CHIP_BLOCKS * BLOCK, K_COLS), jnp.bfloat16),
                 pltpu.SMEM((LIST_SIZE,), jnp.int32),
                 pltpu.SMEM((WORK_SIZE,), jnp.int32),
+                pltpu.VMEM((NOTE_ROWS, HEAD_DIM), jnp.int32),
+                pltpu.SMEM((NOTE_ROWS, HEAD_DIM), jnp.int32),
+                pltpu.SemaphoreType.DMA((1,)),
             ],
         ),
         out_shape=outs + [shaped((n,), jnp.int32) for n in lists],
@@ -442,26 +475,19 @@
     count = lax.axis_size(places)
     core = lax.axis_index("core")
     place = jnp.stack([core, lax.axis_index(chips)]).astype(jnp.int32)
-    half = ROWS * BLOCK
-
-    k_mine, k_give = cut(
-        cut_keys_kernel, place, teacher_keys, [shaped((half, K_COLS), jnp.bfloat16)] * 2, "cut_keys"
-    )
+
+    k_mine, k_give = cut_keys(place, teacher_keys)
     k_prev_own = lax.ppermute(k_mine, places, [(i, i + 2) for i in range(count - 2)])
     k_prev_other = lax.ppermute(
         k_give, places, [(i, (i ^ 1) + 2) for i in range(count - 2)]
     )
     k_other = swap(k_give, "core")
-    (q_give,) = cut(
-        cut_queries_kernel, place, teacher_queries, [shaped((half, Q_COLS), jnp.bfloat16)], "cut_queries"
-    )
-    q_other = swap(q_give, "core")
-    tables = (block_offsets, valid_counts, swap(block_offsets, "core"), swap(valid_counts, "core"))
+    q_other = swap(cut_queries(place, teacher_queries, block_offsets, valid_counts), "core")
     k_far = lax.ppermute(
         jnp.where(core == 1, k_mine, k_other), places, [(i, i + 4) for i in range(count - 4)]
     )
     near = near_call(
-        place, tables, teacher_queries, q_other, k_mine, k_other, query_projection, key_projection
+        place, (block_offsets, valid_counts), teacher_queries, q_other, k_mine, k_other, query_projection, key_projection
     )
     parts = far_call(place, k_prev_own, k_prev_other, k_far, near, key_projection)
 

time: 170 us -> 116 us (0.68); the launches traced: 167 us -> 117 us
  Pallas kernels: 75.6 us -> 24.8 us
  waiting for transfers between devices: 9.62 us -> 6.08 us
    pallas_call x2, Pallas kernels: 51.3 us -> 5.63 us  [the longest x1 3.13 us: cut_queries(): pl.pallas_call(cut_queries_kernel, grid_spec=pltpu.PrefetchScalarGridSpec...]
    ppermute x3, starting transfers between devices: 7.1 us -> 10.3 us  [body(): lax.ppermute(got, 'za', [(i, i ^ step) for i in range(4)])]
    all_to_all x1, blocking collectives: 17.1 us -> 20.2 us  [body(): mine = lax.all_to_all(spread, group, 0, 0)]
    pallas_call x1, Pallas kernels: 13.7 us -> 11.1 us  [near_call(): pl.pallas_call(near_kernel, grid_spec=pltpu.PrefetchScalarGridSpec(num_sc...]
    pallas_call x1, Pallas kernels: 8.54 us -> 6.1 us  [far_call(): pl.pallas_call(far_kernel, grid_spec=pltpu.PrefetchScalarGridSpec(num_sca...]
    ppermute x7 -> x5, starting transfers between devices: 10.1 us -> 7.96 us  [swap(): return lax.ppermute(x, axis, [(0, 1), (1, 0)])]
    ppermute x7 -> x5, waiting for transfers between devices: 3.82 us -> 1.91 us  [swap(): return lax.ppermute(x, axis, [(0, 1), (1, 0)])]
  transfers between devices with their start and end apart: 13 -> 11, of which waited for: 6 -> 4; matrix products, arithmetic and copies ran while one was open for 1% -> 1% of each run, Pallas kernels for 19% -> 12%
where the time goes in v4:
time: 116 us; the launch traced here: 117 us
  blocking collectives  46.5 us (40%)
  starting transfers between devices  29.2 us (25%)
  Pallas kernels  24.8 us (21%)
  waiting for transfers between devices  6.08 us (5%)
  other arithmetic  4.7 us (4%)
  local copies, waits for them, and re-layouts  3.39 us (3%)
  between operations  1.98 us (2%)
    all_to_all x1, blocking collectives, body(): got = lax.all_to_all(parts, group, 0, 0)  26.3 us
    all_to_all x1, blocking collectives, body(): mine = lax.all_to_all(spread, group, 0, 0)  20.2 us
    pallas_call x1, Pallas kernels, near_call(): pl.pallas_call(near_kernel, grid_spec=pltpu.PrefetchScalarGridSpec(num_sc...  11.1 us
    ppermute x3, starting transfers between devices, body(): lax.ppermute(got, 'za', [(i, i ^ step) for i in range(4)])  10.3 us
    ppermute x5, starting transfers between devices, swap(): return lax.ppermute(x, axis, [(0, 1), (1, 0)])  7.96 us
    pallas_call x1, Pallas kernels, far_call(): pl.pallas_call(far_kernel, grid_spec=pltpu.PrefetchScalarGridSpec(num_sca...  6.1 us
    ppermute x1, starting transfers between devices, body(): lax.ppermute(jnp.where(core == 1, k_mine, k_other), places, [(i, i + 4) f...  5.32 us
    ppermute x3, waiting for transfers between devices, body(): lax.ppermute(got, 'za', [(i, i ^ step) for i in range(4)])  4.16 us
  transfers between devices with their start and end apart: 11, of which 4 were waited for; matrix products, arithmetic and copies ran while one was open for 1% of the time, Pallas kernels for 12%

profile of v4, /device:TPU:1, one launch (start us, length us, event | category | flops | bytes accessed | tf_op | source)
XLA Modules:
  0.0 116.7 jit_solution(16278241500848341465)
XLA Ops:
  1.3 3.1 %cut_queries.1 = bf16[528,1024]{1,0:T(8,128)(2,1)} custom-call(s32[2]{0:T(128)} %pad_add_fusion.place_ref.core_ref, s32[8]{0:T(128)} %counts_ref.3, s32[8,24]{1,0:T(8,128)} %offsets_ref.3, bf16[512,2048]{1,0:T(8,128)(2,1)} %q_own_ref.1), custom_call_target="tpu_custom_call" | custom-call | tf_op jit(solution)/shard_map/cut_queries/pallas_call | solution.py:380
  4.4 3.2 %collective-permute-start = (bf16[528,1024]{1,0:T(8,128)(2,1)}, bf16[528,1024]{1,0:T(8,128)(2,1)S(1)}, u32[]{:S(2)}, u32[]{:S(2)}) collective-permute-start(bf16[528,1024]{1,0:T(8,128)(2,1)} %cut_queries.1), channel_id=1, source_target_pairs={{0,2},{2,0},{1,3},{3,1},{4,6},{6,4},{5,7},{7,5},{8,10},{10,8},{9,1... | collective-permute-start | bytes 3244040 | tf_op jit(solution)/shard_map/ppermute | solution.py:345
  7.7 2.5 %cut_keys.1 = (bf16[512,256]{1,0:T(8,128)(2,1)}, bf16[512,256]{1,0:T(8,128)(2,1)}) custom-call(s32[2]{0:T(128)} %pad_add_fusion.place_ref.core_ref, bf16[512,512]{1,0:T(8,128)(2,1)} %give_in.3, bf16[512,512]{1,0:T(8,128)(2,1)} %give_in.3), custom_call_target="tpu_custom_call" | custom-call | tf_op jit(solution)/shard_map/cut_keys/pallas_call | solution.py:362
  10.2 2.5 %collective-permute-start.3 = (bf16[512,256]{1,0:T(8,128)(2,1)}, bf16[512,256]{1,0:T(8,128)(2,1)}, u32[]{:S(2)}, u32[]{:S(2)}) collective-permute-start(bf16[512,256]{1,0:T(8,128)(2,1)} %get-tuple-element.16), channel_id=1, source_target_pairs={{0,6},{2,4},{4,10},{6,8},{8,14},{10,12},{12,18},{14,16},{16,22},{1... | collective-permute-start | bytes 786440 | tf_op jit(solution)/shard_map/ppermute | solution.py:481
  12.6 3.1 %collective-permute-start.2 = (bf16[512,256]{1,0:T(8,128)(2,1)}, bf16[512,256]{1,0:T(8,128)(2,1)}, u32[]{:S(2)}, u32[]{:S(2)}) collective-permute-start(bf16[512,256]{1,0:T(8,128)(2,1)} %get-tuple-element.15.k_own_ref), channel_id=1, source_target_pairs={{0,4},{2,6},{4,8},{6,10},{8,12},{10,14},{12,16},{14,18},{16,20},{1... | collective-permute-start | bytes 786440 | tf_op jit(solution)/shard_map/ppermute | solution.py:480
  15.8 1.1 broadcast_select_fusion.2
  16.8 5.3 %collective-permute-start.4 = (bf16[512,256]{1,0:T(8,128)(2,1)S(1)}, bf16[512,256]{1,0:T(8,128)(2,1)S(1)}, u32[]{:S(2)}, u32[]{:S(2)}) collective-permute-start(bf16[512,256]{1,0:T(8,128)(2,1)S(1)} %broadcast_select_fusion.2), channel_id=1, source_target_pairs={{0,8},{2,10},{4,12},{6,14},{8,16},{10,18},{12,20},{14,22},{16,24},... | collective-permute-start | bytes 786440 | tf_op jit(solution)/shard_map/ppermute | solution.py:486
  22.2 0.9 copy-done.1
  23.2 1.2 %copy-done.5 = f32[16,128,128]{2,1,0:T(8,128)S(1)} copy-done((f32[16,128,128]{2,1,0:T(8,128)S(1)}, f32[16,128,128]{2,1,0:T(8,128)}, u32[]{:S(2)}) %copy-start.5) | copy-done | bytes 1048600
  24.4 1.1 copy-done.6
  25.5 11.1 %near.1 = (bf16[32,256,128]{2,1,0:T(8,128)(2,1)S(1)}, f32[32,32,256]{2,1,0:T(8,128)S(1)}, f32[32,32,256]{2,1,0:T(8,128)S(1)}, f32[2,64,128]{2,1,0:T(8,128)S(1)},...) custom-call(s32[2]{0:T(128)S(1)} %copy-done.3, ...), custom_call_target="tpu_custom_call" | custom-call | flops 2000000000 | bytes 8000000 | tf_op jit(solution)/shard_map/near/pallas_call | solution.py:409
  36.6 6.1 %far.1 = f32[16,80,128]{2,1,0:T(8,128)S(1)} custom-call(s32[2]{0:T(128)S(1)} %copy-done.3, s32[392]{0:T(512)S(1)} %get-tuple-element.17.far_list, s32[104]{0:T(128)S(1)} %get-tuple-element.18.far_work, s32[1]{0:T(128)} %get-tuple-element.19.far_filled, bf16[512,256]{1,0:T(8,128)(2,1)} %collective-permute-done.2.k_prev_own_ref, ...), custom_call_target="tpu_custom_call" | custom-call | flops 2000000000 | bytes 8000000 | tf_op jit(solution)/shard_map/far/pallas_call | solution.py:443
  42.7 26.3 %all_to_all.10.parts_ref = f32[16,80,128]{2,1,0:T(8,128)} all-to-all(f32[16,80,128]{2,1,0:T(8,128)S(1)} %far.1), channel_id=1, replica_groups=mesh['za'=4,'zb'=2,'yh'=2,'x'=4,'core'=2,'head'=2] {'zb','yh','x'}, dimensions={0} | all-to-all | bytes 1310720 | tf_op jit(solution)/shard_map/all_to_all | solution.py:495
  69.0 2.1 %sum.1 = f32[120,128]{1,0:T(8,128)} custom-call(f32[16,80,128]{2,1,0:T(8,128)} %all_to_all.10.parts_ref), custom_call_target="tpu_custom_call" | custom-call | tf_op jit(solution)/shard_map/sum/pallas_call | solution.py:496
  71.1 7.0 %collective-permute-start.5 = (f32[120,128]{1,0:T(8,128)}, f32[120,128]{1,0:T(8,128)S(1)}, u32[]{:S(2)}, u32[]{:S(2)}) collective-permute-start(f32[120,128]{1,0:T(8,128)} %sum.1), channel_id=1, source_target_pairs={{0,64},{64,0},{128,192},{192,128},{1,65},{65,1},{129,193},{193,129... | collective-permute-start | bytes 184328 | tf_op jit(solution)/shard_map/ppermute | solution.py:498
  78.1 3.3 %collective-permute-start.7 = (f32[120,128]{1,0:T(8,128)}, f32[120,128]{1,0:T(8,128)S(1)}, u32[]{:S(2)}, u32[]{:S(2)}) collective-permute-start(f32[120,128]{1,0:T(8,128)} %sum.1), channel_id=1, source_target_pairs={{0,192},{64,128},{128,64},{192,0},{1,193},{65,129},{129,65},{193,1... | collective-permute-start | bytes 184328 | tf_op jit(solution)/shard_map/ppermute | solution.py:498
  82.2 3.3 %collective-permute-done.6 = f32[120,128]{1,0:T(8,128)S(1)} collective-permute-done((f32[120,128]{1,0:T(8,128)}, f32[120,128]{1,0:T(8,128)S(1)}, u32[]{:S(2)}, u32[]{:S(2)}) %collective-permute-start.6) | collective-permute-done | bytes 61472 | tf_op jit(solution)/shard_map/ppermute | solution.py:498
  86.5 20.2 %all_to_all.11 = f32[16,112,128]{2,1,0:T(8,128)S(1)} all-to-all(f32[16,112,128]{2,1,0:T(8,128)S(1)} %broadcast_in_dim.3), channel_id=1, replica_groups=mesh['za'=4,'zb'=2,'yh'=2,'x'=4,'core'=2,'head'=2] {'zb','yh','x'}, dimensions={0} | all-to-all | bytes 1835008 | tf_op jit(solution)/shard_map/all_to_all | solution.py:505
  106.7 2.3 %collective-permute-start.8 = (f32[16,112,128]{2,1,0:T(8,128)S(1)}, f32[16,112,128]{2,1,0:T(8,128)S(1)}, u32[]{:S(2)}, u32[]{:S(2)}) collective-permute-start(f32[16,112,128]{2,1,0:T(8,128)S(1)} %all_to_all.11), channel_id=1, source_target_pairs={{0,2},{2,0},{1,3},{3,1},{4,6},{6,4},{5,7},{7,5},{8,10},{10,8},{9,1... | collective-permute-start | bytes 2752520 | tf_op jit(solution)/shard_map/ppermute | solution.py:345
  109.0 1.3 %collective-permute-start.9 = (f32[1,128]{1,0:T(1,128)S(1)}, f32[1,128]{1,0:T(1,128)S(1)}, u32[]{:S(2)}, u32[]{:S(2)}) collective-permute-start(f32[1,128]{1,0:T(1,128)S(1)} %slice.23), channel_id=1, source_target_pairs={{0,1},{1,0},{2,3},{3,2},{4,5},{5,4},{6,7},{7,6},{8,9},{9,8},{10,11... | collective-permute-start | bytes 1544 | tf_op jit(solution)/shard_map/ppermute | solution.py:345
  110.3 1.1 collective-permute-done.9
  111.4 1.2 collective-permute-start.10
  113.5 0.9 pad_maximum_fusion
  114.5 1.1 fusion
  (32 shorter events, 3.4 us)
Async XLA Ops:
  1.3 20.9 %copy-start = (bf16[512,2048]{1,0:T(8,128)(2,1)S(1)}, bf16[512,2048]{1,0:T(8,128)(2,1)}, u32[]{:S(2)}) copy-start(bf16[512,2048]{1,0:T(8,128)(2,1)} %q_own_ref.1) | copy-start | bytes 6291460
  1.3 20.9 %copy-start.2 = (s32[8,24]{1,0:T(8,128)S(1)}, s32[8,24]{1,0:T(8,128)}, u32[]{:S(2)}) copy-start(s32[8,24]{1,0:T(8,128)} %offsets_ref.3) | copy-start | bytes 2308
  1.3 20.9 %copy-start.3 = (s32[2]{0:T(128)S(1)}, s32[2]{0:T(128)}, u32[]{:S(2)}) copy-start(s32[2]{0:T(128)} %pad_add_fusion.place_ref.core_ref) | copy-start | bytes 28
  1.3 20.9 %copy-start.4 = (s32[8]{0:T(128)S(1)}, s32[8]{0:T(128)}, u32[]{:S(2)}) copy-start(s32[8]{0:T(128)} %counts_ref.3) | copy-start | bytes 100
  4.4 17.7 %collective-permute-start = (bf16[528,1024]{1,0:T(8,128)(2,1)}, bf16[528,1024]{1,0:T(8,128)(2,1)S(1)}, u32[]{:S(2)}, u32[]{:S(2)}) collective-permute-start(bf16[528,1024]{1,0:T(8,128)(2,1)} %cut_queries.1), channel_id=1, source_target_pairs={{0,2},{2,0},{1,3},{3,1},{4,6},{6,4},{5,7},{7,5},{8,10},{10,8},{9,1... | collective-permute-start | bytes 3244040 | tf_op jit(solution)/shard_map/ppermute | solution.py:345
  10.2 5.6 %collective-permute-start.1 = (bf16[512,256]{1,0:T(8,128)(2,1)}, bf16[512,256]{1,0:T(8,128)(2,1)S(1)}, u32[]{:S(2)}, u32[]{:S(2)}) collective-permute-start(bf16[512,256]{1,0:T(8,128)(2,1)} %get-tuple-element.16), channel_id=1, source_target_pairs={{0,2},{2,0},{1,3},{3,1},{4,6},{6,4},{5,7},{7,5},{8,10},{10,8},{9,1... | collective-permute-start | bytes 786440 | tf_op jit(solution)/shard_map/ppermute | solution.py:345
  10.2 26.4 %collective-permute-start.3 = (bf16[512,256]{1,0:T(8,128)(2,1)}, bf16[512,256]{1,0:T(8,128)(2,1)}, u32[]{:S(2)}, u32[]{:S(2)}) collective-permute-start(bf16[512,256]{1,0:T(8,128)(2,1)} %get-tuple-element.16), channel_id=1, source_target_pairs={{0,6},{2,4},{4,10},{6,8},{8,14},{10,12},{12,18},{14,16},{16,22},{1... | collective-permute-start | bytes 786440 | tf_op jit(solution)/shard_map/ppermute | solution.py:481
  12.6 24.0 %collective-permute-start.2 = (bf16[512,256]{1,0:T(8,128)(2,1)}, bf16[512,256]{1,0:T(8,128)(2,1)}, u32[]{:S(2)}, u32[]{:S(2)}) collective-permute-start(bf16[512,256]{1,0:T(8,128)(2,1)} %get-tuple-element.15.k_own_ref), channel_id=1, source_target_pairs={{0,4},{2,6},{4,8},{6,10},{8,12},{10,14},{12,16},{14,18},{16,20},{1... | collective-permute-start | bytes 786440 | tf_op jit(solution)/shard_map/ppermute | solution.py:480
  15.8 20.9 %copy-start.7 = (f32[4,384,128]{2,1,0:T(8,128)S(1)}, f32[4,384,128]{2,1,0:T(8,128)}, u32[]{:S(2)}) copy-start(f32[4,384,128]{2,1,0:T(8,128)} %wk_ref.3) | copy-start | bytes 2359300
  16.8 19.8 %collective-permute-start.4 = (bf16[512,256]{1,0:T(8,128)(2,1)S(1)}, bf16[512,256]{1,0:T(8,128)(2,1)S(1)}, u32[]{:S(2)}, u32[]{:S(2)}) collective-permute-start(bf16[512,256]{1,0:T(8,128)(2,1)S(1)} %broadcast_select_fusion.2), channel_id=1, source_target_pairs={{0,8},{2,10},{4,12},{6,14},{8,16},{10,18},{12,20},{14,22},{16,24},... | collective-permute-start | bytes 786440 | tf_op jit(solution)/shard_map/ppermute | solution.py:486
  22.2 1.0 copy-start.1
  23.2 1.2 %copy-start.5 = (f32[16,128,128]{2,1,0:T(8,128)S(1)}, f32[16,128,128]{2,1,0:T(8,128)}, u32[]{:S(2)}) copy-start(f32[16,128,128]{2,1,0:T(8,128)} %wq_ref.1) | copy-start | bytes 3145732
  24.4 1.1 copy-start.6
  71.1 11.1 %collective-permute-start.5 = (f32[120,128]{1,0:T(8,128)}, f32[120,128]{1,0:T(8,128)S(1)}, u32[]{:S(2)}, u32[]{:S(2)}) collective-permute-start(f32[120,128]{1,0:T(8,128)} %sum.1), channel_id=1, source_target_pairs={{0,64},{64,0},{128,192},{192,128},{1,65},{65,1},{129,193},{193,129... | collective-permute-start | bytes 184328 | tf_op jit(solution)/shard_map/ppermute | solution.py:498
  78.1 7.5 %collective-permute-start.6 = (f32[120,128]{1,0:T(8,128)}, f32[120,128]{1,0:T(8,128)S(1)}, u32[]{:S(2)}, u32[]{:S(2)}) collective-permute-start(f32[120,128]{1,0:T(8,128)} %sum.1), channel_id=1, source_target_pairs={{0,128},{64,192},{128,0},{192,64},{1,129},{65,193},{129,1},{193,65... | collective-permute-start | bytes 184328 | tf_op jit(solution)/shard_map/ppermute | solution.py:498
  78.1 7.5 %collective-permute-start.7 = (f32[120,128]{1,0:T(8,128)}, f32[120,128]{1,0:T(8,128)S(1)}, u32[]{:S(2)}, u32[]{:S(2)}) collective-permute-start(f32[120,128]{1,0:T(8,128)} %sum.1), channel_id=1, source_target_pairs={{0,192},{64,128},{128,64},{192,0},{1,193},{65,129},{129,65},{193,1... | collective-permute-start | bytes 184328 | tf_op jit(solution)/shard_map/ppermute | solution.py:498
  106.7 6.7 %collective-permute-start.8 = (f32[16,112,128]{2,1,0:T(8,128)S(1)}, f32[16,112,128]{2,1,0:T(8,128)S(1)}, u32[]{:S(2)}, u32[]{:S(2)}) collective-permute-start(f32[16,112,128]{2,1,0:T(8,128)S(1)} %all_to_all.11), channel_id=1, source_target_pairs={{0,2},{2,0},{1,3},{3,1},{4,6},{6,4},{5,7},{7,5},{8,10},{10,8},{9,1... | collective-permute-start | bytes 2752520 | tf_op jit(solution)/shard_map/ppermute | solution.py:345
  109.0 2.4 %collective-permute-start.9 = (f32[1,128]{1,0:T(1,128)S(1)}, f32[1,128]{1,0:T(1,128)S(1)}, u32[]{:S(2)}, u32[]{:S(2)}) collective-permute-start(f32[1,128]{1,0:T(1,128)S(1)} %slice.23), channel_id=1, source_target_pairs={{0,1},{1,0},{2,3},{3,2},{4,5},{5,4},{6,7},{7,6},{8,9},{9,8},{10,11... | collective-permute-start | bytes 1544 | tf_op jit(solution)/shard_map/ppermute | solution.py:345
  111.4 2.0 %collective-permute-start.10 = (f32[1,128]{1,0:T(1,128)S(1)}, f32[1,128]{1,0:T(1,128)S(1)}, u32[]{:S(2)}, u32[]{:S(2)}) collective-permute-start(f32[1,128]{1,0:T(1,128)S(1)} %slice_add_fusion), channel_id=1, source_target_pairs={{0,2},{2,0},{1,3},{3,1},{4,6},{6,4},{5,7},{7,5},{8,10},{10,8},{9,1... | collective-permute-start | bytes 1544 | tf_op jit(solution)/shard_map/ppermute | solution.py:345

commit v5 on v4

--- a/solution.py
+++ b/solution.py
@@ -36,6 +36,8 @@
 VMEM_BYTES = 40 * 1024 * 1024
 UNROLL = 3
 NOTE_ROWS = 16
+TILE = 16
+LEVELS = 32760.0
 LIST_SIZE = CHIP_BLOCKS * CAND + 8
 WORK_SIZE = CHIP_BLOCKS * CAND // 4 + 8
 LOW = -1e30
@@ -144,10 +146,10 @@
 
 def near_kernel(
     place_ref, offsets_ref, counts_ref,
-    q_own_ref, q_other_ref, k_own_ref, k_other_ref, wq_ref, wk_ref,
+    q_own_hbm, q_other_ref, k_own_ref, k_other_ref, wq_hbm, wk_hbm,
     queries, slot_max, slot_sum, pooled_query, gate_query, pooled_key, gate_key,
     far_list, far_work, far_filled,
-    keys, near_list, near_work, note_vector, note_scalar, sems,
+    keys, near_list, near_work, note_vector, note_scalar, q_own_ref, wq_ref, wk_ref, sems,
 ):
     core_ref = place_ref
     note_vector[...] = q_other_ref[ROWS * BLOCK:, 0:HEAD_DIM].astype(jnp.float32).astype(jnp.int32)
@@ -155,6 +157,18 @@
     note_copy.start()
     core = core_ref[0]
     half = ROWS * BLOCK
+    q_copy = pltpu.make_async_copy(
+        q_own_hbm.at[:, pl.ds(pl.multiple_of(core * Q_COLS, Q_COLS), Q_COLS)], q_own_ref, sems.at[1]
+    )
+    wq_copy = pltpu.make_async_copy(
+        wq_hbm.at[pl.ds(core * HEADS_HERE, HEADS_HERE)], wq_ref, sems.at[2]
+    )
+    wk_copy = pltpu.make_async_copy(
+        wk_hbm.at[pl.ds(core * KV_HERE, KV_HERE)], wk_ref, sems.at[3]
+    )
+    q_copy.start()
+    wq_copy.start()
+    wk_copy.start()
     for source, ref in ((core, k_own_ref), (1 - core, k_other_ref)):
         tile = ref[...]
         keys[pl.ds(pl.multiple_of(source * half, half), half), :] = tile
@@ -171,8 +185,10 @@
                     tile.astype(jnp.float32), axis=0, keepdims=True
                 ) * (1.0 / BLOCK)
 
-    for source in range(2):
+    for source in (1, 0):
         q_ref = (q_own_ref, q_other_ref)[source]
+        if source == 0:
+            q_copy.wait()
 
         @pl.loop(0, ROWS)
         def _(j):
@@ -195,6 +211,8 @@
         lambda s, row: position(core, s) + jnp.minimum(row, SPAN) - SPAN,
         keys, queries, slot_max, slot_sum, True,
     )
+    wq_copy.wait()
+    wk_copy.wait()
     for g in range(KV_HERE):
         gate_key[g] = dot_f32(pooled_key[g], wk_ref[g], ((1,), (0,)))
         for r in range(GROUP):
@@ -321,12 +339,74 @@
     out_ref[HALF_HEAD:, :] = jnp.sum(parts[:, CHIP_BLOCKS + ROWS:, :], axis=0)
 
 
+def pack_kernel(own_ref, one_ref, two_ref, three_ref, out_ref, total_ref):
+    got = (own_ref[...] + one_ref[...]) + (two_ref[...] + three_ref[...])
+    total_ref[...] = got[SUM_ROWS:, :]
+    coded = []
+    powers = jnp.zeros((TILE, HEAD_DIM), jnp.float32)
+    row = lax.broadcasted_iota(jnp.int32, (TILE, HEAD_DIM), 0)
+    for tile in range(SUM_ROWS // TILE):
+        value = got[tile * TILE:(tile + 1) * TILE, :]
+        top = jnp.max(jnp.abs(value), axis=0, keepdims=True)
+        power = jnp.clip(jnp.ceil(jnp.log2(jnp.maximum(top, 1e-35))), -110.0, 110.0)
+        level = jnp.clip(jnp.round(value * jnp.exp2(-power) * LEVELS), -32767.0, 32767.0)
+        coded.append(level.astype(jnp.int32).astype(jnp.int16))
+        powers = jnp.where(row == tile, power, powers)
+    coded.append(powers.astype(jnp.int32).astype(jnp.int16))
+    coded = jnp.concatenate(coded, axis=0)
+    for i in range(SHARES):
+        out_ref[i] = coded
+
+
+def unpack_kernel(place_ref, mine_ref, other_ref, query_ref, key_ref):
+    core = place_ref[0]
+    for source, ref in ((core, mine_ref), (1 - core, other_ref)):
+
+        @pl.loop(0, SHARES)
+        def _(share):
+            coded = ref[share].astype(jnp.int32).astype(jnp.float32)
+            scale = jnp.exp2(coded[SUM_ROWS:, :]) * (1.0 / LEVELS)
+            for tile in range(SUM_ROWS // TILE):
+                value = coded[tile * TILE:(tile + 1) * TILE, :] * scale[tile:tile + 1, :]
+                if tile < HALF_HEAD // TILE:
+                    at = source * (SHARES * HALF_HEAD) + share * HALF_HEAD + tile * TILE
+                    query_ref[pl.ds(pl.multiple_of(at, TILE), TILE), :] = value
+                else:
+                    at = source * (SHARES * KEY_ROWS) + share * KEY_ROWS + tile * TILE - HALF_HEAD
+                    key_ref[pl.ds(pl.multiple_of(at, TILE), TILE), :] = value
+
+
+def pack(*parts):
+    return pl.pallas_call(
+        pack_kernel,
+        out_shape=[
+            shaped((SHARES, SUM_ROWS + TILE, HEAD_DIM), jnp.int16), shaped((8, HEAD_DIM)),
+        ],
+        name="pack",
+    )(*parts)
+
+
+def unpack(place, mine, other):
+    rows = 2 * SHARES * HALF_HEAD, 2 * SHARES * KEY_ROWS
+    return pl.pallas_call(
+        unpack_kernel,
+        grid_spec=pltpu.PrefetchScalarGridSpec(
+            num_scalar_prefetch=1,
+            grid=(1,),
+            in_specs=[whole(*mine.shape)] * 2,
+            out_specs=[whole(n, HEAD_DIM) for n in rows],
+        ),
+        out_shape=[shaped((n, HEAD_DIM)) for n in rows],
+        name="unpack",
+    )(place, mine, other)
+
+
 def cut_keys_kernel(place_ref, mine_in, give_in, mine_ref, give_ref):
     mine_ref[...] = mine_in[...]
     give_ref[...] = give_in[...]
 
 
-def cut_queries_kernel(place_ref, counts_ref, offsets_ref, give_in, give_ref):
+def cut_queries_kernel(place_ref, counts_ref, offsets_ref, give_in, after_ref, give_ref):
     half = ROWS * BLOCK
     give_ref[0:half, :] = give_in[...]
     row = lax.broadcasted_iota(jnp.int32, (ROWS, HEAD_DIM), 0)
@@ -375,7 +455,7 @@
     )(place, keys, keys)
 
 
-def cut_queries(place, queries, offsets, counts):
+def cut_queries(place, queries, offsets, counts, after):
     half = ROWS * BLOCK
     return pl.pallas_call(
         cut_queries_kernel,
@@ -386,12 +466,13 @@
                 smem(),
                 whole(ROWS, CAND),
                 pl.BlockSpec((half, Q_COLS), lambda i, c: (0, 1 - c[0])),
+                pl.BlockSpec(memory_space=pl.ANY),
             ],
             out_specs=whole(half + NOTE_ROWS, Q_COLS),
         ),
         out_shape=shaped((half + NOTE_ROWS, Q_COLS), jnp.bfloat16),
         name="cut_queries",
-    )(place, counts, offsets, queries)
+    )(place, counts, offsets, queries, after)
 
 
 def near_call(place, tables, q_own, q_other, k_mine, k_other, wq, wk):
@@ -412,12 +493,12 @@
             num_scalar_prefetch=1,
             grid=(1,),
             in_specs=[smem()] * 2 + [
-                pl.BlockSpec((half, Q_COLS), lambda i, c: (0, c[0])),
+                pl.BlockSpec(memory_space=pltpu.HBM),
                 whole(half + NOTE_ROWS, Q_COLS),
                 whole(half, K_COLS),
                 whole(half, K_COLS),
-                pl.BlockSpec((HEADS_HERE, HEAD_DIM, HEAD_DIM), lambda i, c: (c[0], 0, 0)),
-                pl.BlockSpec((KV_HERE, POOL, HEAD_DIM), lambda i, c: (c[0], 0, 0)),
+                pl.BlockSpec(memory_space=pltpu.HBM),
+                pl.BlockSpec(memory_space=pltpu.HBM),
             ],
             out_specs=[whole(*o.shape) for o in outs] + [smem()] * 3,
             scratch_shapes=[
@@ -426,7 +507,10 @@
                 pltpu.SMEM((WORK_SIZE,), jnp.int32),
                 pltpu.VMEM((NOTE_ROWS, HEAD_DIM), jnp.int32),
                 pltpu.SMEM((NOTE_ROWS, HEAD_DIM), jnp.int32),
-                pltpu.SemaphoreType.DMA((1,)),
+                pltpu.VMEM((half, Q_COLS), jnp.bfloat16),
+                pltpu.VMEM((HEADS_HERE, HEAD_DIM, HEAD_DIM), jnp.float32),
+                pltpu.VMEM((KV_HERE, POOL, HEAD_DIM), jnp.float32),
+                pltpu.SemaphoreType.DMA((4,)),
             ],
         ),
         out_shape=outs + [shaped((n,), jnp.int32) for n in lists],
@@ -482,7 +566,7 @@
         k_give, places, [(i, (i ^ 1) + 2) for i in range(count - 2)]
     )
     k_other = swap(k_give, "core")
-    q_other = swap(cut_queries(place, teacher_queries, block_offsets, valid_counts), "core")
+    q_other = swap(cut_queries(place, teacher_queries, block_offsets, valid_counts, k_mine), "core")
     k_far = lax.ppermute(
         jnp.where(core == 1, k_mine, k_other), places, [(i, i + 4) for i in range(count - 4)]
     )
@@ -497,19 +581,17 @@
     one, two, three = (
         lax.ppermute(got, "za", [(i, i ^ step) for i in range(4)]) for step in (1, 2, 3)
     )
-    got = (got + one) + (two + three)
-    total = got[SUM_ROWS:SUM_ROWS + 1, :]
+    coded, total = pack(got, one, two, three)
+    total = total[:1]
     total = total + swap(total, "head")
     total = total + swap(total, "core")
-    spread = jnp.broadcast_to(got[:SUM_ROWS], (SHARES, SUM_ROWS, HEAD_DIM))
-    mine = lax.all_to_all(spread, group, 0, 0)
-    other = swap(mine, "core")
-    first = jnp.where(core == 0, mine, other)
-    second = jnp.where(core == 0, other, mine)
-    both = jnp.concatenate([first, second], axis=0)
-    query_gradient = both[:, :HALF_HEAD].reshape(2 * HEADS_HERE, HEAD_DIM, HEAD_DIM)
-    key_gradient = both[:, HALF_HEAD:].reshape(2 * KV_HERE, POOL, HEAD_DIM)
-    return query_gradient, key_gradient, total[0, 0] / (1024 * HEADS)
+    mine = lax.all_to_all(coded, group, 0, 0)
+    query_gradient, key_gradient = unpack(place, mine, swap(mine, "core"))
+    return (
+        query_gradient.reshape(2 * HEADS_HERE, HEAD_DIM, HEAD_DIM),
+        key_gradient.reshape(2 * KV_HERE, POOL, HEAD_DIM),
+        total[0, 0] / (1024 * HEADS),
+    )
 
 
 def solution(mesh):

time: 116 us -> 116 us (level); the launches traced: 117 us -> 115 us
  Pallas kernels: 24.8 us -> 32.4 us
  starting transfers between devices: 29.2 us -> 25 us
  other arithmetic: 4.7 us -> 1.37 us
  blocking collectives: 46.5 us -> 43.6 us
  waiting for transfers between devices: 6.08 us -> 7.59 us
    pallas_call x0 -> x2, Pallas kernels: none -> 5.39 us  [the longest x1 3.57 us: unpack(): pl.pallas_call(unpack_kernel, grid_spec=pltpu.PrefetchScalarGridSpec(num_...]
    all_to_all x1, blocking collectives: 20.2 us -> 16.1 us  [body(): mine = lax.all_to_all(coded, group, 0, 0)]
    ppermute x3, starting transfers between devices: 10.3 us -> 6.24 us  [body(): lax.ppermute(got, 'za', [(i, i ^ step) for i in range(4)])]
    concatenate x2 -> x0, other arithmetic: 2.02 us -> none  [body(): both = jnp.concatenate([first, second], axis=0)]
    pallas_call x1, Pallas kernels: 11.1 us -> 13.1 us  [near_call(): pl.pallas_call(near_kernel, grid_spec=pltpu.PrefetchScalarGridSpec(num_sc...]
    ppermute x1, starting transfers between devices: 2.46 us -> 3.8 us  [body(): lax.ppermute(k_give, places, [(i, (i ^ 1) + 2) for i in range(count - 2)])]
    all_to_all x1, blocking collectives: 26.3 us -> 27.6 us  [body(): got = lax.all_to_all(parts, group, 0, 0)]
    unnamed x16 -> x24, local copies, waits for them, and re-layouts: 3.32 us -> 2.68 us
  transfers between devices with their start and end apart: 11 -> 11, of which waited for: 4 -> 4; matrix products, arithmetic and copies ran while one was open for 1% -> 1% of each run, Pallas kernels for 12% -> 11%
where the time goes in v5:
time: 116 us; the launch traced here: 115 us
  blocking collectives  43.6 us (38%)
  Pallas kernels  32.4 us (28%)
  starting transfers between devices  25 us (22%)
  waiting for transfers between devices  7.59 us (7%)
  local copies, waits for them, and re-layouts  3.35 us (3%)
  between operations  1.99 us (2%)
  other arithmetic  1.37 us (1%)
    all_to_all x1, blocking collectives, body(): got = lax.all_to_all(parts, group, 0, 0)  27.6 us
    all_to_all x1, blocking collectives, body(): mine = lax.all_to_all(coded, group, 0, 0)  16.1 us
    pallas_call x1, Pallas kernels, near_call(): pl.pallas_call(near_kernel, grid_spec=pltpu.PrefetchScalarGridSpec(num_sc...  13.1 us
    ppermute x5, starting transfers between devices, swap(): return lax.ppermute(x, axis, [(0, 1), (1, 0)])  7.59 us
    ppermute x3, starting transfers between devices, body(): lax.ppermute(got, 'za', [(i, i ^ step) for i in range(4)])  6.24 us
    pallas_call x1, Pallas kernels, far_call(): pl.pallas_call(far_kernel, grid_spec=pltpu.PrefetchScalarGridSpec(num_sca...  6.11 us
    ppermute x1, starting transfers between devices, body(): lax.ppermute(jnp.where(core == 1, k_mine, k_other), places, [(i, i + 4) f...  5.3 us
    ppermute x3, waiting for transfers between devices, body(): lax.ppermute(got, 'za', [(i, i ^ step) for i in range(4)])  5.01 us
  transfers between devices with their start and end apart: 11, of which 4 were waited for; matrix products, arithmetic and copies ran while one was open for 1% of the time, Pallas kernels for 11%

profile of v5, /device:TPU:1, one launch (start us, length us, event | category | flops | bytes accessed | tf_op | source)
XLA Modules:
  0.0 115.3 jit_solution(16008215456094425472)
XLA Ops:
  1.3 2.5 %cut_keys.1 = (bf16[512,256]{1,0:T(8,128)(2,1)}, bf16[512,256]{1,0:T(8,128)(2,1)}) custom-call(s32[2]{0:T(128)} %pad_add_fusion.place_ref.core_ref, bf16[512,512]{1,0:T(8,128)(2,1)} %give_in.2, bf16[512,512]{1,0:T(8,128)(2,1)} %give_in.2), custom_call_target="tpu_custom_call" | custom-call | tf_op jit(solution)/shard_map/cut_keys/pallas_call | solution.py:442
  3.8 3.3 %cut_queries.1 = bf16[528,1024]{1,0:T(8,128)(2,1)} custom-call(s32[2]{0:T(128)} %pad_add_fusion.place_ref.core_ref, s32[8]{0:T(128)} %counts_ref.3, s32[8,24]{1,0:T(8,128)} %offsets_ref.3, bf16[512,2048]{1,0:T(8,128)(2,1)} %q_own_hbm.1, bf16[512,256]{1,0:T(8,128)(2,1)} %get-tuple-element.19.after_ref.k_own_ref), custom_call_target="tpu_custom_call" | custom-call | tf_op jit(solution)/shard_map/cut_queries/pallas_call | solution.py:460
  7.1 3.2 %collective-permute-start = (bf16[528,1024]{1,0:T(8,128)(2,1)}, bf16[528,1024]{1,0:T(8,128)(2,1)}, u32[]{:S(2)}, u32[]{:S(2)}) collective-permute-start(bf16[528,1024]{1,0:T(8,128)(2,1)} %cut_queries.1), channel_id=1, source_target_pairs={{0,2},{2,0},{1,3},{3,1},{4,6},{6,4},{5,7},{7,5},{8,10},{10,8},{9,1... | collective-permute-start | bytes 3244040 | tf_op jit(solution)/shard_map/ppermute | solution.py:425
  10.4 2.1 %collective-permute-start.2 = (bf16[512,256]{1,0:T(8,128)(2,1)S(1)}, bf16[512,256]{1,0:T(8,128)(2,1)}, u32[]{:S(2)}, u32[]{:S(2)}) collective-permute-start(bf16[512,256]{1,0:T(8,128)(2,1)S(1)} %copy-done.1), channel_id=1, source_target_pairs={{0,4},{2,6},{4,8},{6,10},{8,12},{10,14},{12,16},{14,18},{16,20},{1... | collective-permute-start | bytes 786440 | tf_op jit(solution)/shard_map/ppermute | solution.py:564
  12.5 3.8 %collective-permute-start.3 = (bf16[512,256]{1,0:T(8,128)(2,1)}, bf16[512,256]{1,0:T(8,128)(2,1)}, u32[]{:S(2)}, u32[]{:S(2)}) collective-permute-start(bf16[512,256]{1,0:T(8,128)(2,1)} %get-tuple-element.20), channel_id=1, source_target_pairs={{0,6},{2,4},{4,10},{6,8},{8,14},{10,12},{12,18},{14,16},{16,22},{1... | collective-permute-start | bytes 786440 | tf_op jit(solution)/shard_map/ppermute | solution.py:565
  16.3 5.3 %collective-permute-start.4 = (bf16[512,256]{1,0:T(8,128)(2,1)S(1)}, bf16[512,256]{1,0:T(8,128)(2,1)S(1)}, u32[]{:S(2)}, u32[]{:S(2)}) collective-permute-start(bf16[512,256]{1,0:T(8,128)(2,1)S(1)} %broadcast_select_fusion), channel_id=1, source_target_pairs={{0,8},{2,10},{4,12},{6,14},{8,16},{10,18},{12,20},{14,22},{16,24},... | collective-permute-start | bytes 786440 | tf_op jit(solution)/shard_map/ppermute | solution.py:570
  21.7 1.2 %copy-done.5 = f32[16,128,128]{2,1,0:T(8,128)S(1)} copy-done((f32[16,128,128]{2,1,0:T(8,128)S(1)}, f32[16,128,128]{2,1,0:T(8,128)}, u32[]{:S(2)}) %copy-start.5) | copy-done | bytes 1048600
  22.9 13.1 %near.1 = (bf16[32,256,128]{2,1,0:T(8,128)(2,1)S(1)}, f32[32,32,256]{2,1,0:T(8,128)S(1)}, f32[32,32,256]{2,1,0:T(8,128)S(1)}, f32[2,64,128]{2,1,0:T(8,128)S(1)},...) custom-call(s32[2]{0:T(128)S(1)} %copy-done.2, ...), custom_call_target="tpu_custom_call" | custom-call | flops 2000000000 | bytes 8000000 | tf_op jit(solution)/shard_map/near/pallas_call | solution.py:490
  36.0 6.1 %far.1 = f32[16,80,128]{2,1,0:T(8,128)S(1)} custom-call(s32[2]{0:T(128)S(1)} %copy-done.2, s32[392]{0:T(512)S(1)} %get-tuple-element.21.far_list, s32[104]{0:T(128)S(1)} %get-tuple-element.22.far_work, s32[1]{0:T(128)} %get-tuple-element.23.far_filled, bf16[512,256]{1,0:T(8,128)(2,1)} %collective-permute-done.2.k_prev_own_ref, ...), custom_call_target="tpu_custom_call" | custom-call | flops 2000000000 | bytes 8000000 | tf_op jit(solution)/shard_map/far/pallas_call | solution.py:527
  42.1 27.6 %all_to_all.10.parts_ref = f32[16,80,128]{2,1,0:T(8,128)} all-to-all(f32[16,80,128]{2,1,0:T(8,128)S(1)} %far.1), channel_id=1, replica_groups=mesh['za'=4,'zb'=2,'yh'=2,'x'=4,'core'=2,'head'=2] {'zb','yh','x'}, dimensions={0} | all-to-all | bytes 1310720 | tf_op jit(solution)/shard_map/all_to_all | solution.py:579
  69.7 2.1 %sum.1.own_ref = f32[120,128]{1,0:T(8,128)} custom-call(f32[16,80,128]{2,1,0:T(8,128)} %all_to_all.10.parts_ref), custom_call_target="tpu_custom_call" | custom-call | tf_op jit(solution)/shard_map/sum/pallas_call | solution.py:580
  71.7 2.9 %collective-permute-start.5 = (f32[120,128]{1,0:T(8,128)}, f32[120,128]{1,0:T(8,128)S(1)}, u32[]{:S(2)}, u32[]{:S(2)}) collective-permute-start(f32[120,128]{1,0:T(8,128)} %sum.1.own_ref), channel_id=1, source_target_pairs={{0,64},{64,0},{128,192},{192,128},{1,65},{65,1},{129,193},{193,129... | collective-permute-start | bytes 184328 | tf_op jit(solution)/shard_map/ppermute | solution.py:582
  74.7 1.7 %collective-permute-start.6 = (f32[120,128]{1,0:T(8,128)}, f32[120,128]{1,0:T(8,128)S(1)}, u32[]{:S(2)}, u32[]{:S(2)}) collective-permute-start(f32[120,128]{1,0:T(8,128)} %sum.1.own_ref), channel_id=1, source_target_pairs={{0,128},{64,192},{128,0},{192,64},{1,129},{65,193},{129,1},{193,65... | collective-permute-start | bytes 184328 | tf_op jit(solution)/shard_map/ppermute | solution.py:582
  76.4 1.6 %collective-permute-start.7 = (f32[120,128]{1,0:T(8,128)}, f32[120,128]{1,0:T(8,128)S(1)}, u32[]{:S(2)}, u32[]{:S(2)}) collective-permute-start(f32[120,128]{1,0:T(8,128)} %sum.1.own_ref), channel_id=1, source_target_pairs={{0,192},{64,128},{128,64},{192,0},{1,193},{65,129},{129,65},{193,1... | collective-permute-start | bytes 184328 | tf_op jit(solution)/shard_map/ppermute | solution.py:582
  78.0 4.1 %collective-permute-done.6.two_ref = f32[120,128]{1,0:T(8,128)S(1)} collective-permute-done((f32[120,128]{1,0:T(8,128)}, f32[120,128]{1,0:T(8,128)S(1)}, u32[]{:S(2)}, u32[]{:S(2)}) %collective-permute-start.6) | collective-permute-done | bytes 61472 | tf_op jit(solution)/shard_map/ppermute | solution.py:582
  82.1 0.9 collective-permute-done.7.three_ref
  83.6 1.8 %pack.1 = (s16[16,128,128]{2,1,0:T(8,128)(2,1)}, f32[8,128]{1,0:T(8,128)}) custom-call(f32[120,128]{1,0:T(8,128)} %sum.1.own_ref, f32[120,128]{1,0:T(8,128)} %copy-done.9, f32[120,128]{1,0:T(8,128)} %copy-done.10, f32[120,128]{1,0:T(8,128)} %copy-done.11), custom_call_target="tpu_custom_call" | custom-call | tf_op jit(solution)/shard_map/pack/pallas_call | solution.py:380
  85.4 16.1 %all_to_all.11.mine_ref = s16[16,128,128]{2,1,0:T(8,128)(2,1)S(1)} all-to-all(s16[16,128,128]{2,1,0:T(8,128)(2,1)} %get-tuple-element.31), channel_id=1, replica_groups=mesh['za'=4,'zb'=2,'yh'=2,'x'=4,'core'=2,'head'=2] {'zb','yh','x'}, dimensions={0} | all-to-all | bytes 1048576 | tf_op jit(solution)/shard_map/all_to_all | solution.py:588
  101.5 2.6 %collective-permute-start.8 = (s16[16,128,128]{2,1,0:T(8,128)(2,1)S(1)}, s16[16,128,128]{2,1,0:T(8,128)(2,1)S(1)}, u32[]{:S(2)}, u32[]{:S(2)}) collective-permute-start(s16[16,128,128]{2,1,0:T(8,128)(2,1)S(1)} %all_to_all.11.mine_ref), channel_id=1, source_target_pairs={{0,2},{2,0},{1,3},{3,1},{4,6},{6,4},{5,7},{7,5},{8,10},{10,8},{9,1... | collective-permute-start | bytes 1572872 | tf_op jit(solution)/shard_map/ppermute | solution.py:425
  105.4 1.7 %collective-permute-done.9 = f32[1,128]{1,0:T(1,128)S(1)} collective-permute-done((f32[1,128]{1,0:T(1,128)S(1)}, f32[1,128]{1,0:T(1,128)S(1)}, u32[]{:S(2)}, u32[]{:S(2)}) %collective-permute-start.9) | collective-permute-done | bytes 544 | tf_op jit(solution)/shard_map/ppermute | solution.py:425
  107.8 1.2 collective-permute-start.10
  108.9 0.8 collective-permute-done.10
  109.8 0.8 copy-done.8
  110.6 3.6 %unpack.1 = (f32[2048,128]{1,0:T(8,128)}, f32[1536,128]{1,0:T(8,128)}) custom-call(s32[2]{0:T(128)} %pad_add_fusion.place_ref.core_ref, s16[16,128,128]{2,1,0:T(8,128)(2,1)} %copy-done.7, s16[16,128,128]{2,1,0:T(8,128)(2,1)} %copy-done.8), custom_call_target="tpu_custom_call" | custom-call | tf_op jit(solution)/shard_map/unpack/pallas_call | solution.py:391
  (36 shorter events, 3.4 us)
Async XLA Ops:
  3.8 6.6 %copy-start.1 = (bf16[512,256]{1,0:T(8,128)(2,1)S(1)}, bf16[512,256]{1,0:T(8,128)(2,1)}, u32[]{:S(2)}) copy-start(bf16[512,256]{1,0:T(8,128)(2,1)} %get-tuple-element.19.after_ref.k_own_ref) | copy-start | bytes 786436
  3.8 17.8 %copy-start = (bf16[512,2048]{1,0:T(8,128)(2,1)S(1)}, bf16[512,2048]{1,0:T(8,128)(2,1)}, u32[]{:S(2)}) copy-start(bf16[512,2048]{1,0:T(8,128)(2,1)} %q_own_hbm.1) | copy-start | bytes 6291460
  3.8 17.8 %copy-start.2 = (s32[2]{0:T(128)S(1)}, s32[2]{0:T(128)}, u32[]{:S(2)}) copy-start(s32[2]{0:T(128)} %pad_add_fusion.place_ref.core_ref) | copy-start | bytes 28
  3.8 17.8 %copy-start.3 = (s32[8,24]{1,0:T(8,128)S(1)}, s32[8,24]{1,0:T(8,128)}, u32[]{:S(2)}) copy-start(s32[8,24]{1,0:T(8,128)} %offsets_ref.3) | copy-start | bytes 2308
  3.8 17.8 %copy-start.4 = (s32[8]{0:T(128)S(1)}, s32[8]{0:T(128)}, u32[]{:S(2)}) copy-start(s32[8]{0:T(128)} %counts_ref.3) | copy-start | bytes 100
  3.8 17.8 %copy-start.6 = (f32[4,384,128]{2,1,0:T(8,128)S(1)}, f32[4,384,128]{2,1,0:T(8,128)}, u32[]{:S(2)}) copy-start(f32[4,384,128]{2,1,0:T(8,128)} %wk_ref.1) | copy-start | bytes 2359300
  7.1 14.5 %collective-permute-start = (bf16[528,1024]{1,0:T(8,128)(2,1)}, bf16[528,1024]{1,0:T(8,128)(2,1)}, u32[]{:S(2)}, u32[]{:S(2)}) collective-permute-start(bf16[528,1024]{1,0:T(8,128)(2,1)} %cut_queries.1), channel_id=1, source_target_pairs={{0,2},{2,0},{1,3},{3,1},{4,6},{6,4},{5,7},{7,5},{8,10},{10,8},{9,1... | collective-permute-start | bytes 3244040 | tf_op jit(solution)/shard_map/ppermute | solution.py:425
  10.4 5.9 %collective-permute-start.1 = (bf16[512,256]{1,0:T(8,128)(2,1)}, bf16[512,256]{1,0:T(8,128)(2,1)S(1)}, u32[]{:S(2)}, u32[]{:S(2)}) collective-permute-start(bf16[512,256]{1,0:T(8,128)(2,1)} %get-tuple-element.20), channel_id=1, source_target_pairs={{0,2},{2,0},{1,3},{3,1},{4,6},{6,4},{5,7},{7,5},{8,10},{10,8},{9,1... | collective-permute-start | bytes 786440 | tf_op jit(solution)/shard_map/ppermute | solution.py:425
  10.4 25.6 %collective-permute-start.2 = (bf16[512,256]{1,0:T(8,128)(2,1)S(1)}, bf16[512,256]{1,0:T(8,128)(2,1)}, u32[]{:S(2)}, u32[]{:S(2)}) collective-permute-start(bf16[512,256]{1,0:T(8,128)(2,1)S(1)} %copy-done.1), channel_id=1, source_target_pairs={{0,4},{2,6},{4,8},{6,10},{8,12},{10,14},{12,16},{14,18},{16,20},{1... | collective-permute-start | bytes 786440 | tf_op jit(solution)/shard_map/ppermute | solution.py:564
  12.5 23.5 %collective-permute-start.3 = (bf16[512,256]{1,0:T(8,128)(2,1)}, bf16[512,256]{1,0:T(8,128)(2,1)}, u32[]{:S(2)}, u32[]{:S(2)}) collective-permute-start(bf16[512,256]{1,0:T(8,128)(2,1)} %get-tuple-element.20), channel_id=1, source_target_pairs={{0,6},{2,4},{4,10},{6,8},{8,14},{10,12},{12,18},{14,16},{16,22},{1... | collective-permute-start | bytes 786440 | tf_op jit(solution)/shard_map/ppermute | solution.py:565
  16.3 19.7 %collective-permute-start.4 = (bf16[512,256]{1,0:T(8,128)(2,1)S(1)}, bf16[512,256]{1,0:T(8,128)(2,1)S(1)}, u32[]{:S(2)}, u32[]{:S(2)}) collective-permute-start(bf16[512,256]{1,0:T(8,128)(2,1)S(1)} %broadcast_select_fusion), channel_id=1, source_target_pairs={{0,8},{2,10},{4,12},{6,14},{8,16},{10,18},{12,20},{14,22},{16,24},... | collective-permute-start | bytes 786440 | tf_op jit(solution)/shard_map/ppermute | solution.py:570
  21.7 1.2 %copy-start.5 = (f32[16,128,128]{2,1,0:T(8,128)S(1)}, f32[16,128,128]{2,1,0:T(8,128)}, u32[]{:S(2)}) copy-start(f32[16,128,128]{2,1,0:T(8,128)} %wq_hbm.1) | copy-start | bytes 3145732
  71.7 6.2 %collective-permute-start.5 = (f32[120,128]{1,0:T(8,128)}, f32[120,128]{1,0:T(8,128)S(1)}, u32[]{:S(2)}, u32[]{:S(2)}) collective-permute-start(f32[120,128]{1,0:T(8,128)} %sum.1.own_ref), channel_id=1, source_target_pairs={{0,64},{64,0},{128,192},{192,128},{1,65},{65,1},{129,193},{193,129... | collective-permute-start | bytes 184328 | tf_op jit(solution)/shard_map/ppermute | solution.py:582
  74.7 7.4 %collective-permute-start.6 = (f32[120,128]{1,0:T(8,128)}, f32[120,128]{1,0:T(8,128)S(1)}, u32[]{:S(2)}, u32[]{:S(2)}) collective-permute-start(f32[120,128]{1,0:T(8,128)} %sum.1.own_ref), channel_id=1, source_target_pairs={{0,128},{64,192},{128,0},{192,64},{1,129},{65,193},{129,1},{193,65... | collective-permute-start | bytes 184328 | tf_op jit(solution)/shard_map/ppermute | solution.py:582
  76.4 6.6 %collective-permute-start.7 = (f32[120,128]{1,0:T(8,128)}, f32[120,128]{1,0:T(8,128)S(1)}, u32[]{:S(2)}, u32[]{:S(2)}) collective-permute-start(f32[120,128]{1,0:T(8,128)} %sum.1.own_ref), channel_id=1, source_target_pairs={{0,192},{64,128},{128,64},{192,0},{1,193},{65,129},{129,65},{193,1... | collective-permute-start | bytes 184328 | tf_op jit(solution)/shard_map/ppermute | solution.py:582
  78.0 5.0 %copy-start.9 = (f32[120,128]{1,0:T(8,128)}, f32[120,128]{1,0:T(8,128)S(1)}, u32[]{:S(2)}) copy-start(f32[120,128]{1,0:T(8,128)S(1)} %collective-permute-done.5.one_ref) | copy-start | bytes 184324
  82.1 0.9 copy-start.10
  83.0 0.6 copy-start.11
  101.5 8.3 %copy-start.7 = (s16[16,128,128]{2,1,0:T(8,128)(2,1)}, s16[16,128,128]{2,1,0:T(8,128)(2,1)S(1)}, u32[]{:S(2)}) copy-start(s16[16,128,128]{2,1,0:T(8,128)(2,1)S(1)} %all_to_all.11.mine_ref) | copy-start | bytes 1572868
  101.5 8.3 %collective-permute-start.8 = (s16[16,128,128]{2,1,0:T(8,128)(2,1)S(1)}, s16[16,128,128]{2,1,0:T(8,128)(2,1)S(1)}, u32[]{:S(2)}, u32[]{:S(2)}) collective-permute-start(s16[16,128,128]{2,1,0:T(8,128)(2,1)S(1)} %all_to_all.11.mine_ref), channel_id=1, source_target_pairs={{0,2},{2,0},{1,3},{3,1},{4,6},{6,4},{5,7},{7,5},{8,10},{10,8},{9,1... | collective-permute-start | bytes 1572872 | tf_op jit(solution)/shard_map/ppermute | solution.py:425
  104.7 2.4 %collective-permute-start.9 = (f32[1,128]{1,0:T(1,128)S(1)}, f32[1,128]{1,0:T(1,128)S(1)}, u32[]{:S(2)}, u32[]{:S(2)}) collective-permute-start(f32[1,128]{1,0:T(1,128)S(1)} %slice.6), channel_id=1, source_target_pairs={{0,1},{1,0},{2,3},{3,2},{4,5},{5,4},{6,7},{7,6},{8,9},{9,8},{10,11... | collective-permute-start | bytes 1544 | tf_op jit(solution)/shard_map/ppermute | solution.py:425
  107.8 2.0 %collective-permute-start.10 = (f32[1,128]{1,0:T(1,128)S(1)}, f32[1,128]{1,0:T(1,128)S(1)}, u32[]{:S(2)}, u32[]{:S(2)}) collective-permute-start(f32[1,128]{1,0:T(1,128)S(1)} %slice_add_fusion), channel_id=1, source_target_pairs={{0,2},{2,0},{1,3},{3,1},{4,6},{6,4},{5,7},{7,5},{8,10},{10,8},{9,1... | collective-permute-start | bytes 1544 | tf_op jit(solution)/shard_map/ppermute | solution.py:425
  109.8 0.8 copy-start.8

commit v6 on v5

--- a/solution.py
+++ b/solution.py
@@ -34,21 +34,25 @@
 PART_ROWS = CHIP_BLOCKS + ROWS + KEY_ROWS + 8
 SUM_ROWS = HALF_HEAD + KEY_ROWS
 VMEM_BYTES = 40 * 1024 * 1024
-UNROLL = 3
+NEAR_UNROLL = 4
+FAR_UNROLL = 6
 NOTE_ROWS = 16
 TILE = 16
 LEVELS = 32760.0
-LIST_SIZE = CHIP_BLOCKS * CAND + 8
-WORK_SIZE = CHIP_BLOCKS * CAND // 4 + 8
+WORK_SIZE = CHIP_BLOCKS * CAND // 4 + 16
 LOW = -1e30
 EXP_SCALE = math.log2(math.e) / math.sqrt(HEAD_DIM)
-HIGH = lax.Precision.HIGHEST
 
 
 def dot_f32(a, b, dims):
-    return lax.dot_general(
-        a, b, (dims, ((), ())), precision=HIGH, preferred_element_type=jnp.float32
-    )
+    def one(x, y):
+        return lax.dot_general(x, y, (dims, ((), ())), preferred_element_type=jnp.float32)
+
+    a_top = a.astype(jnp.bfloat16)
+    b_top = b.astype(jnp.bfloat16)
+    a_low = (a - a_top.astype(jnp.float32)).astype(jnp.bfloat16)
+    b_low = (b - b_top.astype(jnp.float32)).astype(jnp.bfloat16)
+    return one(a_top, b_top) + (one(a_top, b_low) + one(a_low, b_top))
 
 
 def pool_keys(tile):
@@ -64,43 +68,44 @@
     ]
 
 
-def make_lists(core, chip, tables, near_list, near_work, far_list, far_work):
-    filled = (jnp.int32(0), jnp.int32(0))
-    for source, table in enumerate(tables):
-        first = ROWS * core if source == 0 else ROWS * (1 - core)
-
-        def per_block(j, filled):
-            block = first + j
-            limit = chip * CHIP_BLOCKS + block
-            count = table(j, CAND)
-            base = (source * ROWS + j) * CAND
-            near_end = far_end = base
-            for c in range(CAND):
-                offset = table(j, c)
-                here = (c < count) & (offset <= limit)
-                near = jnp.where(here & (offset <= block), 1, 0)
-                far = jnp.where(here & (offset > block), 1, 0)
-                near_list[near_end] = SPAN - offset
-                far_list[far_end] = SPAN - offset
-                near_end += near
-                far_end += far
-            out = []
-            for end, slots, work, total in zip(
-                (near_end, far_end), (near_list, far_list), (near_work, far_work), filled
-            ):
-                for extra in range(3):
-                    slots[end + extra] = DUMMY
-                for i in range(CAND // 4):
-                    work[total] = base + i * 4
-                    total += jnp.where(i * 4 < end - base, 1, 0)
-                out.append(total)
-            return tuple(out)
-
-        filled = lax.fori_loop(0, ROWS, per_block, filled)
-    for work, total in zip((near_work, far_work), filled):
-        spare = jnp.where(total > 0, work[jnp.maximum(total - 1, 0)], 0)
-        for extra in range(UNROLL - 1):
-            work[total + extra] = spare
+def make_lists(core, chip, table):
+    shape = (CHIP_BLOCKS, HEAD_DIM)
+    lane = lax.broadcasted_iota(jnp.int32, shape, 1)
+    row = lax.broadcasted_iota(jnp.int32, shape, 0)
+    block = position(core, row)
+    offset = table.astype(jnp.int32)
+    count = jnp.sum(jnp.where(lane == CAND, table, 0.0), axis=1, keepdims=True).astype(jnp.int32)
+    usable = (lane < count) & (offset <= chip * CHIP_BLOCKS + block)
+    near = jnp.where(usable & (offset <= block), 1.0, 0.0)
+    far = jnp.where(usable & (offset > block), 1.0, 0.0)
+    picked = jnp.concatenate([near, far], axis=0)
+    before = jnp.where(
+        lax.broadcasted_iota(jnp.int32, (HEAD_DIM, HEAD_DIM), 0)
+        < lax.broadcasted_iota(jnp.int32, (HEAD_DIM, HEAD_DIM), 1), 1.0, 0.0,
+    ).astype(jnp.bfloat16)
+    rank = jnp.dot(picked.astype(jnp.bfloat16), before, preferred_element_type=jnp.float32)
+    rank = jnp.where(picked > 0.0, rank, -1.0)
+    value = (SPAN - DUMMY) - jnp.concatenate([table, table], axis=0)
+    lane = jnp.concatenate([lane, lane], axis=0)
+    packed = jnp.where(lane == CAND, jnp.sum(picked, axis=1, keepdims=True), float(DUMMY))
+    for slot in range(CAND):
+        here = jnp.sum(jnp.where(rank == slot, value, 0.0), axis=1, keepdims=True)
+        packed = jnp.where(lane == slot, here + DUMMY, packed)
+    return packed.astype(jnp.int32)
+
+
+def make_work(list_ref, work, unroll):
+    def per_block(s, total):
+        count = list_ref[s, CAND]
+        for i in range(CAND // 4):
+            work[total] = s * CAND + i * 4
+            total += jnp.where(i * 4 < count, 1, 0)
+        return total
+
+    filled = lax.fori_loop(0, CHIP_BLOCKS, per_block, jnp.int32(0))
+    spare = work[jnp.maximum(filled - 1, 0)]
+    for extra in range(unroll - 1):
+        work[filled + extra] = spare
     return filled
 
 
@@ -108,17 +113,17 @@
     return jnp.where(s < ROWS, ROWS * core + s, ROWS * (1 - core) + s - ROWS)
 
 
-def slot_loop(filled, work, list_ref, tile_start, keys, queries, slot_max, slot_sum, diagonal):
+def slot_loop(filled, work, unroll, list_ref, tile_start, keys, queries, slot_max, slot_sum, diagonal):
     lane = lax.broadcasted_iota(jnp.int32, (BLOCK, WIDTH), 1) % BLOCK
     key_row = lax.broadcasted_iota(jnp.int32, (BLOCK, WIDTH), 0)
 
-    @pl.loop(0, (filled + UNROLL - 1) // UNROLL)
+    @pl.loop(0, (filled + unroll - 1) // unroll)
     def _(step):
         found = []
-        for e in range(UNROLL):
-            first = work[step * UNROLL + e]
+        for e in range(unroll):
+            first = work[step * unroll + e]
             s = first // CAND
-            rows = [list_ref[first + i] for i in range(4)]
+            rows = [list_ref[s, first - s * CAND + i] for i in range(4)]
             starts = [pl.multiple_of(tile_start(s, row) * BLOCK, BLOCK) for row in rows]
             if diagonal:
                 keep = key_row <= lane + jnp.where(first == s * CAND, 0, BLOCK)
@@ -148,13 +153,10 @@
     place_ref, offsets_ref, counts_ref,
     q_own_hbm, q_other_ref, k_own_ref, k_other_ref, wq_hbm, wk_hbm,
     queries, slot_max, slot_sum, pooled_query, gate_query, pooled_key, gate_key,
-    far_list, far_work, far_filled,
-    keys, near_list, near_work, note_vector, note_scalar, q_own_ref, wq_ref, wk_ref, sems,
+    far_list,
+    keys, near_vector, near_list, near_work, q_own_ref, wq_ref, wk_ref, sems,
 ):
     core_ref = place_ref
-    note_vector[...] = q_other_ref[ROWS * BLOCK:, 0:HEAD_DIM].astype(jnp.float32).astype(jnp.int32)
-    note_copy = pltpu.make_async_copy(note_vector, note_scalar, sems.at[0])
-    note_copy.start()
     core = core_ref[0]
     half = ROWS * BLOCK
     q_copy = pltpu.make_async_copy(
@@ -169,6 +171,21 @@
     q_copy.start()
     wq_copy.start()
     wk_copy.start()
+    table = jnp.concatenate(
+        [offsets_ref[...], jnp.zeros((ROWS, HEAD_DIM - CAND), jnp.int32)], axis=1
+    )
+    row = lax.broadcasted_iota(jnp.int32, (ROWS, HEAD_DIM), 0)
+    lane = lax.broadcasted_iota(jnp.int32, (ROWS, HEAD_DIM), 1)
+    for j in range(ROWS):
+        table = jnp.where((lane == CAND) & (row == j), counts_ref[j], table)
+    note = q_other_ref[half:, 0:HEAD_DIM].astype(jnp.float32)
+    lists = make_lists(
+        core, place_ref[1], jnp.concatenate([table.astype(jnp.float32), note[0:ROWS]], axis=0)
+    )
+    far_list[...] = lists[CHIP_BLOCKS:]
+    near_vector[...] = lists[0:CHIP_BLOCKS]
+    list_copy = pltpu.make_async_copy(near_vector, near_list, sems.at[0])
+    list_copy.start()
     for source, ref in ((core, k_own_ref), (1 - core, k_other_ref)):
         tile = ref[...]
         keys[pl.ds(pl.multiple_of(source * half, half), half), :] = tile
@@ -196,18 +213,10 @@
 
     slot_max[...] = jnp.full_like(slot_max, LOW)
     slot_sum[...] = jnp.zeros_like(slot_sum)
-    note_copy.wait()
-    filled, filled_far = make_lists(
-        core, place_ref[1],
-        (
-            lambda j, c: counts_ref[j] if c == CAND else offsets_ref[j, c],
-            lambda j, c: note_scalar[j, c],
-        ),
-        near_list, near_work, far_list, far_work,
-    )
-    far_filled[0] = filled_far
+    list_copy.wait()
+    filled = make_work(near_list, near_work, NEAR_UNROLL)
     slot_loop(
-        filled, near_work, near_list,
+        filled, near_work, NEAR_UNROLL, near_list,
         lambda s, row: position(core, s) + jnp.minimum(row, SPAN) - SPAN,
         keys, queries, slot_max, slot_sum, True,
     )
@@ -223,11 +232,11 @@
 
 
 def far_kernel(
-    core_ref, far_list, far_work, far_filled,
+    core_ref, far_list,
     k_prev_own_ref, k_prev_other_ref, k_far_ref, queries,
     max_ref, sum_ref, pooled_query, gate_query, near_key, near_gate_key, wk_ref,
     out_ref,
-    keys, slot_max, slot_sum, pooled_key, shares, hits,
+    keys, slot_max, slot_sum, pooled_key, shares, hits, far_work,
 ):
     core = core_ref[0]
     half = ROWS * BLOCK
@@ -244,8 +253,9 @@
     slot_sum[...] = sum_ref[...]
     shares[...] = jnp.zeros_like(shares)
     hits[...] = jnp.zeros_like(hits)
+    filled = make_work(far_list, far_work, FAR_UNROLL)
     slot_loop(
-        far_filled[0], far_work, far_list,
+        filled, far_work, FAR_UNROLL, far_list,
         lambda s, row: jnp.where(row <= SPAN, position(core, s) + row, 0),
         keys, queries, slot_max, slot_sum, False,
     )
@@ -361,19 +371,17 @@
 def unpack_kernel(place_ref, mine_ref, other_ref, query_ref, key_ref):
     core = place_ref[0]
     for source, ref in ((core, mine_ref), (1 - core, other_ref)):
-
-        @pl.loop(0, SHARES)
-        def _(share):
-            coded = ref[share].astype(jnp.int32).astype(jnp.float32)
-            scale = jnp.exp2(coded[SUM_ROWS:, :]) * (1.0 / LEVELS)
+        for share in range(SHARES):
+            powers = ref[share, SUM_ROWS:SUM_ROWS + TILE, :].astype(jnp.int32).astype(jnp.float32)
+            scale = jnp.exp2(powers[0:8, :]) * (1.0 / LEVELS)
             for tile in range(SUM_ROWS // TILE):
-                value = coded[tile * TILE:(tile + 1) * TILE, :] * scale[tile:tile + 1, :]
+                coded = ref[share, tile * TILE:(tile + 1) * TILE, :]
+                value = coded.astype(jnp.int32).astype(jnp.float32) * scale[tile:tile + 1, :]
                 if tile < HALF_HEAD // TILE:
-                    at = source * (SHARES * HALF_HEAD) + share * HALF_HEAD + tile * TILE
-                    query_ref[pl.ds(pl.multiple_of(at, TILE), TILE), :] = value
+                    query_ref[source, pl.ds(share * HALF_HEAD + tile * TILE, TILE), :] = value
                 else:
-                    at = source * (SHARES * KEY_ROWS) + share * KEY_ROWS + tile * TILE - HALF_HEAD
-                    key_ref[pl.ds(pl.multiple_of(at, TILE), TILE), :] = value
+                    at = share * KEY_ROWS + tile * TILE - HALF_HEAD
+                    key_ref[source, pl.ds(at, TILE), :] = value
 
 
 def pack(*parts):
@@ -387,23 +395,18 @@
 
 
 def unpack(place, mine, other):
-    rows = 2 * SHARES * HALF_HEAD, 2 * SHARES * KEY_ROWS
+    rows = SHARES * HALF_HEAD, SHARES * KEY_ROWS
     return pl.pallas_call(
         unpack_kernel,
         grid_spec=pltpu.PrefetchScalarGridSpec(
             num_scalar_prefetch=1,
             grid=(1,),
             in_specs=[whole(*mine.shape)] * 2,
-            out_specs=[whole(n, HEAD_DIM) for n in rows],
+            out_specs=[whole(2, n, HEAD_DIM) for n in rows],
         ),
-        out_shape=[shaped((n, HEAD_DIM)) for n in rows],
+        out_shape=[shaped((2, n, HEAD_DIM)) for n in rows],
         name="unpack",
     )(place, mine, other)
-
-
-def cut_keys_kernel(place_ref, mine_in, give_in, mine_ref, give_ref):
-    mine_ref[...] = mine_in[...]
-    give_ref[...] = give_in[...]
 
 
 def cut_queries_kernel(place_ref, counts_ref, offsets_ref, give_in, after_ref, give_ref):
@@ -435,24 +438,6 @@
 
 def smem():
     return pl.BlockSpec(memory_space=pltpu.SMEM)
-
-
-def cut_keys(place, keys):
-    half = ROWS * BLOCK
-    return pl.pallas_call(
-        cut_keys_kernel,
-        grid_spec=pltpu.PrefetchScalarGridSpec(
-            num_scalar_prefetch=1,
-            grid=(1,),
-            in_specs=[
-                pl.BlockSpec((half, K_COLS), lambda i, c: (0, c[0])),
-                pl.BlockSpec((half, K_COLS), lambda i, c: (0, 1 - c[0])),
-            ],
-            out_specs=[whole(half, K_COLS)] * 2,
-        ),
-        out_shape=[shaped((half, K_COLS), jnp.bfloat16)] * 2,
-        name="cut_keys",
-    )(place, keys, keys)
 
 
 def cut_queries(place, queries, offsets, counts, after):
@@ -471,6 +456,9 @@
             out_specs=whole(half + NOTE_ROWS, Q_COLS),
         ),
         out_shape=shaped((half + NOTE_ROWS, Q_COLS), jnp.bfloat16),
+        cost_estimate=pl.CostEstimate(
+            flops=0, bytes_accessed=30_000_000, transcendentals=0
+        ),
         name="cut_queries",
     )(place, counts, offsets, queries, after)
 
@@ -485,14 +473,14 @@
         shaped((KV_HERE, LANES, HEAD_DIM)),
         shaped((KV_HERE, CHIP_BLOCKS, POOL)),
         shaped((KV_HERE, CHIP_BLOCKS, HEAD_DIM)),
+        shaped((CHIP_BLOCKS, HEAD_DIM), jnp.int32),
     ]
-    lists = [LIST_SIZE, WORK_SIZE, 1]
     return pl.pallas_call(
         near_kernel,
         grid_spec=pltpu.PrefetchScalarGridSpec(
             num_scalar_prefetch=1,
             grid=(1,),
-            in_specs=[smem()] * 2 + [
+            in_specs=[whole(ROWS, CAND), smem()] + [
                 pl.BlockSpec(memory_space=pltpu.HBM),
                 whole(half + NOTE_ROWS, Q_COLS),
                 whole(half, K_COLS),
@@ -500,20 +488,19 @@
                 pl.BlockSpec(memory_space=pltpu.HBM),
                 pl.BlockSpec(memory_space=pltpu.HBM),
             ],
-            out_specs=[whole(*o.shape) for o in outs] + [smem()] * 3,
+            out_specs=[whole(*o.shape) for o in outs],
             scratch_shapes=[
                 pltpu.VMEM((CHIP_BLOCKS * BLOCK, K_COLS), jnp.bfloat16),
-                pltpu.SMEM((LIST_SIZE,), jnp.int32),
+                pltpu.VMEM((CHIP_BLOCKS, HEAD_DIM), jnp.int32),
+                pltpu.SMEM((CHIP_BLOCKS, HEAD_DIM), jnp.int32),
                 pltpu.SMEM((WORK_SIZE,), jnp.int32),
-                pltpu.VMEM((NOTE_ROWS, HEAD_DIM), jnp.int32),
-                pltpu.SMEM((NOTE_ROWS, HEAD_DIM), jnp.int32),
                 pltpu.VMEM((half, Q_COLS), jnp.bfloat16),
                 pltpu.VMEM((HEADS_HERE, HEAD_DIM, HEAD_DIM), jnp.float32),
                 pltpu.VMEM((KV_HERE, POOL, HEAD_DIM), jnp.float32),
                 pltpu.SemaphoreType.DMA((4,)),
             ],
         ),
-        out_shape=outs + [shaped((n,), jnp.int32) for n in lists],
+        out_shape=outs,
         compiler_params=pltpu.CompilerParams(vmem_limit_bytes=VMEM_BYTES),
         cost_estimate=pl.CostEstimate(
             flops=2_000_000_000, bytes_accessed=8_000_000, transcendentals=8_000_000
@@ -523,13 +510,13 @@
 
 
 def far_call(place, k_prev_own, k_prev_other, k_far, near, wk):
-    args = (k_prev_own, k_prev_other, k_far, *near[:-3])
+    args = (k_prev_own, k_prev_other, k_far, *near[:-1])
     return pl.pallas_call(
         far_kernel,
         grid_spec=pltpu.PrefetchScalarGridSpec(
             num_scalar_prefetch=1,
             grid=(1,),
-            in_specs=[smem()] * 3 + [whole(*a.shape) for a in args] + [
+            in_specs=[smem()] + [whole(*a.shape) for a in args] + [
                 pl.BlockSpec((KV_HERE, POOL, HEAD_DIM), lambda i, c: (c[0], 0, 0)),
             ],
             out_specs=whole(SHARES, PART_ROWS, HEAD_DIM),
@@ -540,6 +527,7 @@
                 pltpu.VMEM((KV_HERE, SPAN + CHIP_BLOCKS, POOL), jnp.float32),
                 pltpu.VMEM((KV_HERE, PADDED, LANES), jnp.float32),
                 pltpu.VMEM((PADDED, LANES), jnp.float32),
+                pltpu.SMEM((WORK_SIZE,), jnp.int32),
             ],
         ),
         out_shape=shaped((SHARES, PART_ROWS, HEAD_DIM)),
@@ -548,7 +536,7 @@
             flops=2_000_000_000, bytes_accessed=8_000_000, transcendentals=8_000_000
         ),
         name="far",
-    )(place, *near[-3:], *args, wk)
+    )(place, near[-1], *args, wk)
 
 
 def body(
@@ -560,7 +548,8 @@
     core = lax.axis_index("core")
     place = jnp.stack([core, lax.axis_index(chips)]).astype(jnp.int32)
 
-    k_mine, k_give = cut_keys(place, teacher_keys)
+    k_mine = lax.dynamic_slice_in_dim(teacher_keys, core * K_COLS, K_COLS, 1)
+    k_give = lax.dynamic_slice_in_dim(teacher_keys, (1 - core) * K_COLS, K_COLS, 1)
     k_prev_own = lax.ppermute(k_mine, places, [(i, i + 2) for i in range(count - 2)])
     k_prev_other = lax.ppermute(
         k_give, places, [(i, (i ^ 1) + 2) for i in range(count - 2)]

time: 116 us -> 115 us (level)
  Pallas kernels: 32.4 us -> 23.5 us
  starting transfers between devices: 25 us -> 28.4 us
  other arithmetic: 1.37 us -> 3.44 us
    pallas_call x1, Pallas kernels: 13.1 us -> 8.42 us  [near_call(): pl.pallas_call(near_kernel, grid_spec=pltpu.PrefetchScalarGridSpec(num_sc...]
    pallas_call x1 -> x0, Pallas kernels: 2.5 us -> none  [cut_keys(): pl.pallas_call(cut_keys_kernel, grid_spec=pltpu.PrefetchScalarGridSpec(nu...]
    all_to_all x1, blocking collectives: 16.1 us -> 13.8 us  [body(): mine = lax.all_to_all(coded, group, 0, 0)]
    ppermute x1, starting transfers between devices: 3.8 us -> 1.63 us  [body(): lax.ppermute(k_give, places, [(i, (i ^ 1) + 2) for i in range(count - 2)])]
    all_to_all x1, blocking collectives: 27.6 us -> 29.7 us  [body(): got = lax.all_to_all(parts, group, 0, 0)]
    ppermute x5, starting transfers between devices: 7.59 us -> 9.68 us  [swap(): return lax.ppermute(x, axis, [(0, 1), (1, 0)])]
    select_n x1, other arithmetic: 0.03 us -> 2.09 us  [body(): jnp.where(core == 1, k_mine, k_other)]
    ppermute x3, starting transfers between devices: 6.24 us -> 8.01 us  [body(): lax.ppermute(got, 'za', [(i, i ^ step) for i in range(4)])]
  transfers between devices with their start and end apart: 11 -> 11, of which waited for: 4 -> 5; matrix products, arithmetic and copies ran while one was open for 1% -> 2% of each run, Pallas kernels for 11% -> 7%
where the time goes in v6:
time: 115 us; the launch traced here: 114 us
  blocking collectives  43.4 us (38%)
  starting transfers between devices  28.4 us (25%)
  Pallas kernels  23.5 us (20%)
  waiting for transfers between devices  8.45 us (7%)
  local copies, waits for them, and re-layouts  4.33 us (4%)
  other arithmetic  3.44 us (3%)
  between operations  2 us (2%)
    all_to_all x1, blocking collectives, body(): got = lax.all_to_all(parts, group, 0, 0)  29.7 us
    all_to_all x1, blocking collectives, body(): mine = lax.all_to_all(coded, group, 0, 0)  13.8 us
    ppermute x5, starting transfers between devices, swap(): return lax.ppermute(x, axis, [(0, 1), (1, 0)])  9.68 us
    pallas_call x1, Pallas kernels, near_call(): pl.pallas_call(near_kernel, grid_spec=pltpu.PrefetchScalarGridSpec(num_sc...  8.42 us
    ppermute x3, starting transfers between devices, body(): lax.ppermute(got, 'za', [(i, i ^ step) for i in range(4)])  8.01 us
    ppermute x3, waiting for transfers between devices, body(): lax.ppermute(got, 'za', [(i, i ^ step) for i in range(4)])  6.04 us
    ppermute x1, starting transfers between devices, body(): lax.ppermute(jnp.where(core == 1, k_mine, k_other), places, [(i, i + 4) f...  5.98 us
    pallas_call x1, Pallas kernels, far_call(): pl.pallas_call(far_kernel, grid_spec=pltpu.PrefetchScalarGridSpec(num_sca...  4.84 us
  transfers between devices with their start and end apart: 11, of which 5 were waited for; matrix products, arithmetic and copies ran while one was open for 2% of the time, Pallas kernels for 7%

profile of v6, /device:TPU:1, one launch (start us, length us, event | category | flops | bytes accessed | tf_op | source)
XLA Modules:
  0.0 113.6 jit_solution(10383907349418050098)
XLA Ops:
  0.6 1.0 constant_dynamic-slice_fusion
  1.6 3.3 %collective-permute-start.1 = (bf16[512,256]{1,0:T(8,128)(2,1)S(1)}, bf16[512,256]{1,0:T(8,128)(2,1)S(1)}, u32[]{:S(2)}, u32[]{:S(2)}) collective-permute-start(bf16[512,256]{1,0:T(8,128)(2,1)S(1)} %constant_dynamic-slice_fusion), channel_id=1, source_target_pairs={{0,2},{2,0},{1,3},{3,1},{4,6},{6,4},{5,7},{7,5},{8,10},{10,8},{9,1... | collective-permute-start | bytes 786440 | tf_op jit(solution)/shard_map/ppermute | solution.py:428
  6.1 2.1 %broadcast_select_fusion = (bf16[512,256]{1,0:T(8,128)(2,1)}, bf16[512,256]{1,0:T(8,128)(2,1)}) fusion(bf16[512,256]{1,0:T(8,128)(2,1)S(1)} %collective-permute-done.1.k_other_ref, pred[]{:T(512)S(6)} %eq.3, bf16[512,512]{1,0:T(8,128)(2,1)} %param.7, s32[]{:T(128)S(6)} %select_n.14), kind=kLoop, calls=%fused_computation | loop fusion | flops 131072 | bytes 1048581 | tf_op jit(solution)/shard_map/jit(_where)/select_n | solution.py:560
  8.2 3.1 %cut_queries.1 = bf16[528,1024]{1,0:T(8,128)(2,1)} custom-call(s32[2]{0:T(128)} %pad_add_fusion.place_ref.core_ref, s32[8]{0:T(128)} %counts_ref.3, s32[8,24]{1,0:T(8,128)} %offsets_ref.3, bf16[512,2048]{1,0:T(8,128)(2,1)} %q_own_hbm.1, bf16[512,256]{1,0:T(8,128)(2,1)} %get-tuple-element.28.after_ref.k_own_ref), custom_call_target="tpu_custom_call" | custom-call | bytes 30000000 | tf_op jit(solution)/shard_map/cut_queries/pallas_call | solution.py:445
  11.5 1.6 %collective-permute-start.3 = (bf16[512,256]{1,0:T(8,128)(2,1)}, bf16[512,256]{1,0:T(8,128)(2,1)S(1)}, u32[]{:S(2)}, u32[]{:S(2)}) collective-permute-start(bf16[512,256]{1,0:T(8,128)(2,1)} %copy-done.9), channel_id=1, source_target_pairs={{0,6},{2,4},{4,10},{6,8},{8,14},{10,12},{12,18},{14,16},{16,22},{1... | collective-permute-start | bytes 786440 | tf_op jit(solution)/shard_map/ppermute | solution.py:554
  13.1 3.1 %collective-permute-start.2 = (bf16[512,256]{1,0:T(8,128)(2,1)S(1)}, bf16[512,256]{1,0:T(8,128)(2,1)S(1)}, u32[]{:S(2)}, u32[]{:S(2)}) collective-permute-start(bf16[512,256]{1,0:T(8,128)(2,1)S(1)} %copy-done.1), channel_id=1, source_target_pairs={{0,4},{2,6},{4,8},{6,10},{8,12},{10,14},{12,16},{14,18},{16,20},{1... | collective-permute-start | bytes 786440 | tf_op jit(solution)/shard_map/ppermute | solution.py:553
  16.3 6.0 %collective-permute-start.4 = (bf16[512,256]{1,0:T(8,128)(2,1)}, bf16[512,256]{1,0:T(8,128)(2,1)S(1)}, u32[]{:S(2)}, u32[]{:S(2)}) collective-permute-start(bf16[512,256]{1,0:T(8,128)(2,1)} %get-tuple-element.27), channel_id=1, source_target_pairs={{0,8},{2,10},{4,12},{6,14},{8,16},{10,18},{12,20},{14,22},{16,24},... | collective-permute-start | bytes 786440 | tf_op jit(solution)/shard_map/ppermute | solution.py:559
  22.3 1.2 %copy-done.5 = f32[16,128,128]{2,1,0:T(8,128)S(1)} copy-done((f32[16,128,128]{2,1,0:T(8,128)S(1)}, f32[16,128,128]{2,1,0:T(8,128)}, u32[]{:S(2)}) %copy-start.5) | copy-done | bytes 1048600
  23.5 8.4 %near.1 = (bf16[32,256,128]{2,1,0:T(8,128)(2,1)S(1)}, f32[32,32,256]{2,1,0:T(8,128)S(1)}, f32[32,32,256]{2,1,0:T(8,128)S(1)}, f32[2,64,128]{2,1,0:T(8,128)S(1)},...) custom-call(s32[2]{0:T(128)S(1)} %copy-done.3, ...), custom_call_target="tpu_custom_call" | custom-call | flops 2000000000 | bytes 8000000 | tf_op jit(solution)/shard_map/near/pallas_call | solution.py:478
  32.0 4.8 %far.1 = f32[16,80,128]{2,1,0:T(8,128)S(1)} custom-call(s32[2]{0:T(128)S(1)} %copy-done.3, s32[16,128]{1,0:T(8,128)S(1)} %get-tuple-element.15.far_list, bf16[512,256]{1,0:T(8,128)(2,1)S(1)} %collective-permute-done.2.k_prev_own_ref, bf16[512,256]{1,0:T(8,128)(2,1)S(1)} %collective-permute-done.3.k_prev_other_ref, ...), custom_call_target="tpu_custom_call" | custom-call | flops 2000000000 | bytes 8000000 | tf_op jit(solution)/shard_map/far/pallas_call | solution.py:514
  36.8 29.7 %all_to_all.10.parts_ref = f32[16,80,128]{2,1,0:T(8,128)} all-to-all(f32[16,80,128]{2,1,0:T(8,128)S(1)} %far.1), channel_id=1, replica_groups=mesh['za'=4,'zb'=2,'yh'=2,'x'=4,'core'=2,'head'=2] {'zb','yh','x'}, dimensions={0} | all-to-all | bytes 1310720 | tf_op jit(solution)/shard_map/all_to_all | solution.py:568
  66.5 2.0 %sum.1.own_ref = f32[120,128]{1,0:T(8,128)} custom-call(f32[16,80,128]{2,1,0:T(8,128)} %all_to_all.10.parts_ref), custom_call_target="tpu_custom_call" | custom-call | tf_op jit(solution)/shard_map/sum/pallas_call | solution.py:569
  68.5 3.8 %collective-permute-start.5 = (f32[120,128]{1,0:T(8,128)}, f32[120,128]{1,0:T(8,128)S(1)}, u32[]{:S(2)}, u32[]{:S(2)}) collective-permute-start(f32[120,128]{1,0:T(8,128)} %sum.1.own_ref), channel_id=1, source_target_pairs={{0,64},{64,0},{128,192},{192,128},{1,65},{65,1},{129,193},{193,129... | collective-permute-start | bytes 184328 | tf_op jit(solution)/shard_map/ppermute | solution.py:571
  72.3 4.0 %collective-permute-start.6 = (f32[120,128]{1,0:T(8,128)}, f32[120,128]{1,0:T(8,128)S(1)}, u32[]{:S(2)}, u32[]{:S(2)}) collective-permute-start(f32[120,128]{1,0:T(8,128)} %sum.1.own_ref), channel_id=1, source_target_pairs={{0,128},{64,192},{128,0},{192,64},{1,129},{65,193},{129,1},{193,65... | collective-permute-start | bytes 184328 | tf_op jit(solution)/shard_map/ppermute | solution.py:571
  76.5 3.0 %collective-permute-done.6.two_ref = f32[120,128]{1,0:T(8,128)S(1)} collective-permute-done((f32[120,128]{1,0:T(8,128)}, f32[120,128]{1,0:T(8,128)S(1)}, u32[]{:S(2)}, u32[]{:S(2)}) %collective-permute-start.6) | collective-permute-done | bytes 61472 | tf_op jit(solution)/shard_map/ppermute | solution.py:571
  79.5 3.0 %collective-permute-done.7.three_ref = f32[120,128]{1,0:T(8,128)S(1)} collective-permute-done((f32[120,128]{1,0:T(8,128)}, f32[120,128]{1,0:T(8,128)S(1)}, u32[]{:S(2)}, u32[]{:S(2)}) %collective-permute-start.7) | collective-permute-done | bytes 61472 | tf_op jit(solution)/shard_map/ppermute | solution.py:571
  83.2 1.8 %pack.1 = (s16[16,128,128]{2,1,0:T(8,128)(2,1)}, f32[8,128]{1,0:T(8,128)}) custom-call(f32[120,128]{1,0:T(8,128)} %sum.1.own_ref, f32[120,128]{1,0:T(8,128)} %copy-done.10, f32[120,128]{1,0:T(8,128)} %copy-done.11, f32[120,128]{1,0:T(8,128)} %copy-done.12), custom_call_target="tpu_custom_call" | custom-call | tf_op jit(solution)/shard_map/pack/pallas_call | solution.py:388
  85.0 13.8 %all_to_all.11.mine_ref = s16[16,128,128]{2,1,0:T(8,128)(2,1)S(1)} all-to-all(s16[16,128,128]{2,1,0:T(8,128)(2,1)} %get-tuple-element.23), channel_id=1, replica_groups=mesh['za'=4,'zb'=2,'yh'=2,'x'=4,'core'=2,'head'=2] {'zb','yh','x'}, dimensions={0} | all-to-all | bytes 1048576 | tf_op jit(solution)/shard_map/all_to_all | solution.py:577
  98.8 3.8 %collective-permute-start.8 = (s16[16,128,128]{2,1,0:T(8,128)(2,1)S(1)}, s16[16,128,128]{2,1,0:T(8,128)(2,1)S(1)}, u32[]{:S(2)}, u32[]{:S(2)}) collective-permute-start(s16[16,128,128]{2,1,0:T(8,128)(2,1)S(1)} %all_to_all.11.mine_ref), channel_id=1, source_target_pairs={{0,2},{2,0},{1,3},{3,1},{4,6},{6,4},{5,7},{7,5},{8,10},{10,8},{9,1... | collective-permute-start | bytes 1572872 | tf_op jit(solution)/shard_map/ppermute | solution.py:428
  103.2 1.3 %collective-permute-start.9 = (f32[1,128]{1,0:T(1,128)S(1)}, f32[1,128]{1,0:T(1,128)S(1)}, u32[]{:S(2)}, u32[]{:S(2)}) collective-permute-start(f32[1,128]{1,0:T(1,128)S(1)} %slice.6), channel_id=1, source_target_pairs={{0,1},{1,0},{2,3},{3,2},{4,5},{5,4},{6,7},{7,6},{8,9},{9,8},{10,11... | collective-permute-start | bytes 1544 | tf_op jit(solution)/shard_map/ppermute | solution.py:428
  104.5 1.1 collective-permute-done.9
  106.3 1.2 %collective-permute-start.10 = (f32[1,128]{1,0:T(1,128)S(1)}, f32[1,128]{1,0:T(1,128)S(1)}, u32[]{:S(2)}, u32[]{:S(2)}) collective-permute-start(f32[1,128]{1,0:T(1,128)S(1)} %slice_add_fusion), channel_id=1, source_target_pairs={{0,2},{2,0},{1,3},{3,1},{4,6},{6,4},{5,7},{7,5},{8,10},{10,8},{9,1... | collective-permute-start | bytes 1544 | tf_op jit(solution)/shard_map/ppermute | solution.py:428
  107.4 0.8 collective-permute-done.10
  109.1 3.3 %unpack.1 = (f32[2,1024,128]{2,1,0:T(8,128)}, f32[2,768,128]{2,1,0:T(8,128)}) custom-call(s32[2]{0:T(128)} %pad_add_fusion.place_ref.core_ref, s16[16,128,128]{2,1,0:T(8,128)(2,1)} %copy-done.7, s16[16,128,128]{2,1,0:T(8,128)(2,1)} %copy-done.8), custom_call_target="tpu_custom_call" | custom-call | tf_op jit(solution)/shard_map/unpack/pallas_call | solution.py:399
  (38 shorter events, 4.4 us)
Async XLA Ops:
  1.6 4.5 %copy-start.9 = (bf16[512,256]{1,0:T(8,128)(2,1)}, bf16[512,256]{1,0:T(8,128)(2,1)S(1)}, u32[]{:S(2)}) copy-start(bf16[512,256]{1,0:T(8,128)(2,1)S(1)} %constant_dynamic-slice_fusion) | copy-start | bytes 786436
  1.6 4.5 %collective-permute-start.1 = (bf16[512,256]{1,0:T(8,128)(2,1)S(1)}, bf16[512,256]{1,0:T(8,128)(2,1)S(1)}, u32[]{:S(2)}, u32[]{:S(2)}) collective-permute-start(bf16[512,256]{1,0:T(8,128)(2,1)S(1)} %constant_dynamic-slice_fusion), channel_id=1, source_target_pairs={{0,2},{2,0},{1,3},{3,1},{4,6},{6,4},{5,7},{7,5},{8,10},{10,8},{9,1... | collective-permute-start | bytes 786440 | tf_op jit(solution)/shard_map/ppermute | solution.py:428
  5.6 16.6 %copy-start = (bf16[512,2048]{1,0:T(8,128)(2,1)S(1)}, bf16[512,2048]{1,0:T(8,128)(2,1)}, u32[]{:S(2)}) copy-start(bf16[512,2048]{1,0:T(8,128)(2,1)} %q_own_hbm.1) | copy-start | bytes 6291460
  5.6 16.6 %copy-start.2 = (s32[8,24]{1,0:T(8,128)S(1)}, s32[8,24]{1,0:T(8,128)}, u32[]{:S(2)}) copy-start(s32[8,24]{1,0:T(8,128)} %offsets_ref.3) | copy-start | bytes 2308
  5.6 16.7 %copy-start.3 = (s32[2]{0:T(128)S(1)}, s32[2]{0:T(128)}, u32[]{:S(2)}) copy-start(s32[2]{0:T(128)} %pad_add_fusion.place_ref.core_ref) | copy-start | bytes 28
  5.6 16.7 %copy-start.4 = (s32[8]{0:T(128)S(1)}, s32[8]{0:T(128)}, u32[]{:S(2)}) copy-start(s32[8]{0:T(128)} %counts_ref.3) | copy-start | bytes 100
  5.6 16.7 %copy-start.6 = (f32[4,384,128]{2,1,0:T(8,128)S(1)}, f32[4,384,128]{2,1,0:T(8,128)}, u32[]{:S(2)}) copy-start(f32[4,384,128]{2,1,0:T(8,128)} %wk_ref.1) | copy-start | bytes 2359300
  8.2 4.9 %copy-start.1 = (bf16[512,256]{1,0:T(8,128)(2,1)S(1)}, bf16[512,256]{1,0:T(8,128)(2,1)}, u32[]{:S(2)}) copy-start(bf16[512,256]{1,0:T(8,128)(2,1)} %get-tuple-element.28.after_ref.k_own_ref) | copy-start | bytes 786436
  11.3 10.9 %collective-permute-start = (bf16[528,1024]{1,0:T(8,128)(2,1)}, bf16[528,1024]{1,0:T(8,128)(2,1)S(1)}, u32[]{:S(2)}, u32[]{:S(2)}) collective-permute-start(bf16[528,1024]{1,0:T(8,128)(2,1)} %cut_queries.1), channel_id=1, source_target_pairs={{0,2},{2,0},{1,3},{3,1},{4,6},{6,4},{5,7},{7,5},{8,10},{10,8},{9,1... | collective-permute-start | bytes 3244040 | tf_op jit(solution)/shard_map/ppermute | solution.py:428
  11.5 20.5 %collective-permute-start.3 = (bf16[512,256]{1,0:T(8,128)(2,1)}, bf16[512,256]{1,0:T(8,128)(2,1)S(1)}, u32[]{:S(2)}, u32[]{:S(2)}) collective-permute-start(bf16[512,256]{1,0:T(8,128)(2,1)} %copy-done.9), channel_id=1, source_target_pairs={{0,6},{2,4},{4,10},{6,8},{8,14},{10,12},{12,18},{14,16},{16,22},{1... | collective-permute-start | bytes 786440 | tf_op jit(solution)/shard_map/ppermute | solution.py:554
  13.1 18.8 %collective-permute-start.2 = (bf16[512,256]{1,0:T(8,128)(2,1)S(1)}, bf16[512,256]{1,0:T(8,128)(2,1)S(1)}, u32[]{:S(2)}, u32[]{:S(2)}) collective-permute-start(bf16[512,256]{1,0:T(8,128)(2,1)S(1)} %copy-done.1), channel_id=1, source_target_pairs={{0,4},{2,6},{4,8},{6,10},{8,12},{10,14},{12,16},{14,18},{16,20},{1... | collective-permute-start | bytes 786440 | tf_op jit(solution)/shard_map/ppermute | solution.py:553
  16.3 15.7 %collective-permute-start.4 = (bf16[512,256]{1,0:T(8,128)(2,1)}, bf16[512,256]{1,0:T(8,128)(2,1)S(1)}, u32[]{:S(2)}, u32[]{:S(2)}) collective-permute-start(bf16[512,256]{1,0:T(8,128)(2,1)} %get-tuple-element.27), channel_id=1, source_target_pairs={{0,8},{2,10},{4,12},{6,14},{8,16},{10,18},{12,20},{14,22},{16,24},... | collective-permute-start | bytes 786440 | tf_op jit(solution)/shard_map/ppermute | solution.py:559
  22.3 1.2 %copy-start.5 = (f32[16,128,128]{2,1,0:T(8,128)S(1)}, f32[16,128,128]{2,1,0:T(8,128)}, u32[]{:S(2)}) copy-start(f32[16,128,128]{2,1,0:T(8,128)} %wq_hbm.1) | copy-start | bytes 3145732
  68.5 8.0 %collective-permute-start.5 = (f32[120,128]{1,0:T(8,128)}, f32[120,128]{1,0:T(8,128)S(1)}, u32[]{:S(2)}, u32[]{:S(2)}) collective-permute-start(f32[120,128]{1,0:T(8,128)} %sum.1.own_ref), channel_id=1, source_target_pairs={{0,64},{64,0},{128,192},{192,128},{1,65},{65,1},{129,193},{193,129... | collective-permute-start | bytes 184328 | tf_op jit(solution)/shard_map/ppermute | solution.py:571
  72.3 7.3 %collective-permute-start.6 = (f32[120,128]{1,0:T(8,128)}, f32[120,128]{1,0:T(8,128)S(1)}, u32[]{:S(2)}, u32[]{:S(2)}) collective-permute-start(f32[120,128]{1,0:T(8,128)} %sum.1.own_ref), channel_id=1, source_target_pairs={{0,128},{64,192},{128,0},{192,64},{1,129},{65,193},{129,1},{193,65... | collective-permute-start | bytes 184328 | tf_op jit(solution)/shard_map/ppermute | solution.py:571
  76.2 6.3 %collective-permute-start.7 = (f32[120,128]{1,0:T(8,128)}, f32[120,128]{1,0:T(8,128)S(1)}, u32[]{:S(2)}, u32[]{:S(2)}) collective-permute-start(f32[120,128]{1,0:T(8,128)} %sum.1.own_ref), channel_id=1, source_target_pairs={{0,192},{64,128},{128,64},{192,0},{1,193},{65,129},{129,65},{193,1... | collective-permute-start | bytes 184328 | tf_op jit(solution)/shard_map/ppermute | solution.py:571
  76.5 6.0 %copy-start.10 = (f32[120,128]{1,0:T(8,128)}, f32[120,128]{1,0:T(8,128)S(1)}, u32[]{:S(2)}) copy-start(f32[120,128]{1,0:T(8,128)S(1)} %collective-permute-done.5.one_ref) | copy-start | bytes 184324
  79.5 3.1 %copy-start.11 = (f32[120,128]{1,0:T(8,128)}, f32[120,128]{1,0:T(8,128)S(1)}, u32[]{:S(2)}) copy-start(f32[120,128]{1,0:T(8,128)S(1)} %collective-permute-done.6.two_ref) | copy-start | bytes 184324
  82.6 0.6 copy-start.12
  98.8 9.5 %copy-start.7 = (s16[16,128,128]{2,1,0:T(8,128)(2,1)}, s16[16,128,128]{2,1,0:T(8,128)(2,1)S(1)}, u32[]{:S(2)}) copy-start(s16[16,128,128]{2,1,0:T(8,128)(2,1)S(1)} %all_to_all.11.mine_ref) | copy-start | bytes 1572868
  98.8 9.5 %collective-permute-start.8 = (s16[16,128,128]{2,1,0:T(8,128)(2,1)S(1)}, s16[16,128,128]{2,1,0:T(8,128)(2,1)S(1)}, u32[]{:S(2)}, u32[]{:S(2)}) collective-permute-start(s16[16,128,128]{2,1,0:T(8,128)(2,1)S(1)} %all_to_all.11.mine_ref), channel_id=1, source_target_pairs={{0,2},{2,0},{1,3},{3,1},{4,6},{6,4},{5,7},{7,5},{8,10},{10,8},{9,1... | collective-permute-start | bytes 1572872 | tf_op jit(solution)/shard_map/ppermute | solution.py:428
  103.2 2.4 %collective-permute-start.9 = (f32[1,128]{1,0:T(1,128)S(1)}, f32[1,128]{1,0:T(1,128)S(1)}, u32[]{:S(2)}, u32[]{:S(2)}) collective-permute-start(f32[1,128]{1,0:T(1,128)S(1)} %slice.6), channel_id=1, source_target_pairs={{0,1},{1,0},{2,3},{3,2},{4,5},{5,4},{6,7},{7,6},{8,9},{9,8},{10,11... | collective-permute-start | bytes 1544 | tf_op jit(solution)/shard_map/ppermute | solution.py:428
  106.3 2.0 %collective-permute-start.10 = (f32[1,128]{1,0:T(1,128)S(1)}, f32[1,128]{1,0:T(1,128)S(1)}, u32[]{:S(2)}, u32[]{:S(2)}) collective-permute-start(f32[1,128]{1,0:T(1,128)S(1)} %slice_add_fusion), channel_id=1, source_target_pairs={{0,2},{2,0},{1,3},{3,1},{4,6},{6,4},{5,7},{7,5},{8,10},{10,8},{9,1... | collective-permute-start | bytes 1544 | tf_op jit(solution)/shard_map/ppermute | solution.py:428
  108.3 0.8 copy-start.8

commit v7 on v6

--- a/solution.py
+++ b/solution.py
@@ -36,8 +36,8 @@
 VMEM_BYTES = 40 * 1024 * 1024
 NEAR_UNROLL = 4
 FAR_UNROLL = 6
-NOTE_ROWS = 16
 TILE = 16
+STEP_SHARES = 4
 LEVELS = 32760.0
 WORK_SIZE = CHIP_BLOCKS * CAND // 4 + 16
 LOW = -1e30
@@ -66,6 +66,17 @@
         )
         for g in range(KV_HERE)
     ]
+
+
+def slot_table(offsets_ref, counts_ref):
+    table = jnp.concatenate(
+        [offsets_ref[...], jnp.zeros((ROWS, HEAD_DIM - CAND), jnp.int32)], axis=1
+    )
+    row = lax.broadcasted_iota(jnp.int32, (ROWS, HEAD_DIM), 0)
+    lane = lax.broadcasted_iota(jnp.int32, (ROWS, HEAD_DIM), 1)
+    for j in range(ROWS):
+        table = jnp.where((lane == CAND) & (row == j), counts_ref[j], table)
+    return table.astype(jnp.float32)
 
 
 def make_lists(core, chip, table):
@@ -150,7 +161,7 @@
 
 
 def near_kernel(
-    place_ref, offsets_ref, counts_ref,
+    place_ref, offsets_own_ref, counts_own_ref, offsets_other_ref, counts_other_ref,
     q_own_hbm, q_other_ref, k_own_ref, k_other_ref, wq_hbm, wk_hbm,
     queries, slot_max, slot_sum, pooled_query, gate_query, pooled_key, gate_key,
     far_list,
@@ -171,16 +182,15 @@
     q_copy.start()
     wq_copy.start()
     wk_copy.start()
-    table = jnp.concatenate(
-        [offsets_ref[...], jnp.zeros((ROWS, HEAD_DIM - CAND), jnp.int32)], axis=1
-    )
-    row = lax.broadcasted_iota(jnp.int32, (ROWS, HEAD_DIM), 0)
-    lane = lax.broadcasted_iota(jnp.int32, (ROWS, HEAD_DIM), 1)
-    for j in range(ROWS):
-        table = jnp.where((lane == CAND) & (row == j), counts_ref[j], table)
-    note = q_other_ref[half:, 0:HEAD_DIM].astype(jnp.float32)
     lists = make_lists(
-        core, place_ref[1], jnp.concatenate([table.astype(jnp.float32), note[0:ROWS]], axis=0)
+        core, place_ref[1],
+        jnp.concatenate(
+            [
+                slot_table(offsets_own_ref, counts_own_ref),
+                slot_table(offsets_other_ref, counts_other_ref),
+            ],
+            axis=0,
+        ),
     )
     far_list[...] = lists[CHIP_BLOCKS:]
     near_vector[...] = lists[0:CHIP_BLOCKS]
@@ -371,7 +381,7 @@
 def unpack_kernel(place_ref, mine_ref, other_ref, query_ref, key_ref):
     core = place_ref[0]
     for source, ref in ((core, mine_ref), (1 - core, other_ref)):
-        for share in range(SHARES):
+        for share in range(STEP_SHARES):
             powers = ref[share, SUM_ROWS:SUM_ROWS + TILE, :].astype(jnp.int32).astype(jnp.float32)
             scale = jnp.exp2(powers[0:8, :]) * (1.0 / LEVELS)
             for tile in range(SUM_ROWS // TILE):
@@ -395,35 +405,24 @@
 
 
 def unpack(place, mine, other):
-    rows = SHARES * HALF_HEAD, SHARES * KEY_ROWS
+    rows = HALF_HEAD, KEY_ROWS
     return pl.pallas_call(
         unpack_kernel,
         grid_spec=pltpu.PrefetchScalarGridSpec(
             num_scalar_prefetch=1,
-            grid=(1,),
-            in_specs=[whole(*mine.shape)] * 2,
-            out_specs=[whole(2, n, HEAD_DIM) for n in rows],
+            grid=(SHARES // STEP_SHARES,),
+            in_specs=[
+                pl.BlockSpec((STEP_SHARES, SUM_ROWS + TILE, HEAD_DIM), lambda i, c: (i, 0, 0))
+            ] * 2,
+            out_specs=[
+                pl.BlockSpec((2, STEP_SHARES * n, HEAD_DIM), lambda i, c: (0, i, 0)) for n in rows
+            ],
         ),
-        out_shape=[shaped((2, n, HEAD_DIM)) for n in rows],
+        out_shape=[shaped((2, SHARES * n, HEAD_DIM)) for n in rows],
         name="unpack",
     )(place, mine, other)
 
 
-def cut_queries_kernel(place_ref, counts_ref, offsets_ref, give_in, after_ref, give_ref):
-    half = ROWS * BLOCK
-    give_ref[0:half, :] = give_in[...]
-    row = lax.broadcasted_iota(jnp.int32, (ROWS, HEAD_DIM), 0)
-    lane = lax.broadcasted_iota(jnp.int32, (ROWS, HEAD_DIM), 1)
-    note = jnp.concatenate(
-        [offsets_ref[...], jnp.zeros((ROWS, HEAD_DIM - CAND), jnp.int32)], axis=1
-    )
-    for j in range(ROWS):
-        note = jnp.where((lane == CAND) & (row == j), counts_ref[j], note)
-    note = note.astype(jnp.float32).astype(jnp.bfloat16)
-    give_ref[half:, :] = jnp.zeros((NOTE_ROWS, Q_COLS), jnp.bfloat16)
-    give_ref[half:, 0:HEAD_DIM] = jnp.concatenate([note, jnp.zeros_like(note)], axis=0)
-
-
 def swap(x, axis):
     return lax.ppermute(x, axis, [(0, 1), (1, 0)])
 
@@ -440,27 +439,26 @@
     return pl.BlockSpec(memory_space=pltpu.SMEM)
 
 
-def cut_queries(place, queries, offsets, counts, after):
+def cut_prev_kernel(place_ref, give_in, after_ref, give_ref):
+    give_ref[...] = give_in[...]
+
+
+def cut_prev(place, keys, after):
     half = ROWS * BLOCK
     return pl.pallas_call(
-        cut_queries_kernel,
+        cut_prev_kernel,
         grid_spec=pltpu.PrefetchScalarGridSpec(
             num_scalar_prefetch=1,
             grid=(1,),
             in_specs=[
-                smem(),
-                whole(ROWS, CAND),
-                pl.BlockSpec((half, Q_COLS), lambda i, c: (0, 1 - c[0])),
+                pl.BlockSpec((half, K_COLS), lambda i, c: (0, 1 - c[0])),
                 pl.BlockSpec(memory_space=pl.ANY),
             ],
-            out_specs=whole(half + NOTE_ROWS, Q_COLS),
+            out_specs=whole(half, K_COLS),
         ),
-        out_shape=shaped((half + NOTE_ROWS, Q_COLS), jnp.bfloat16),
-        cost_estimate=pl.CostEstimate(
-            flops=0, bytes_accessed=30_000_000, transcendentals=0
-        ),
-        name="cut_queries",
-    )(place, counts, offsets, queries, after)
+        out_shape=shaped((half, K_COLS), jnp.bfloat16),
+        name="cut_prev",
+    )(place, keys, after)
 
 
 def near_call(place, tables, q_own, q_other, k_mine, k_other, wq, wk):
@@ -480,11 +478,11 @@
         grid_spec=pltpu.PrefetchScalarGridSpec(
             num_scalar_prefetch=1,
             grid=(1,),
-            in_specs=[whole(ROWS, CAND), smem()] + [
+            in_specs=[whole(ROWS, CAND), smem()] * 2 + [
                 pl.BlockSpec(memory_space=pltpu.HBM),
-                whole(half + NOTE_ROWS, Q_COLS),
-                whole(half, K_COLS),
-                whole(half, K_COLS),
+                pl.BlockSpec((half, Q_COLS), lambda i, c: (0, c[0])),
+                pl.BlockSpec((half, K_COLS), lambda i, c: (0, c[0])),
+                pl.BlockSpec((half, K_COLS), lambda i, c: (0, c[0])),
                 pl.BlockSpec(memory_space=pltpu.HBM),
                 pl.BlockSpec(memory_space=pltpu.HBM),
             ],
@@ -510,13 +508,15 @@
 
 
 def far_call(place, k_prev_own, k_prev_other, k_far, near, wk):
+    half = ROWS * BLOCK
     args = (k_prev_own, k_prev_other, k_far, *near[:-1])
     return pl.pallas_call(
         far_kernel,
         grid_spec=pltpu.PrefetchScalarGridSpec(
             num_scalar_prefetch=1,
             grid=(1,),
-            in_specs=[smem()] + [whole(*a.shape) for a in args] + [
+            in_specs=[smem(), pl.BlockSpec((half, K_COLS), lambda i, c: (0, c[0]))]
+            + [whole(*a.shape) for a in args[1:]] + [
                 pl.BlockSpec((KV_HERE, POOL, HEAD_DIM), lambda i, c: (c[0], 0, 0)),
             ],
             out_specs=whole(SHARES, PART_ROWS, HEAD_DIM),
@@ -548,21 +548,21 @@
     core = lax.axis_index("core")
     place = jnp.stack([core, lax.axis_index(chips)]).astype(jnp.int32)
 
-    k_mine = lax.dynamic_slice_in_dim(teacher_keys, core * K_COLS, K_COLS, 1)
-    k_give = lax.dynamic_slice_in_dim(teacher_keys, (1 - core) * K_COLS, K_COLS, 1)
-    k_prev_own = lax.ppermute(k_mine, places, [(i, i + 2) for i in range(count - 2)])
-    k_prev_other = lax.ppermute(
-        k_give, places, [(i, (i ^ 1) + 2) for i in range(count - 2)]
-    )
-    k_other = swap(k_give, "core")
-    q_other = swap(cut_queries(place, teacher_queries, block_offsets, valid_counts, k_mine), "core")
+    columns = lambda x, which: lax.dynamic_slice_in_dim(x, which * K_COLS, K_COLS, 1)
+    k_prev = lax.ppermute(teacher_keys, places, [(i, i + 2) for i in range(count - 2)])
+    k_other = swap(teacher_keys, "core")
+    q_other = swap(teacher_queries, "core")
+    tables = (block_offsets, valid_counts, swap(block_offsets, "core"), swap(valid_counts, "core"))
     k_far = lax.ppermute(
-        jnp.where(core == 1, k_mine, k_other), places, [(i, i + 4) for i in range(count - 4)]
+        jnp.where(core == 1, columns(teacher_keys, core), columns(k_other, core)),
+        places, [(i, i + 4) for i in range(count - 4)],
     )
     near = near_call(
-        place, (block_offsets, valid_counts), teacher_queries, q_other, k_mine, k_other, query_projection, key_projection
-    )
-    parts = far_call(place, k_prev_own, k_prev_other, k_far, near, key_projection)
+        place, tables, teacher_queries, q_other, teacher_keys, k_other,
+        query_projection, key_projection,
+    )
+    k_prev_other = swap(cut_prev(place, k_prev, near[-1]), "core")
+    parts = far_call(place, k_prev, k_prev_other, k_far, near, key_projection)
 
     group = ("zb", "yh", "x")
     got = lax.all_to_all(parts, group, 0, 0)
@@ -571,7 +571,6 @@
         lax.ppermute(got, "za", [(i, i ^ step) for i in range(4)]) for step in (1, 2, 3)
     )
     coded, total = pack(got, one, two, three)
-    total = total[:1]
     total = total + swap(total, "head")
     total = total + swap(total, "core")
     mine = lax.all_to_all(coded, group, 0, 0)

time: 115 us -> 129 us (1.12)
  local copies, waits for them, and re-layouts: 4.33 us -> 23.3 us
  starting transfers between devices: 28.4 us -> 22.4 us
  waiting for transfers between devices: 8.45 us -> 11.2 us
  blocking collectives: 43.4 us -> 41.3 us
    unnamed x26 -> x56, local copies, waits for them, and re-layouts: 2.68 us -> 22.8 us
    ppermute x3 -> x2, starting transfers between devices: 10.7 us -> 4.32 us  [the longest x1 2.92 us: body(): lax.ppermute(jnp.where(core == 1, columns(teacher_keys, core), columns(k_...]
    ppermute x5 -> x8, waiting for transfers between devices: 2.4 us -> 5.85 us  [swap(): return lax.ppermute(x, axis, [(0, 1), (1, 0)])]
    all_to_all x1, blocking collectives: 29.7 us -> 26.6 us  [body(): got = lax.all_to_all(parts, group, 0, 0)]
    ppermute x5 -> x8, starting transfers between devices: 9.68 us -> 10.8 us  [swap(): return lax.ppermute(x, axis, [(0, 1), (1, 0)])]
  transfers between devices with their start and end apart: 11 -> 13, of which waited for: 5 -> 6; matrix products, arithmetic and copies ran while one was open for 2% -> 2% of each run, Pallas kernels for 7% -> 8%
where the time goes in v7:
time: 129 us; the launch traced here: 127 us
  blocking collectives  41.3 us (32%)
  Pallas kernels  23.7 us (18%)
  local copies, waits for them, and re-layouts  23.3 us (18%)
  starting transfers between devices  22.4 us (17%)
  waiting for transfers between devices  11.2 us (9%)
  between operations  2.56 us (2%)
  other arithmetic  2.49 us (2%)
    all_to_all x1, blocking collectives, body(): got = lax.all_to_all(parts, group, 0, 0)  26.6 us
    unnamed x56, local copies, waits for them, and re-layouts  22.8 us
    all_to_all x1, blocking collectives, body(): mine = lax.all_to_all(coded, group, 0, 0)  14.7 us
    ppermute x8, starting transfers between devices, swap(): return lax.ppermute(x, axis, [(0, 1), (1, 0)])  10.8 us
    pallas_call x1, Pallas kernels, near_call(): pl.pallas_call(near_kernel, grid_spec=pltpu.PrefetchScalarGridSpec(num_sc...  8.47 us
    ppermute x3, starting transfers between devices, body(): lax.ppermute(got, 'za', [(i, i ^ step) for i in range(4)])  7.29 us
    ppermute x8, waiting for transfers between devices, swap(): return lax.ppermute(x, axis, [(0, 1), (1, 0)])  5.85 us
    ppermute x3, waiting for transfers between devices, body(): lax.ppermute(got, 'za', [(i, i ^ step) for i in range(4)])  5.37 us
  transfers between devices with their start and end apart: 13, of which 6 were waited for; matrix products, arithmetic and copies ran while one was open for 2% of the time, Pallas kernels for 8%

profile of v7, /device:TPU:1, one launch (start us, length us, event | category | flops | bytes accessed | tf_op | source)
XLA Modules:
  0.0 127.0 jit_solution(11271658557515569282)
XLA Ops:
  0.6 3.3 %collective-permute-start.2 = (bf16[512,2048]{1,0:T(8,128)(2,1)}, bf16[512,2048]{1,0:T(8,128)(2,1)S(1)}, u32[]{:S(2)}, u32[]{:S(2)}) collective-permute-start(bf16[512,2048]{1,0:T(8,128)(2,1)} %q_own_hbm.1), channel_id=1, source_target_pairs={{0,2},{2,0},{1,3},{3,1},{4,6},{6,4},{5,7},{7,5},{8,10},{10,8},{9,1... | collective-permute-start | bytes 6291464 | tf_op jit(solution)/shard_map/ppermute | solution.py:427
  4.1 1.4 %collective-permute-start.4 = (bf16[512,512]{1,0:T(8,128)(2,1)}, bf16[512,512]{1,0:T(8,128)(2,1)S(1)}, u32[]{:S(2)}, u32[]{:S(2)}) collective-permute-start(bf16[512,512]{1,0:T(8,128)(2,1)} %k_own_ref.1), channel_id=1, source_target_pairs={{0,4},{2,6},{4,8},{6,10},{8,12},{10,14},{12,16},{14,18},{16,20},{1... | collective-permute-start | bytes 1572872 | tf_op jit(solution)/shard_map/ppermute | solution.py:552
  6.4 2.3 %collective-permute-done.3.k_other_ref = bf16[512,512]{1,0:T(8,128)(2,1)S(1)} collective-permute-done((bf16[512,512]{1,0:T(8,128)(2,1)}, bf16[512,512]{1,0:T(8,128)(2,1)S(1)}, u32[]{:S(2)}, u32[]{:S(2)}) %collective-permute-start.3) | collective-permute-done | bytes 524320 | tf_op jit(solution)/shard_map/ppermute | solution.py:427
  8.7 1.7 %dynamic-slice_select_fusion = bf16[512,256]{1,0:T(8,128)(2,1)} fusion(bf16[512,512]{1,0:T(8,128)(2,1)S(1)} %collective-permute-done.3.k_other_ref, s32[]{:T(128)S(6)} %select_n.13, bf16[512,512]{1,0:T(8,128)(2,1)} %k_own_ref.1, pred[]{:T(512)S(6)} %eq.3), kind=kLoop, calls=%fused_computation | loop fusion | flops 131072 | bytes 786437 | tf_op jit(solution)/shard_map/jit(_where)/select_n | solution.py:557
  10.4 2.9 %collective-permute-start.6 = (bf16[512,256]{1,0:T(8,128)(2,1)}, bf16[512,256]{1,0:T(8,128)(2,1)S(1)}, u32[]{:S(2)}, u32[]{:S(2)}) collective-permute-start(bf16[512,256]{1,0:T(8,128)(2,1)} %dynamic-slice_select_fusion), channel_id=1, source_target_pairs={{0,8},{2,10},{4,12},{6,14},{8,16},{10,18},{12,20},{14,22},{16,24},... | collective-permute-start | bytes 786440 | tf_op jit(solution)/shard_map/ppermute | solution.py:556
  14.4 1.6 %copy-done.7 = bf16[512,2048]{1,0:T(8,128)(2,1)S(1)} copy-done((bf16[512,2048]{1,0:T(8,128)(2,1)S(1)}, bf16[512,2048]{1,0:T(8,128)(2,1)}, u32[]{:S(2)}) %copy-start.7) | copy-done | bytes 2097176
  16.0 1.2 copy-done.8
  19.7 8.5 %near.1 = (bf16[32,256,128]{2,1,0:T(8,128)(2,1)S(1)}, f32[32,32,256]{2,1,0:T(8,128)S(1)}, f32[32,32,256]{2,1,0:T(8,128)S(1)}, f32[2,64,128]{2,1,0:T(8,128)S(1)},...) custom-call(s32[2]{0:T(128)S(1)} %pad_add_fusion.place_ref.core_ref, ...), custom_call_target="tpu_custom_call" | custom-call | flops 2000000000 | bytes 8000000 | tf_op jit(solution)/shard_map/near/pallas_call | solution.py:476
  28.8 1.4 %copy-done.13 = bf16[32,256,128]{2,1,0:T(8,128)(2,1)} copy-done((bf16[32,256,128]{2,1,0:T(8,128)(2,1)}, bf16[32,256,128]{2,1,0:T(8,128)(2,1)S(1)}, u32[]{:S(2)}) %copy-start.13) | copy-done | bytes 2097176
  34.1 2.3 %cut_prev.1 = bf16[512,256]{1,0:T(8,128)(2,1)} custom-call(s32[2]{0:T(128)} %copy-done.5, bf16[512,512]{1,0:T(8,128)(2,1)} %copy-done, s32[16,128]{1,0:T(8,128)} %copy-done.3), custom_call_target="tpu_custom_call" | custom-call | tf_op jit(solution)/shard_map/cut_prev/pallas_call | solution.py:448
  37.1 1.4 %collective-permute-done.5.k_prev_other_ref = bf16[512,256]{1,0:T(8,128)(2,1)S(1)} collective-permute-done((bf16[512,256]{1,0:T(8,128)(2,1)}, bf16[512,256]{1,0:T(8,128)(2,1)S(1)}, u32[]{:S(2)}, u32[]{:S(2)}) %collective-permute-start.5) | collective-permute-done | bytes 262176 | tf_op jit(solution)/shard_map/ppermute | solution.py:427
  42.0 1.6 %copy-done.14 = bf16[32,256,128]{2,1,0:T(8,128)(2,1)S(1)} copy-done((bf16[32,256,128]{2,1,0:T(8,128)(2,1)S(1)}, bf16[32,256,128]{2,1,0:T(8,128)(2,1)}, u32[]{:S(2)}) %copy-start.14) | copy-done | bytes 2097176
  47.6 4.8 %far.1 = f32[16,80,128]{2,1,0:T(8,128)S(1)} custom-call(s32[2]{0:T(128)S(1)} %copy-done.6, s32[16,128]{1,0:T(8,128)S(1)} %copy-done.4, bf16[512,512]{1,0:T(8,128)(2,1)S(1)} %copy-done.1, bf16[512,256]{1,0:T(8,128)(2,1)S(1)} %collective-permute-done.5.k_prev_other_ref, bf16[512,256]{1,0:T(8,128)(2,1)S(1)} %collective-permute-done.6.k_far_ref, ...), custom_call_target="tpu_custom_call" | custom-call | flops 2000000000 | bytes 8000000 | tf_op jit(solution)/shard_map/far/pallas_call | solution.py:513
  52.4 26.6 %all_to_all.10.parts_ref = f32[16,80,128]{2,1,0:T(8,128)} all-to-all(f32[16,80,128]{2,1,0:T(8,128)S(1)} %far.1), channel_id=1, replica_groups=mesh['za'=4,'zb'=2,'yh'=2,'x'=4,'core'=2,'head'=2] {'zb','yh','x'}, dimensions={0} | all-to-all | bytes 1310720 | tf_op jit(solution)/shard_map/all_to_all | solution.py:568
  79.1 2.0 %sum.1.own_ref = f32[120,128]{1,0:T(8,128)} custom-call(f32[16,80,128]{2,1,0:T(8,128)} %all_to_all.10.parts_ref), custom_call_target="tpu_custom_call" | custom-call | tf_op jit(solution)/shard_map/sum/pallas_call | solution.py:569
  81.1 4.0 %collective-permute-start.7 = (f32[120,128]{1,0:T(8,128)}, f32[120,128]{1,0:T(8,128)S(1)}, u32[]{:S(2)}, u32[]{:S(2)}) collective-permute-start(f32[120,128]{1,0:T(8,128)} %sum.1.own_ref), channel_id=1, source_target_pairs={{0,64},{64,0},{128,192},{192,128},{1,65},{65,1},{129,193},{193,129... | collective-permute-start | bytes 184328 | tf_op jit(solution)/shard_map/ppermute | solution.py:571
  85.1 2.9 %collective-permute-start.8 = (f32[120,128]{1,0:T(8,128)}, f32[120,128]{1,0:T(8,128)S(1)}, u32[]{:S(2)}, u32[]{:S(2)}) collective-permute-start(f32[120,128]{1,0:T(8,128)} %sum.1.own_ref), channel_id=1, source_target_pairs={{0,128},{64,192},{128,0},{192,64},{1,129},{65,193},{129,1},{193,65... | collective-permute-start | bytes 184328 | tf_op jit(solution)/shard_map/ppermute | solution.py:571
  88.4 4.3 %collective-permute-done.8.two_ref = f32[120,128]{1,0:T(8,128)S(1)} collective-permute-done((f32[120,128]{1,0:T(8,128)}, f32[120,128]{1,0:T(8,128)S(1)}, u32[]{:S(2)}, u32[]{:S(2)}) %collective-permute-start.8) | collective-permute-done | bytes 61472 | tf_op jit(solution)/shard_map/ppermute | solution.py:571
  94.4 1.8 %pack.1 = (s16[16,128,128]{2,1,0:T(8,128)(2,1)}, f32[8,128]{1,0:T(8,128)}) custom-call(f32[120,128]{1,0:T(8,128)} %sum.1.own_ref, f32[120,128]{1,0:T(8,128)} %copy-done.25, f32[120,128]{1,0:T(8,128)} %copy-done.26, f32[120,128]{1,0:T(8,128)} %copy-done.27), custom_call_target="tpu_custom_call" | custom-call | tf_op jit(solution)/shard_map/pack/pallas_call | solution.py:398
  96.2 14.7 %all_to_all.11.mine_ref = s16[16,128,128]{2,1,0:T(8,128)(2,1)S(1)} all-to-all(s16[16,128,128]{2,1,0:T(8,128)(2,1)} %get-tuple-element.23), channel_id=1, replica_groups=mesh['za'=4,'zb'=2,'yh'=2,'x'=4,'core'=2,'head'=2] {'zb','yh','x'}, dimensions={0} | all-to-all | bytes 1048576 | tf_op jit(solution)/shard_map/all_to_all | solution.py:576
  110.9 3.4 %collective-permute-start.10 = (s16[16,128,128]{2,1,0:T(8,128)(2,1)S(1)}, s16[16,128,128]{2,1,0:T(8,128)(2,1)S(1)}, u32[]{:S(2)}, u32[]{:S(2)}) collective-permute-start(s16[16,128,128]{2,1,0:T(8,128)(2,1)S(1)} %all_to_all.11.mine_ref), channel_id=1, source_target_pairs={{0,2},{2,0},{1,3},{3,1},{4,6},{6,4},{5,7},{7,5},{8,10},{10,8},{9,1... | collective-permute-start | bytes 1572872 | tf_op jit(solution)/shard_map/ppermute | solution.py:427
  114.3 1.3 %collective-permute-start.11 = (f32[8,128]{1,0:T(8,128)}, f32[8,128]{1,0:T(8,128)S(1)}, u32[]{:S(2)}, u32[]{:S(2)}) collective-permute-start(f32[8,128]{1,0:T(8,128)} %get-tuple-element.26), channel_id=1, source_target_pairs={{0,1},{1,0},{2,3},{3,2},{4,5},{5,4},{6,7},{7,6},{8,9},{9,8},{10,11... | collective-permute-start | bytes 12296 | tf_op jit(solution)/shard_map/ppermute | solution.py:427
  115.6 1.4 %collective-permute-done.11 = f32[8,128]{1,0:T(8,128)S(1)} collective-permute-done((f32[8,128]{1,0:T(8,128)}, f32[8,128]{1,0:T(8,128)S(1)}, u32[]{:S(2)}, u32[]{:S(2)}) %collective-permute-start.11) | collective-permute-done | bytes 4128 | tf_op jit(solution)/shard_map/ppermute | solution.py:427
  121.6 4.3 %unpack.1 = (f32[2,1024,128]{2,1,0:T(8,128)}, f32[2,768,128]{2,1,0:T(8,128)}) custom-call(s32[2]{0:T(128)} %copy-done.5, s16[16,128,128]{2,1,0:T(8,128)(2,1)} %copy-done.23, s16[16,128,128]{2,1,0:T(8,128)(2,1)} %copy-done.24), custom_call_target="tpu_custom_call" | custom-call | tf_op jit(solution)/shard_map/unpack/pallas_call | solution.py:409
  (71 shorter events, 23.4 us)
Async XLA Ops:
  0.6 12.7 %collective-permute-start.2 = (bf16[512,2048]{1,0:T(8,128)(2,1)}, bf16[512,2048]{1,0:T(8,128)(2,1)S(1)}, u32[]{:S(2)}, u32[]{:S(2)}) collective-permute-start(bf16[512,2048]{1,0:T(8,128)(2,1)} %q_own_hbm.1), channel_id=1, source_target_pairs={{0,2},{2,0},{1,3},{3,1},{4,6},{6,4},{5,7},{7,5},{8,10},{10,8},{9,1... | collective-permute-start | bytes 6291464 | tf_op jit(solution)/shard_map/ppermute | solution.py:427
  4.0 4.7 %collective-permute-start.3 = (bf16[512,512]{1,0:T(8,128)(2,1)}, bf16[512,512]{1,0:T(8,128)(2,1)S(1)}, u32[]{:S(2)}, u32[]{:S(2)}) collective-permute-start(bf16[512,512]{1,0:T(8,128)(2,1)} %k_own_ref.1), channel_id=1, source_target_pairs={{0,2},{2,0},{1,3},{3,1},{4,6},{6,4},{5,7},{7,5},{8,10},{10,8},{9,1... | collective-permute-start | bytes 1572872 | tf_op jit(solution)/shard_map/ppermute | solution.py:427
  4.1 29.3 %collective-permute-start.4 = (bf16[512,512]{1,0:T(8,128)(2,1)}, bf16[512,512]{1,0:T(8,128)(2,1)S(1)}, u32[]{:S(2)}, u32[]{:S(2)}) collective-permute-start(bf16[512,512]{1,0:T(8,128)(2,1)} %k_own_ref.1), channel_id=1, source_target_pairs={{0,4},{2,6},{4,8},{6,10},{8,12},{10,14},{12,16},{14,18},{16,20},{1... | collective-permute-start | bytes 1572872 | tf_op jit(solution)/shard_map/ppermute | solution.py:552
  5.5 7.9 %collective-permute-start = (s32[8,24]{1,0:T(8,128)}, s32[8,24]{1,0:T(8,128)S(1)}, u32[]{:S(2)}, u32[]{:S(2)}) collective-permute-start(s32[8,24]{1,0:T(8,128)} %offsets_own_ref.1), channel_id=1, source_target_pairs={{0,2},{2,0},{1,3},{3,1},{4,6},{6,4},{5,7},{7,5},{8,10},{10,8},{9,1... | collective-permute-start | bytes 2312 | tf_op jit(solution)/shard_map/ppermute | solution.py:427
  6.2 7.1 %collective-permute-start.1 = (s32[8]{0:T(128)}, s32[8]{0:T(128)S(1)}, u32[]{:S(2)}, u32[]{:S(2)}) collective-permute-start(s32[8]{0:T(128)} %counts_own_ref.1), channel_id=1, source_target_pairs={{0,2},{2,0},{1,3},{3,1},{4,6},{6,4},{5,7},{7,5},{8,10},{10,8},{9,1... | collective-permute-start | bytes 104 | tf_op jit(solution)/shard_map/ppermute | solution.py:427
  6.4 21.8 %copy-start.5 = (s32[2]{0:T(128)}, s32[2]{0:T(128)S(1)}, u32[]{:S(2)}) copy-start(s32[2]{0:T(128)S(1)} %pad_add_fusion.place_ref.core_ref) | copy-start | bytes 28
  10.4 26.7 %collective-permute-start.6 = (bf16[512,256]{1,0:T(8,128)(2,1)}, bf16[512,256]{1,0:T(8,128)(2,1)S(1)}, u32[]{:S(2)}, u32[]{:S(2)}) collective-permute-start(bf16[512,256]{1,0:T(8,128)(2,1)} %dynamic-slice_select_fusion), channel_id=1, source_target_pairs={{0,8},{2,10},{4,12},{6,14},{8,16},{10,18},{12,20},{14,22},{16,24},... | collective-permute-start | bytes 786440 | tf_op jit(solution)/shard_map/ppermute | solution.py:556
  14.4 1.6 %copy-start.7 = (bf16[512,2048]{1,0:T(8,128)(2,1)S(1)}, bf16[512,2048]{1,0:T(8,128)(2,1)}, u32[]{:S(2)}) copy-start(bf16[512,2048]{1,0:T(8,128)(2,1)} %q_own_hbm.1) | copy-start | bytes 6291460
  16.0 1.2 copy-start.8
  17.2 1.1 copy-start.9
  28.8 1.4 %copy-start.13 = (bf16[32,256,128]{2,1,0:T(8,128)(2,1)}, bf16[32,256,128]{2,1,0:T(8,128)(2,1)S(1)}, u32[]{:S(2)}) copy-start(bf16[32,256,128]{2,1,0:T(8,128)(2,1)S(1)} %get-tuple-element.16.queries) | copy-start | bytes 6291460
  36.5 2.0 %collective-permute-start.5 = (bf16[512,256]{1,0:T(8,128)(2,1)}, bf16[512,256]{1,0:T(8,128)(2,1)S(1)}, u32[]{:S(2)}, u32[]{:S(2)}) collective-permute-start(bf16[512,256]{1,0:T(8,128)(2,1)} %cut_prev.1), channel_id=1, source_target_pairs={{0,2},{2,0},{1,3},{3,1},{4,6},{6,4},{5,7},{7,5},{8,10},{10,8},{9,1... | collective-permute-start | bytes 786440 | tf_op jit(solution)/shard_map/ppermute | solution.py:427
  40.9 1.1 copy-start.10
  42.0 1.6 %copy-start.14 = (bf16[32,256,128]{2,1,0:T(8,128)(2,1)S(1)}, bf16[32,256,128]{2,1,0:T(8,128)(2,1)}, u32[]{:S(2)}) copy-start(bf16[32,256,128]{2,1,0:T(8,128)(2,1)} %copy-done.13) | copy-start | bytes 6291460
  43.6 1.2 copy-start.16
  44.9 1.2 copy-start.18
  81.1 7.3 %collective-permute-start.7 = (f32[120,128]{1,0:T(8,128)}, f32[120,128]{1,0:T(8,128)S(1)}, u32[]{:S(2)}, u32[]{:S(2)}) collective-permute-start(f32[120,128]{1,0:T(8,128)} %sum.1.own_ref), channel_id=1, source_target_pairs={{0,64},{64,0},{128,192},{192,128},{1,65},{65,1},{129,193},{193,129... | collective-permute-start | bytes 184328 | tf_op jit(solution)/shard_map/ppermute | solution.py:571
  85.1 7.6 %collective-permute-start.8 = (f32[120,128]{1,0:T(8,128)}, f32[120,128]{1,0:T(8,128)S(1)}, u32[]{:S(2)}, u32[]{:S(2)}) collective-permute-start(f32[120,128]{1,0:T(8,128)} %sum.1.own_ref), channel_id=1, source_target_pairs={{0,128},{64,192},{128,0},{192,64},{1,129},{65,193},{129,1},{193,65... | collective-permute-start | bytes 184328 | tf_op jit(solution)/shard_map/ppermute | solution.py:571
  88.0 5.7 %collective-permute-start.9 = (f32[120,128]{1,0:T(8,128)}, f32[120,128]{1,0:T(8,128)S(1)}, u32[]{:S(2)}, u32[]{:S(2)}) collective-permute-start(f32[120,128]{1,0:T(8,128)} %sum.1.own_ref), channel_id=1, source_target_pairs={{0,192},{64,128},{128,64},{192,0},{1,193},{65,129},{129,65},{193,1... | collective-permute-start | bytes 184328 | tf_op jit(solution)/shard_map/ppermute | solution.py:571
  88.4 5.4 %copy-start.25 = (f32[120,128]{1,0:T(8,128)}, f32[120,128]{1,0:T(8,128)S(1)}, u32[]{:S(2)}) copy-start(f32[120,128]{1,0:T(8,128)S(1)} %collective-permute-done.7.one_ref) | copy-start | bytes 184324
  110.9 9.9 %copy-start.23 = (s16[16,128,128]{2,1,0:T(8,128)(2,1)}, s16[16,128,128]{2,1,0:T(8,128)(2,1)S(1)}, u32[]{:S(2)}) copy-start(s16[16,128,128]{2,1,0:T(8,128)(2,1)S(1)} %all_to_all.11.mine_ref) | copy-start | bytes 1572868
  110.9 9.9 %collective-permute-start.10 = (s16[16,128,128]{2,1,0:T(8,128)(2,1)S(1)}, s16[16,128,128]{2,1,0:T(8,128)(2,1)S(1)}, u32[]{:S(2)}, u32[]{:S(2)}) collective-permute-start(s16[16,128,128]{2,1,0:T(8,128)(2,1)S(1)} %all_to_all.11.mine_ref), channel_id=1, source_target_pairs={{0,2},{2,0},{1,3},{3,1},{4,6},{6,4},{5,7},{7,5},{8,10},{10,8},{9,1... | collective-permute-start | bytes 1572872 | tf_op jit(solution)/shard_map/ppermute | solution.py:427
  114.3 2.7 %collective-permute-start.11 = (f32[8,128]{1,0:T(8,128)}, f32[8,128]{1,0:T(8,128)S(1)}, u32[]{:S(2)}, u32[]{:S(2)}) collective-permute-start(f32[8,128]{1,0:T(8,128)} %get-tuple-element.26), channel_id=1, source_target_pairs={{0,1},{1,0},{2,3},{3,2},{4,5},{5,4},{6,7},{7,6},{8,9},{9,8},{10,11... | collective-permute-start | bytes 12296 | tf_op jit(solution)/shard_map/ppermute | solution.py:427
  117.6 2.0 %collective-permute-start.12 = (f32[8,128]{1,0:T(8,128)S(1)}, f32[8,128]{1,0:T(8,128)S(1)}, u32[]{:S(2)}, u32[]{:S(2)}) collective-permute-start(f32[8,128]{1,0:T(8,128)S(1)} %add.23), channel_id=1, source_target_pairs={{0,2},{2,0},{1,3},{3,1},{4,6},{6,4},{5,7},{7,5},{8,10},{10,8},{9,1... | collective-permute-start | bytes 12296 | tf_op jit(solution)/shard_map/ppermute | solution.py:427
  (17 other events, 13.4 us)

commit v8 on v7

--- a/solution.py
+++ b/solution.py
@@ -37,7 +37,7 @@
 NEAR_UNROLL = 4
 FAR_UNROLL = 6
 TILE = 16
-STEP_SHARES = 4
+STEP_SHARES = 16
 LEVELS = 32760.0
 WORK_SIZE = CHIP_BLOCKS * CAND // 4 + 16
 LOW = -1e30
@@ -162,10 +162,11 @@
 
 def near_kernel(
     place_ref, offsets_own_ref, counts_own_ref, offsets_other_ref, counts_other_ref,
-    q_own_hbm, q_other_ref, k_own_ref, k_other_ref, wq_hbm, wk_hbm,
+    q_own_hbm, q_other_hbm, k_own_hbm, k_other_hbm, wq_hbm, wk_hbm,
     queries, slot_max, slot_sum, pooled_query, gate_query, pooled_key, gate_key,
     far_list,
-    keys, near_vector, near_list, near_work, q_own_ref, wq_ref, wk_ref, sems,
+    keys, near_vector, near_list, near_work, q_own_ref, q_other_ref, k_own_ref, k_other_ref,
+    wq_ref, wk_ref, sems,
 ):
     core_ref = place_ref
     core = core_ref[0]
@@ -179,6 +180,14 @@
     wk_copy = pltpu.make_async_copy(
         wk_hbm.at[pl.ds(core * KV_HERE, KV_HERE)], wk_ref, sems.at[3]
     )
+    q_cols = pl.ds(pl.multiple_of(core * Q_COLS, Q_COLS), Q_COLS)
+    k_cols = pl.ds(pl.multiple_of(core * K_COLS, K_COLS), K_COLS)
+    q_other_copy = pltpu.make_async_copy(q_other_hbm.at[:, q_cols], q_other_ref, sems.at[4])
+    k_own_copy = pltpu.make_async_copy(k_own_hbm.at[:, k_cols], k_own_ref, sems.at[5])
+    k_other_copy = pltpu.make_async_copy(k_other_hbm.at[:, k_cols], k_other_ref, sems.at[6])
+    k_own_copy.start()
+    k_other_copy.start()
+    q_other_copy.start()
     q_copy.start()
     wq_copy.start()
     wk_copy.start()
@@ -196,6 +205,8 @@
     near_vector[...] = lists[0:CHIP_BLOCKS]
     list_copy = pltpu.make_async_copy(near_vector, near_list, sems.at[0])
     list_copy.start()
+    k_own_copy.wait()
+    k_other_copy.wait()
     for source, ref in ((core, k_own_ref), (1 - core, k_other_ref)):
         tile = ref[...]
         keys[pl.ds(pl.multiple_of(source * half, half), half), :] = tile
@@ -212,6 +223,7 @@
                     tile.astype(jnp.float32), axis=0, keepdims=True
                 ) * (1.0 / BLOCK)
 
+    q_other_copy.wait()
     for source in (1, 0):
         q_ref = (q_own_ref, q_other_ref)[source]
         if source == 0:
@@ -243,14 +255,22 @@
 
 def far_kernel(
     core_ref, far_list,
-    k_prev_own_ref, k_prev_other_ref, k_far_ref, queries,
+    k_prev_hbm, k_prev_other_ref, k_far_ref, queries,
     max_ref, sum_ref, pooled_query, gate_query, near_key, near_gate_key, wk_ref,
     out_ref,
     keys, slot_max, slot_sum, pooled_key, shares, hits, far_work,
+    k_prev_own_ref, sems,
 ):
     core = core_ref[0]
     half = ROWS * BLOCK
-    for place, ref in ((0, k_far_ref), (1 + core, k_prev_own_ref), (2 - core, k_prev_other_ref)):
+    k_copy = pltpu.make_async_copy(
+        k_prev_hbm.at[:, pl.ds(pl.multiple_of(core * K_COLS, K_COLS), K_COLS)],
+        k_prev_own_ref, sems.at[0],
+    )
+    k_copy.start()
+    for place, ref in ((0, k_far_ref), (2 - core, k_prev_other_ref), (1 + core, k_prev_own_ref)):
+        if ref is k_prev_own_ref:
+            k_copy.wait()
         tile = ref[...]
         at = place * half if isinstance(place, int) else pl.multiple_of(place * half, half)
         row = place * ROWS if isinstance(place, int) else pl.multiple_of(place * ROWS, ROWS)
@@ -439,8 +459,11 @@
     return pl.BlockSpec(memory_space=pltpu.SMEM)
 
 
-def cut_prev_kernel(place_ref, give_in, after_ref, give_ref):
-    give_ref[...] = give_in[...]
+def cut_prev_kernel(place_ref, keys_hbm, after_ref, give_ref, sems):
+    cols = pl.ds(pl.multiple_of((1 - place_ref[0]) * K_COLS, K_COLS), K_COLS)
+    give = pltpu.make_async_copy(keys_hbm.at[:, cols], give_ref, sems.at[0])
+    give.start()
+    give.wait()
 
 
 def cut_prev(place, keys, after):
@@ -451,12 +474,14 @@
             num_scalar_prefetch=1,
             grid=(1,),
             in_specs=[
-                pl.BlockSpec((half, K_COLS), lambda i, c: (0, 1 - c[0])),
+                pl.BlockSpec(memory_space=pltpu.HBM),
                 pl.BlockSpec(memory_space=pl.ANY),
             ],
             out_specs=whole(half, K_COLS),
+            scratch_shapes=[pltpu.SemaphoreType.DMA((1,))],
         ),
         out_shape=shaped((half, K_COLS), jnp.bfloat16),
+        compiler_params=pltpu.CompilerParams(vmem_limit_bytes=4 * 1024 * 1024),
         name="cut_prev",
     )(place, keys, after)
 
@@ -478,14 +503,7 @@
         grid_spec=pltpu.PrefetchScalarGridSpec(
             num_scalar_prefetch=1,
             grid=(1,),
-            in_specs=[whole(ROWS, CAND), smem()] * 2 + [
-                pl.BlockSpec(memory_space=pltpu.HBM),
-                pl.BlockSpec((half, Q_COLS), lambda i, c: (0, c[0])),
-                pl.BlockSpec((half, K_COLS), lambda i, c: (0, c[0])),
-                pl.BlockSpec((half, K_COLS), lambda i, c: (0, c[0])),
-                pl.BlockSpec(memory_space=pltpu.HBM),
-                pl.BlockSpec(memory_space=pltpu.HBM),
-            ],
+            in_specs=[whole(ROWS, CAND), smem()] * 2 + [pl.BlockSpec(memory_space=pltpu.HBM)] * 6,
             out_specs=[whole(*o.shape) for o in outs],
             scratch_shapes=[
                 pltpu.VMEM((CHIP_BLOCKS * BLOCK, K_COLS), jnp.bfloat16),
@@ -493,9 +511,12 @@
                 pltpu.SMEM((CHIP_BLOCKS, HEAD_DIM), jnp.int32),
                 pltpu.SMEM((WORK_SIZE,), jnp.int32),
                 pltpu.VMEM((half, Q_COLS), jnp.bfloat16),
+                pltpu.VMEM((half, Q_COLS), jnp.bfloat16),
+                pltpu.VMEM((half, K_COLS), jnp.bfloat16),
+                pltpu.VMEM((half, K_COLS), jnp.bfloat16),
                 pltpu.VMEM((HEADS_HERE, HEAD_DIM, HEAD_DIM), jnp.float32),
                 pltpu.VMEM((KV_HERE, POOL, HEAD_DIM), jnp.float32),
-                pltpu.SemaphoreType.DMA((4,)),
+                pltpu.SemaphoreType.DMA((7,)),
             ],
         ),
         out_shape=outs,
@@ -515,7 +536,7 @@
         grid_spec=pltpu.PrefetchScalarGridSpec(
             num_scalar_prefetch=1,
             grid=(1,),
-            in_specs=[smem(), pl.BlockSpec((half, K_COLS), lambda i, c: (0, c[0]))]
+            in_specs=[smem(), pl.BlockSpec(memory_space=pltpu.HBM)]
             + [whole(*a.shape) for a in args[1:]] + [
                 pl.BlockSpec((KV_HERE, POOL, HEAD_DIM), lambda i, c: (c[0], 0, 0)),
             ],
@@ -528,6 +549,8 @@
                 pltpu.VMEM((KV_HERE, PADDED, LANES), jnp.float32),
                 pltpu.VMEM((PADDED, LANES), jnp.float32),
                 pltpu.SMEM((WORK_SIZE,), jnp.int32),
+                pltpu.VMEM((half, K_COLS), jnp.bfloat16),
+                pltpu.SemaphoreType.DMA((1,)),
             ],
         ),
         out_shape=shaped((SHARES, PART_ROWS, HEAD_DIM)),

time: 129 us -> 110 us (0.85); the launches traced: 127 us -> 109 us
  local copies, waits for them, and re-layouts: 23.3 us -> 8.29 us
  Pallas kernels: 23.7 us -> 21.3 us
    unnamed x56 -> x26, local copies, waits for them, and re-layouts: 22.8 us -> 7.77 us
    pallas_call x1, Pallas kernels: 2.32 us -> 0.58 us  [cut_prev(): pl.pallas_call(cut_prev_kernel, grid_spec=pltpu.PrefetchScalarGridSpec(nu...]
where the time goes in v8:
time: 110 us; the launch traced here: 109 us
  blocking collectives  41.6 us (38%)
  starting transfers between devices  23 us (21%)
  Pallas kernels  21.3 us (19%)
  waiting for transfers between devices  10.9 us (10%)
  local copies, waits for them, and re-layouts  8.29 us (8%)
  between operations  2.54 us (2%)
  other arithmetic  1.84 us (2%)
    all_to_all x1, blocking collectives, body(): got = lax.all_to_all(parts, group, 0, 0)  27.1 us
    all_to_all x1, blocking collectives, body(): mine = lax.all_to_all(coded, group, 0, 0)  14.5 us
    ppermute x8, starting transfers between devices, swap(): return lax.ppermute(x, axis, [(0, 1), (1, 0)])  11.8 us
    pallas_call x1, Pallas kernels, near_call(): pl.pallas_call(near_kernel, grid_spec=pltpu.PrefetchScalarGridSpec(num_sc...  8.73 us
    unnamed x26, local copies, waits for them, and re-layouts  7.77 us
    ppermute x3, starting transfers between devices, body(): lax.ppermute(got, 'za', [(i, i ^ step) for i in range(4)])  6.87 us
    ppermute x8, waiting for transfers between devices, swap(): return lax.ppermute(x, axis, [(0, 1), (1, 0)])  5.48 us
    ppermute x3, waiting for transfers between devices, body(): lax.ppermute(got, 'za', [(i, i ^ step) for i in range(4)])  5.42 us
  transfers between devices with their start and end apart: 13, of which 6 were waited for; matrix products, arithmetic and copies ran while one was open for 2% of the time, Pallas kernels for 8%

profile of v8, /device:TPU:1, one launch (start us, length us, event | category | flops | bytes accessed | tf_op | source)
XLA Modules:
  0.0 109.5 jit_solution(8000776937682963428)
XLA Ops:
  0.6 3.3 %collective-permute-start.2 = (bf16[512,2048]{1,0:T(8,128)(2,1)}, bf16[512,2048]{1,0:T(8,128)(2,1)S(1)}, u32[]{:S(2)}, u32[]{:S(2)}) collective-permute-start(bf16[512,2048]{1,0:T(8,128)(2,1)} %q_own_hbm.1), channel_id=1, source_target_pairs={{0,2},{2,0},{1,3},{3,1},{4,6},{6,4},{5,7},{7,5},{8,10},{10,8},{9,1... | collective-permute-start | bytes 6291464 | tf_op jit(solution)/shard_map/ppermute | solution.py:447
  4.1 1.4 %collective-permute-start.4 = (bf16[512,512]{1,0:T(8,128)(2,1)}, bf16[512,512]{1,0:T(8,128)(2,1)S(1)}, u32[]{:S(2)}, u32[]{:S(2)}) collective-permute-start(bf16[512,512]{1,0:T(8,128)(2,1)} %k_own_hbm.1), channel_id=1, source_target_pairs={{0,4},{2,6},{4,8},{6,10},{8,12},{10,14},{12,16},{14,18},{16,20},{1... | collective-permute-start | bytes 1572872 | tf_op jit(solution)/shard_map/ppermute | solution.py:575
  6.4 2.3 %collective-permute-done.3.k_other_hbm = bf16[512,512]{1,0:T(8,128)(2,1)S(1)} collective-permute-done((bf16[512,512]{1,0:T(8,128)(2,1)}, bf16[512,512]{1,0:T(8,128)(2,1)S(1)}, u32[]{:S(2)}, u32[]{:S(2)}) %collective-permute-start.3) | collective-permute-done | bytes 524320 | tf_op jit(solution)/shard_map/ppermute | solution.py:447
  8.7 1.1 dynamic-slice_select_fusion
  9.8 2.9 %collective-permute-start.6 = (bf16[512,256]{1,0:T(8,128)(2,1)S(1)}, bf16[512,256]{1,0:T(8,128)(2,1)S(1)}, u32[]{:S(2)}, u32[]{:S(2)}) collective-permute-start(bf16[512,256]{1,0:T(8,128)(2,1)S(1)} %dynamic-slice_select_fusion), channel_id=1, source_target_pairs={{0,8},{2,10},{4,12},{6,14},{8,16},{10,18},{12,20},{14,22},{16,24},... | collective-permute-start | bytes 786440 | tf_op jit(solution)/shard_map/ppermute | solution.py:579
  12.8 1.0 copy-done
  13.8 1.6 %copy-done.2 = bf16[512,2048]{1,0:T(8,128)(2,1)S(1)} copy-done((bf16[512,2048]{1,0:T(8,128)(2,1)S(1)}, bf16[512,2048]{1,0:T(8,128)(2,1)}, u32[]{:S(2)}) %copy-start.2) | copy-done | bytes 2097176
  15.4 1.2 %copy-done.3 = f32[16,128,128]{2,1,0:T(8,128)S(1)} copy-done((f32[16,128,128]{2,1,0:T(8,128)S(1)}, f32[16,128,128]{2,1,0:T(8,128)}, u32[]{:S(2)}) %copy-start.3) | copy-done | bytes 1048600
  16.6 1.1 %copy-done.4 = f32[4,384,128]{2,1,0:T(8,128)S(1)} copy-done((f32[4,384,128]{2,1,0:T(8,128)S(1)}, f32[4,384,128]{2,1,0:T(8,128)}, u32[]{:S(2)}) %copy-start.4) | copy-done | bytes 786456
  19.1 8.7 %near.1 = (bf16[32,256,128]{2,1,0:T(8,128)(2,1)S(1)}, f32[32,32,256]{2,1,0:T(8,128)S(1)}, f32[32,32,256]{2,1,0:T(8,128)S(1)}, f32[2,64,128]{2,1,0:T(8,128)S(1)},...) custom-call(s32[2]{0:T(128)S(1)} %pad_add_fusion.place_ref.core_ref, ...), custom_call_target="tpu_custom_call" | custom-call | flops 2000000000 | bytes 8000000 | tf_op jit(solution)/shard_map/near/pallas_call | solution.py:501
  29.2 1.2 %collective-permute-done.5.k_prev_other_ref = bf16[512,256]{1,0:T(8,128)(2,1)S(1)} collective-permute-done((bf16[512,256]{1,0:T(8,128)(2,1)S(1)}, bf16[512,256]{1,0:T(8,128)(2,1)S(1)}, u32[]{:S(2)}, u32[]{:S(2)}) %collective-permute-start.5) | collective-permute-done | bytes 262176 | tf_op jit(solution)/shard_map/ppermute | solution.py:447
  30.3 4.9 %far.1 = f32[16,80,128]{2,1,0:T(8,128)S(1)} custom-call(s32[2]{0:T(128)S(1)} %pad_add_fusion.place_ref.core_ref, s32[16,128]{1,0:T(8,128)S(1)} %get-tuple-element.15.after_ref.far_list, bf16[512,512]{1,0:T(8,128)(2,1)S(1)} %collective-permute-done.4.keys_hbm.k_prev_hbm, bf16[512,256]{1,0:T(8,128)(2,1)S(1)} %collective-permute-done.5.k_prev_other_ref, ...), custom_call_target="tpu_custom_call" | custom-call | flops 2000000000 | bytes 8000000 | tf_op jit(solution)/shard_map/far/pallas_call | solution.py:534
  35.2 27.1 %all_to_all.10.parts_ref = f32[16,80,128]{2,1,0:T(8,128)} all-to-all(f32[16,80,128]{2,1,0:T(8,128)S(1)} %far.1), channel_id=1, replica_groups=mesh['za'=4,'zb'=2,'yh'=2,'x'=4,'core'=2,'head'=2] {'zb','yh','x'}, dimensions={0} | all-to-all | bytes 1310720 | tf_op jit(solution)/shard_map/all_to_all | solution.py:591
  62.4 2.0 %sum.1.own_ref = f32[120,128]{1,0:T(8,128)} custom-call(f32[16,80,128]{2,1,0:T(8,128)} %all_to_all.10.parts_ref), custom_call_target="tpu_custom_call" | custom-call | tf_op jit(solution)/shard_map/sum/pallas_call | solution.py:592
  64.3 3.6 %collective-permute-start.7 = (f32[120,128]{1,0:T(8,128)}, f32[120,128]{1,0:T(8,128)S(1)}, u32[]{:S(2)}, u32[]{:S(2)}) collective-permute-start(f32[120,128]{1,0:T(8,128)} %sum.1.own_ref), channel_id=1, source_target_pairs={{0,64},{64,0},{128,192},{192,128},{1,65},{65,1},{129,193},{193,129... | collective-permute-start | bytes 184328 | tf_op jit(solution)/shard_map/ppermute | solution.py:594
  67.9 3.1 %collective-permute-start.8 = (f32[120,128]{1,0:T(8,128)}, f32[120,128]{1,0:T(8,128)S(1)}, u32[]{:S(2)}, u32[]{:S(2)}) collective-permute-start(f32[120,128]{1,0:T(8,128)} %sum.1.own_ref), channel_id=1, source_target_pairs={{0,128},{64,192},{128,0},{192,64},{1,129},{65,193},{129,1},{193,65... | collective-permute-start | bytes 184328 | tf_op jit(solution)/shard_map/ppermute | solution.py:594
  71.2 4.7 %collective-permute-done.8.two_ref = f32[120,128]{1,0:T(8,128)S(1)} collective-permute-done((f32[120,128]{1,0:T(8,128)}, f32[120,128]{1,0:T(8,128)S(1)}, u32[]{:S(2)}, u32[]{:S(2)}) %collective-permute-start.8) | collective-permute-done | bytes 61472 | tf_op jit(solution)/shard_map/ppermute | solution.py:594
  77.3 1.8 %pack.1 = (s16[16,128,128]{2,1,0:T(8,128)(2,1)}, f32[8,128]{1,0:T(8,128)}) custom-call(f32[120,128]{1,0:T(8,128)} %sum.1.own_ref, f32[120,128]{1,0:T(8,128)} %copy-done.10, f32[120,128]{1,0:T(8,128)} %copy-done.11, f32[120,128]{1,0:T(8,128)} %copy-done.12), custom_call_target="tpu_custom_call" | custom-call | tf_op jit(solution)/shard_map/pack/pallas_call | solution.py:418
  79.1 14.5 %all_to_all.11.mine_ref = s16[16,128,128]{2,1,0:T(8,128)(2,1)S(1)} all-to-all(s16[16,128,128]{2,1,0:T(8,128)(2,1)} %get-tuple-element.23), channel_id=1, replica_groups=mesh['za'=4,'zb'=2,'yh'=2,'x'=4,'core'=2,'head'=2] {'zb','yh','x'}, dimensions={0} | all-to-all | bytes 1048576 | tf_op jit(solution)/shard_map/all_to_all | solution.py:599
  93.6 3.7 %collective-permute-start.10 = (s16[16,128,128]{2,1,0:T(8,128)(2,1)S(1)}, s16[16,128,128]{2,1,0:T(8,128)(2,1)S(1)}, u32[]{:S(2)}, u32[]{:S(2)}) collective-permute-start(s16[16,128,128]{2,1,0:T(8,128)(2,1)S(1)} %all_to_all.11.mine_ref), channel_id=1, source_target_pairs={{0,2},{2,0},{1,3},{3,1},{4,6},{6,4},{5,7},{7,5},{8,10},{10,8},{9,1... | collective-permute-start | bytes 1572872 | tf_op jit(solution)/shard_map/ppermute | solution.py:447
  97.3 2.1 %collective-permute-start.11 = (f32[8,128]{1,0:T(8,128)}, f32[8,128]{1,0:T(8,128)S(1)}, u32[]{:S(2)}, u32[]{:S(2)}) collective-permute-start(f32[8,128]{1,0:T(8,128)} %get-tuple-element.26), channel_id=1, source_target_pairs={{0,1},{1,0},{2,3},{3,2},{4,5},{5,4},{6,7},{7,6},{8,9},{9,8},{10,11... | collective-permute-start | bytes 12296 | tf_op jit(solution)/shard_map/ppermute | solution.py:447
  99.4 1.2 %collective-permute-done.11 = f32[8,128]{1,0:T(8,128)S(1)} collective-permute-done((f32[8,128]{1,0:T(8,128)}, f32[8,128]{1,0:T(8,128)S(1)}, u32[]{:S(2)}, u32[]{:S(2)}) %collective-permute-start.11) | collective-permute-done | bytes 4128 | tf_op jit(solution)/shard_map/ppermute | solution.py:447
  101.3 0.9 collective-permute-start.12
  105.0 3.3 %unpack.1 = (f32[2,1024,128]{2,1,0:T(8,128)}, f32[2,768,128]{2,1,0:T(8,128)}) custom-call(s32[2]{0:T(128)} %copy-done.1, s16[16,128,128]{2,1,0:T(8,128)(2,1)} %copy-done.8, s16[16,128,128]{2,1,0:T(8,128)(2,1)} %copy-done.9), custom_call_target="tpu_custom_call" | custom-call | tf_op jit(solution)/shard_map/unpack/pallas_call | solution.py:429
  (41 shorter events, 8.1 us)
Async XLA Ops:
  0.6 12.1 %collective-permute-start.2 = (bf16[512,2048]{1,0:T(8,128)(2,1)}, bf16[512,2048]{1,0:T(8,128)(2,1)S(1)}, u32[]{:S(2)}, u32[]{:S(2)}) collective-permute-start(bf16[512,2048]{1,0:T(8,128)(2,1)} %q_own_hbm.1), channel_id=1, source_target_pairs={{0,2},{2,0},{1,3},{3,1},{4,6},{6,4},{5,7},{7,5},{8,10},{10,8},{9,1... | collective-permute-start | bytes 6291464 | tf_op jit(solution)/shard_map/ppermute | solution.py:447
  4.0 4.7 %collective-permute-start.3 = (bf16[512,512]{1,0:T(8,128)(2,1)}, bf16[512,512]{1,0:T(8,128)(2,1)S(1)}, u32[]{:S(2)}, u32[]{:S(2)}) collective-permute-start(bf16[512,512]{1,0:T(8,128)(2,1)} %k_own_hbm.1), channel_id=1, source_target_pairs={{0,2},{2,0},{1,3},{3,1},{4,6},{6,4},{5,7},{7,5},{8,10},{10,8},{9,1... | collective-permute-start | bytes 1572872 | tf_op jit(solution)/shard_map/ppermute | solution.py:447
  4.1 23.8 %collective-permute-start.4 = (bf16[512,512]{1,0:T(8,128)(2,1)}, bf16[512,512]{1,0:T(8,128)(2,1)S(1)}, u32[]{:S(2)}, u32[]{:S(2)}) collective-permute-start(bf16[512,512]{1,0:T(8,128)(2,1)} %k_own_hbm.1), channel_id=1, source_target_pairs={{0,4},{2,6},{4,8},{6,10},{8,12},{10,14},{12,16},{14,18},{16,20},{1... | collective-permute-start | bytes 1572872 | tf_op jit(solution)/shard_map/ppermute | solution.py:575
  5.5 7.3 %collective-permute-start = (s32[8,24]{1,0:T(8,128)}, s32[8,24]{1,0:T(8,128)S(1)}, u32[]{:S(2)}, u32[]{:S(2)}) collective-permute-start(s32[8,24]{1,0:T(8,128)} %offsets_own_ref.1), channel_id=1, source_target_pairs={{0,2},{2,0},{1,3},{3,1},{4,6},{6,4},{5,7},{7,5},{8,10},{10,8},{9,1... | collective-permute-start | bytes 2312 | tf_op jit(solution)/shard_map/ppermute | solution.py:447
  6.2 6.5 %collective-permute-start.1 = (s32[8]{0:T(128)}, s32[8]{0:T(128)S(1)}, u32[]{:S(2)}, u32[]{:S(2)}) collective-permute-start(s32[8]{0:T(128)} %counts_own_ref.1), channel_id=1, source_target_pairs={{0,2},{2,0},{1,3},{3,1},{4,6},{6,4},{5,7},{7,5},{8,10},{10,8},{9,1... | collective-permute-start | bytes 104 | tf_op jit(solution)/shard_map/ppermute | solution.py:447
  6.4 23.9 %copy-start.1 = (s32[2]{0:T(128)}, s32[2]{0:T(128)S(1)}, u32[]{:S(2)}) copy-start(s32[2]{0:T(128)S(1)} %pad_add_fusion.place_ref.core_ref) | copy-start | bytes 28
  8.7 21.6 %copy-start.5 = (f32[4,384,128]{2,1,0:T(8,128)S(1)}, f32[4,384,128]{2,1,0:T(8,128)}, u32[]{:S(2)}) copy-start(f32[4,384,128]{2,1,0:T(8,128)} %wk_ref.1) | copy-start | bytes 2359300
  9.8 19.4 %collective-permute-start.6 = (bf16[512,256]{1,0:T(8,128)(2,1)S(1)}, bf16[512,256]{1,0:T(8,128)(2,1)S(1)}, u32[]{:S(2)}, u32[]{:S(2)}) collective-permute-start(bf16[512,256]{1,0:T(8,128)(2,1)S(1)} %dynamic-slice_select_fusion), channel_id=1, source_target_pairs={{0,8},{2,10},{4,12},{6,14},{8,16},{10,18},{12,20},{14,22},{16,24},... | collective-permute-start | bytes 786440 | tf_op jit(solution)/shard_map/ppermute | solution.py:579
  12.8 1.0 copy-start
  13.8 1.6 %copy-start.2 = (bf16[512,2048]{1,0:T(8,128)(2,1)S(1)}, bf16[512,2048]{1,0:T(8,128)(2,1)}, u32[]{:S(2)}) copy-start(bf16[512,2048]{1,0:T(8,128)(2,1)} %q_own_hbm.1) | copy-start | bytes 6291460
  15.4 1.2 %copy-start.3 = (f32[16,128,128]{2,1,0:T(8,128)S(1)}, f32[16,128,128]{2,1,0:T(8,128)}, u32[]{:S(2)}) copy-start(f32[16,128,128]{2,1,0:T(8,128)} %wq_hbm.1) | copy-start | bytes 3145732
  16.6 1.1 %copy-start.4 = (f32[4,384,128]{2,1,0:T(8,128)S(1)}, f32[4,384,128]{2,1,0:T(8,128)}, u32[]{:S(2)}) copy-start(f32[4,384,128]{2,1,0:T(8,128)} %wk_ref.1) | copy-start | bytes 2359300
  17.8 0.7 copy-start.6
  28.4 1.9 %collective-permute-start.5 = (bf16[512,256]{1,0:T(8,128)(2,1)S(1)}, bf16[512,256]{1,0:T(8,128)(2,1)S(1)}, u32[]{:S(2)}, u32[]{:S(2)}) collective-permute-start(bf16[512,256]{1,0:T(8,128)(2,1)S(1)} %cut_prev.1), channel_id=1, source_target_pairs={{0,2},{2,0},{1,3},{3,1},{4,6},{6,4},{5,7},{7,5},{8,10},{10,8},{9,1... | collective-permute-start | bytes 786440 | tf_op jit(solution)/shard_map/ppermute | solution.py:447
  64.3 6.9 %collective-permute-start.7 = (f32[120,128]{1,0:T(8,128)}, f32[120,128]{1,0:T(8,128)S(1)}, u32[]{:S(2)}, u32[]{:S(2)}) collective-permute-start(f32[120,128]{1,0:T(8,128)} %sum.1.own_ref), channel_id=1, source_target_pairs={{0,64},{64,0},{128,192},{192,128},{1,65},{65,1},{129,193},{193,129... | collective-permute-start | bytes 184328 | tf_op jit(solution)/shard_map/ppermute | solution.py:594
  67.9 8.0 %collective-permute-start.8 = (f32[120,128]{1,0:T(8,128)}, f32[120,128]{1,0:T(8,128)S(1)}, u32[]{:S(2)}, u32[]{:S(2)}) collective-permute-start(f32[120,128]{1,0:T(8,128)} %sum.1.own_ref), channel_id=1, source_target_pairs={{0,128},{64,192},{128,0},{192,64},{1,129},{65,193},{129,1},{193,65... | collective-permute-start | bytes 184328 | tf_op jit(solution)/shard_map/ppermute | solution.py:594
  71.0 5.7 %collective-permute-start.9 = (f32[120,128]{1,0:T(8,128)}, f32[120,128]{1,0:T(8,128)S(1)}, u32[]{:S(2)}, u32[]{:S(2)}) collective-permute-start(f32[120,128]{1,0:T(8,128)} %sum.1.own_ref), channel_id=1, source_target_pairs={{0,192},{64,128},{128,64},{192,0},{1,193},{65,129},{129,65},{193,1... | collective-permute-start | bytes 184328 | tf_op jit(solution)/shard_map/ppermute | solution.py:594
  71.2 5.4 %copy-start.10 = (f32[120,128]{1,0:T(8,128)}, f32[120,128]{1,0:T(8,128)S(1)}, u32[]{:S(2)}) copy-start(f32[120,128]{1,0:T(8,128)S(1)} %collective-permute-done.7.one_ref) | copy-start | bytes 184324
  75.9 0.7 copy-start.11
  93.6 10.6 %copy-start.8 = (s16[16,128,128]{2,1,0:T(8,128)(2,1)}, s16[16,128,128]{2,1,0:T(8,128)(2,1)S(1)}, u32[]{:S(2)}) copy-start(s16[16,128,128]{2,1,0:T(8,128)(2,1)S(1)} %all_to_all.11.mine_ref) | copy-start | bytes 1572868
  93.6 10.6 %collective-permute-start.10 = (s16[16,128,128]{2,1,0:T(8,128)(2,1)S(1)}, s16[16,128,128]{2,1,0:T(8,128)(2,1)S(1)}, u32[]{:S(2)}, u32[]{:S(2)}) collective-permute-start(s16[16,128,128]{2,1,0:T(8,128)(2,1)S(1)} %all_to_all.11.mine_ref), channel_id=1, source_target_pairs={{0,2},{2,0},{1,3},{3,1},{4,6},{6,4},{5,7},{7,5},{8,10},{10,8},{9,1... | collective-permute-start | bytes 1572872 | tf_op jit(solution)/shard_map/ppermute | solution.py:447
  97.3 3.3 %collective-permute-start.11 = (f32[8,128]{1,0:T(8,128)}, f32[8,128]{1,0:T(8,128)S(1)}, u32[]{:S(2)}, u32[]{:S(2)}) collective-permute-start(f32[8,128]{1,0:T(8,128)} %get-tuple-element.26), channel_id=1, source_target_pairs={{0,1},{1,0},{2,3},{3,2},{4,5},{5,4},{6,7},{7,6},{8,9},{9,8},{10,11... | collective-permute-start | bytes 12296 | tf_op jit(solution)/shard_map/ppermute | solution.py:447
  101.3 1.7 %collective-permute-start.12 = (f32[8,128]{1,0:T(8,128)S(1)}, f32[8,128]{1,0:T(8,128)S(1)}, u32[]{:S(2)}, u32[]{:S(2)}) collective-permute-start(f32[8,128]{1,0:T(8,128)S(1)} %add.23), channel_id=1, source_target_pairs={{0,2},{2,0},{1,3},{3,1},{4,6},{6,4},{5,7},{7,5},{8,10},{10,8},{9,1... | collective-permute-start | bytes 12296 | tf_op jit(solution)/shard_map/ppermute | solution.py:447
  104.2 0.8 copy-start.9
  (2 other events, 1.3 us)

commit v9 on v8

--- a/solution.py
+++ b/solution.py
@@ -35,7 +35,7 @@
 SUM_ROWS = HALF_HEAD + KEY_ROWS
 VMEM_BYTES = 40 * 1024 * 1024
 NEAR_UNROLL = 4
-FAR_UNROLL = 6
+FAR_UNROLL = 8
 TILE = 16
 STEP_SHARES = 16
 LEVELS = 32760.0
@@ -379,8 +379,8 @@
     out_ref[HALF_HEAD:, :] = jnp.sum(parts[:, CHIP_BLOCKS + ROWS:, :], axis=0)
 
 
-def pack_kernel(own_ref, one_ref, two_ref, three_ref, out_ref, total_ref):
-    got = (own_ref[...] + one_ref[...]) + (two_ref[...] + three_ref[...])
+def pack_kernel(got_ref, out_ref, total_ref):
+    got = got_ref[...]
     total_ref[...] = got[SUM_ROWS:, :]
     coded = []
     powers = jnp.zeros((TILE, HEAD_DIM), jnp.float32)
@@ -593,7 +593,7 @@
     one, two, three = (
         lax.ppermute(got, "za", [(i, i ^ step) for i in range(4)]) for step in (1, 2, 3)
     )
-    coded, total = pack(got, one, two, three)
+    coded, total = pack((got + one) + (two + three))
     total = total + swap(total, "head")
     total = total + swap(total, "core")
     mine = lax.all_to_all(coded, group, 0, 0)

time: 110 us -> 111 us (level)
  starting transfers between devices: 23 us -> 25.3 us
  other arithmetic: 1.84 us -> 3.31 us
  blocking collectives: 41.6 us -> 40.3 us
  waiting for transfers between devices: 10.9 us -> 9.69 us
    ppermute x3, starting transfers between devices: 6.87 us -> 8.66 us  [body(): lax.ppermute(got, 'za', [(i, i ^ step) for i in range(4)])]
    ppermute x3, waiting for transfers between devices: 5.42 us -> 3.95 us  [body(): lax.ppermute(got, 'za', [(i, i ^ step) for i in range(4)])]
    add x0 -> x1, other arithmetic: none -> 1.47 us  [body(): coded, total = pack(got + one + (two + three))]
    unnamed x26 -> x20, local copies, waits for them, and re-layouts: 7.77 us -> 7.13 us
  transfers between devices with their start and end apart: 13 -> 13, of which waited for: 6 -> 5; matrix products, arithmetic and copies ran while one was open for 2% -> 2% of each run, Pallas kernels for 8% -> 9%
where the time goes in v9:
time: 111 us
  blocking collectives  40.3 us (36%)
  starting transfers between devices  25.3 us (23%)
  Pallas kernels  21.9 us (20%)
  waiting for transfers between devices  9.69 us (9%)
  local copies, waits for them, and re-layouts  7.64 us (7%)
  other arithmetic  3.31 us (3%)
  between operations  2.54 us (2%)
    all_to_all x1, blocking collectives, body(): got = lax.all_to_all(parts, group, 0, 0)  26 us
    all_to_all x1, blocking collectives, body(): mine = lax.all_to_all(coded, group, 0, 0)  14.3 us
    ppermute x8, starting transfers between devices, swap(): return lax.ppermute(x, axis, [(0, 1), (1, 0)])  12.3 us
    pallas_call x1, Pallas kernels, near_call(): pl.pallas_call(near_kernel, grid_spec=pltpu.PrefetchScalarGridSpec(num_sc...  9.43 us
    ppermute x3, starting transfers between devices, body(): lax.ppermute(got, 'za', [(i, i ^ step) for i in range(4)])  8.66 us
    unnamed x20, local copies, waits for them, and re-layouts  7.13 us
    ppermute x8, waiting for transfers between devices, swap(): return lax.ppermute(x, axis, [(0, 1), (1, 0)])  5.74 us
    pallas_call x1, Pallas kernels, far_call(): pl.pallas_call(far_kernel, grid_spec=pltpu.PrefetchScalarGridSpec(num_sca...  4.86 us
  transfers between devices with their start and end apart: 13, of which 5 were waited for; matrix products, arithmetic and copies ran while one was open for 2% of the time, Pallas kernels for 9%

profile of v9, /device:TPU:1, one launch (start us, length us, event | category | flops | bytes accessed | tf_op | source)
XLA Modules:
  0.0 110.7 jit_solution(14718162186661865252)
XLA Ops:
  0.6 3.3 %collective-permute-start.2 = (bf16[512,2048]{1,0:T(8,128)(2,1)}, bf16[512,2048]{1,0:T(8,128)(2,1)S(1)}, u32[]{:S(2)}, u32[]{:S(2)}) collective-permute-start(bf16[512,2048]{1,0:T(8,128)(2,1)} %q_own_hbm.1), channel_id=1, source_target_pairs={{0,2},{2,0},{1,3},{3,1},{4,6},{6,4},{5,7},{7,5},{8,10},{10,8},{9,1... | collective-permute-start | bytes 6291464 | tf_op jit(solution)/shard_map/ppermute | solution.py:447
  4.1 1.4 %collective-permute-start.4 = (bf16[512,512]{1,0:T(8,128)(2,1)}, bf16[512,512]{1,0:T(8,128)(2,1)S(1)}, u32[]{:S(2)}, u32[]{:S(2)}) collective-permute-start(bf16[512,512]{1,0:T(8,128)(2,1)} %k_own_hbm.1), channel_id=1, source_target_pairs={{0,4},{2,6},{4,8},{6,10},{8,12},{10,14},{12,16},{14,18},{16,20},{1... | collective-permute-start | bytes 1572872 | tf_op jit(solution)/shard_map/ppermute | solution.py:575
  6.4 2.3 %collective-permute-done.3.k_other_hbm = bf16[512,512]{1,0:T(8,128)(2,1)S(1)} collective-permute-done((bf16[512,512]{1,0:T(8,128)(2,1)}, bf16[512,512]{1,0:T(8,128)(2,1)S(1)}, u32[]{:S(2)}, u32[]{:S(2)}) %collective-permute-start.3) | collective-permute-done | bytes 524320 | tf_op jit(solution)/shard_map/ppermute | solution.py:447
  9.8 2.9 %collective-permute-start.6 = (bf16[512,256]{1,0:T(8,128)(2,1)S(1)}, bf16[512,256]{1,0:T(8,128)(2,1)S(1)}, u32[]{:S(2)}, u32[]{:S(2)}) collective-permute-start(bf16[512,256]{1,0:T(8,128)(2,1)S(1)} %dynamic-slice_select_fusion), channel_id=1, source_target_pairs={{0,8},{2,10},{4,12},{6,14},{8,16},{10,18},{12,20},{14,22},{16,24},... | collective-permute-start | bytes 786440 | tf_op jit(solution)/shard_map/ppermute | solution.py:579
  13.8 1.6 %copy-done.2 = bf16[512,2048]{1,0:T(8,128)(2,1)S(1)} copy-done((bf16[512,2048]{1,0:T(8,128)(2,1)S(1)}, bf16[512,2048]{1,0:T(8,128)(2,1)}, u32[]{:S(2)}) %copy-start.2) | copy-done | bytes 2097176
  15.4 1.2 %copy-done.3 = f32[16,128,128]{2,1,0:T(8,128)S(1)} copy-done((f32[16,128,128]{2,1,0:T(8,128)S(1)}, f32[16,128,128]{2,1,0:T(8,128)}, u32[]{:S(2)}) %copy-start.3) | copy-done | bytes 1048600
  16.6 1.1 %copy-done.4 = f32[4,384,128]{2,1,0:T(8,128)S(1)} copy-done((f32[4,384,128]{2,1,0:T(8,128)S(1)}, f32[4,384,128]{2,1,0:T(8,128)}, u32[]{:S(2)}) %copy-start.4) | copy-done | bytes 786456
  19.1 9.4 %near.1 = (bf16[32,256,128]{2,1,0:T(8,128)(2,1)S(1)}, f32[32,32,256]{2,1,0:T(8,128)S(1)}, f32[32,32,256]{2,1,0:T(8,128)S(1)}, f32[2,64,128]{2,1,0:T(8,128)S(1)},...) custom-call(s32[2]{0:T(128)S(1)} %pad_add_fusion.place_ref.core_ref, ...), custom_call_target="tpu_custom_call" | custom-call | flops 2000000000 | bytes 8000000 | tf_op jit(solution)/shard_map/near/pallas_call | solution.py:501
  29.9 1.2 %collective-permute-done.5.k_prev_other_ref = bf16[512,256]{1,0:T(8,128)(2,1)S(1)} collective-permute-done((bf16[512,256]{1,0:T(8,128)(2,1)S(1)}, bf16[512,256]{1,0:T(8,128)(2,1)S(1)}, u32[]{:S(2)}, u32[]{:S(2)}) %collective-permute-start.5) | collective-permute-done | bytes 262176 | tf_op jit(solution)/shard_map/ppermute | solution.py:447
  31.0 4.9 %far.1 = f32[16,80,128]{2,1,0:T(8,128)S(1)} custom-call(s32[2]{0:T(128)S(1)} %pad_add_fusion.place_ref.core_ref, s32[16,128]{1,0:T(8,128)S(1)} %get-tuple-element.15.after_ref.far_list, bf16[512,512]{1,0:T(8,128)(2,1)S(1)} %collective-permute-done.4.keys_hbm.k_prev_hbm, bf16[512,256]{1,0:T(8,128)(2,1)S(1)} %collective-permute-done.5.k_prev_other_ref, ...), custom_call_target="tpu_custom_call" | custom-call | flops 2000000000 | bytes 8000000 | tf_op jit(solution)/shard_map/far/pallas_call | solution.py:534
  35.9 26.0 %all_to_all.10.parts_ref = f32[16,80,128]{2,1,0:T(8,128)} all-to-all(f32[16,80,128]{2,1,0:T(8,128)S(1)} %far.1), channel_id=1, replica_groups=mesh['za'=4,'zb'=2,'yh'=2,'x'=4,'core'=2,'head'=2] {'zb','yh','x'}, dimensions={0} | all-to-all | bytes 1310720 | tf_op jit(solution)/shard_map/all_to_all | solution.py:591
  62.0 2.0 %sum.1 = f32[120,128]{1,0:T(8,128)} custom-call(f32[16,80,128]{2,1,0:T(8,128)} %all_to_all.10.parts_ref), custom_call_target="tpu_custom_call" | custom-call | tf_op jit(solution)/shard_map/sum/pallas_call | solution.py:592
  63.9 5.4 %collective-permute-start.7 = (f32[120,128]{1,0:T(8,128)}, f32[120,128]{1,0:T(8,128)S(1)}, u32[]{:S(2)}, u32[]{:S(2)}) collective-permute-start(f32[120,128]{1,0:T(8,128)} %sum.1), channel_id=1, source_target_pairs={{0,64},{64,0},{128,192},{192,128},{1,65},{65,1},{129,193},{193,129... | collective-permute-start | bytes 184328 | tf_op jit(solution)/shard_map/ppermute | solution.py:594
  69.3 1.1 %collective-permute-start.8 = (f32[120,128]{1,0:T(8,128)}, f32[120,128]{1,0:T(8,128)S(1)}, u32[]{:S(2)}, u32[]{:S(2)}) collective-permute-start(f32[120,128]{1,0:T(8,128)} %sum.1), channel_id=1, source_target_pairs={{0,128},{64,192},{128,0},{192,64},{1,129},{65,193},{129,1},{193,65... | collective-permute-start | bytes 184328 | tf_op jit(solution)/shard_map/ppermute | solution.py:594
  70.4 2.2 %collective-permute-start.9 = (f32[120,128]{1,0:T(8,128)}, f32[120,128]{1,0:T(8,128)S(1)}, u32[]{:S(2)}, u32[]{:S(2)}) collective-permute-start(f32[120,128]{1,0:T(8,128)} %sum.1), channel_id=1, source_target_pairs={{0,192},{64,128},{128,64},{192,0},{1,193},{65,129},{129,65},{193,1... | collective-permute-start | bytes 184328 | tf_op jit(solution)/shard_map/ppermute | solution.py:594
  72.6 3.9 %collective-permute-done.8 = f32[120,128]{1,0:T(8,128)S(1)} collective-permute-done((f32[120,128]{1,0:T(8,128)}, f32[120,128]{1,0:T(8,128)S(1)}, u32[]{:S(2)}, u32[]{:S(2)}) %collective-permute-start.8) | collective-permute-done | bytes 61472 | tf_op jit(solution)/shard_map/ppermute | solution.py:594
  76.6 1.5 %add_add_fusion.got_ref = f32[120,128]{1,0:T(8,128)} fusion(f32[120,128]{1,0:T(8,128)S(1)} %collective-permute-done.8, f32[120,128]{1,0:T(8,128)S(1)} %collective-permute-done.9, f32[120,128]{1,0:T(8,128)} %sum.1, f32[120,128]{1,0:T(8,128)S(1)} %collective-permute-done.7), kind=kLoop, calls=%fused_computation.1 | loop fusion | flops 46080 | bytes 307200 | tf_op jit(solution)/shard_map/add | solution.py:596
  78.0 1.7 %pack.1 = (s16[16,128,128]{2,1,0:T(8,128)(2,1)}, f32[8,128]{1,0:T(8,128)}) custom-call(f32[120,128]{1,0:T(8,128)} %add_add_fusion.got_ref), custom_call_target="tpu_custom_call" | custom-call | tf_op jit(solution)/shard_map/pack/pallas_call | solution.py:418
  79.8 14.3 %all_to_all.11.mine_ref = s16[16,128,128]{2,1,0:T(8,128)(2,1)S(1)} all-to-all(s16[16,128,128]{2,1,0:T(8,128)(2,1)} %get-tuple-element.23), channel_id=1, replica_groups=mesh['za'=4,'zb'=2,'yh'=2,'x'=4,'core'=2,'head'=2] {'zb','yh','x'}, dimensions={0} | all-to-all | bytes 1048576 | tf_op jit(solution)/shard_map/all_to_all | solution.py:599
  94.0 4.9 %collective-permute-start.10 = (s16[16,128,128]{2,1,0:T(8,128)(2,1)S(1)}, s16[16,128,128]{2,1,0:T(8,128)(2,1)S(1)}, u32[]{:S(2)}, u32[]{:S(2)}) collective-permute-start(s16[16,128,128]{2,1,0:T(8,128)(2,1)S(1)} %all_to_all.11.mine_ref), channel_id=1, source_target_pairs={{0,2},{2,0},{1,3},{3,1},{4,6},{6,4},{5,7},{7,5},{8,10},{10,8},{9,1... | collective-permute-start | bytes 1572872 | tf_op jit(solution)/shard_map/ppermute | solution.py:447
  98.9 1.2 %collective-permute-start.11 = (f32[8,128]{1,0:T(8,128)}, f32[8,128]{1,0:T(8,128)S(1)}, u32[]{:S(2)}, u32[]{:S(2)}) collective-permute-start(f32[8,128]{1,0:T(8,128)} %get-tuple-element.26), channel_id=1, source_target_pairs={{0,1},{1,0},{2,3},{3,2},{4,5},{5,4},{6,7},{7,6},{8,9},{9,8},{10,11... | collective-permute-start | bytes 12296 | tf_op jit(solution)/shard_map/ppermute | solution.py:447
  100.1 1.5 %collective-permute-done.11 = f32[8,128]{1,0:T(8,128)S(1)} collective-permute-done((f32[8,128]{1,0:T(8,128)}, f32[8,128]{1,0:T(8,128)S(1)}, u32[]{:S(2)}, u32[]{:S(2)}) %collective-permute-start.11) | collective-permute-done | bytes 4128 | tf_op jit(solution)/shard_map/ppermute | solution.py:447
  102.2 1.2 %collective-permute-start.12 = (f32[8,128]{1,0:T(8,128)S(1)}, f32[8,128]{1,0:T(8,128)S(1)}, u32[]{:S(2)}, u32[]{:S(2)}) collective-permute-start(f32[8,128]{1,0:T(8,128)S(1)} %add.35), channel_id=1, source_target_pairs={{0,2},{2,0},{1,3},{3,1},{4,6},{6,4},{5,7},{7,5},{8,10},{10,8},{9,1... | collective-permute-start | bytes 12296 | tf_op jit(solution)/shard_map/ppermute | solution.py:447
  106.2 3.3 %unpack.1 = (f32[2,1024,128]{2,1,0:T(8,128)}, f32[2,768,128]{2,1,0:T(8,128)}) custom-call(s32[2]{0:T(128)} %copy-done.1, s16[16,128,128]{2,1,0:T(8,128)(2,1)} %copy-done.8, s16[16,128,128]{2,1,0:T(8,128)(2,1)} %copy-done.9), custom_call_target="tpu_custom_call" | custom-call | tf_op jit(solution)/shard_map/unpack/pallas_call | solution.py:429
  (36 shorter events, 8.7 us)
Async XLA Ops:
  0.6 12.1 %collective-permute-start.2 = (bf16[512,2048]{1,0:T(8,128)(2,1)}, bf16[512,2048]{1,0:T(8,128)(2,1)S(1)}, u32[]{:S(2)}, u32[]{:S(2)}) collective-permute-start(bf16[512,2048]{1,0:T(8,128)(2,1)} %q_own_hbm.1), channel_id=1, source_target_pairs={{0,2},{2,0},{1,3},{3,1},{4,6},{6,4},{5,7},{7,5},{8,10},{10,8},{9,1... | collective-permute-start | bytes 6291464 | tf_op jit(solution)/shard_map/ppermute | solution.py:447
  4.0 4.7 %collective-permute-start.3 = (bf16[512,512]{1,0:T(8,128)(2,1)}, bf16[512,512]{1,0:T(8,128)(2,1)S(1)}, u32[]{:S(2)}, u32[]{:S(2)}) collective-permute-start(bf16[512,512]{1,0:T(8,128)(2,1)} %k_own_hbm.1), channel_id=1, source_target_pairs={{0,2},{2,0},{1,3},{3,1},{4,6},{6,4},{5,7},{7,5},{8,10},{10,8},{9,1... | collective-permute-start | bytes 1572872 | tf_op jit(solution)/shard_map/ppermute | solution.py:447
  4.1 24.5 %collective-permute-start.4 = (bf16[512,512]{1,0:T(8,128)(2,1)}, bf16[512,512]{1,0:T(8,128)(2,1)S(1)}, u32[]{:S(2)}, u32[]{:S(2)}) collective-permute-start(bf16[512,512]{1,0:T(8,128)(2,1)} %k_own_hbm.1), channel_id=1, source_target_pairs={{0,4},{2,6},{4,8},{6,10},{8,12},{10,14},{12,16},{14,18},{16,20},{1... | collective-permute-start | bytes 1572872 | tf_op jit(solution)/shard_map/ppermute | solution.py:575
  5.5 7.3 %collective-permute-start = (s32[8,24]{1,0:T(8,128)}, s32[8,24]{1,0:T(8,128)S(1)}, u32[]{:S(2)}, u32[]{:S(2)}) collective-permute-start(s32[8,24]{1,0:T(8,128)} %offsets_own_ref.1), channel_id=1, source_target_pairs={{0,2},{2,0},{1,3},{3,1},{4,6},{6,4},{5,7},{7,5},{8,10},{10,8},{9,1... | collective-permute-start | bytes 2312 | tf_op jit(solution)/shard_map/ppermute | solution.py:447
  6.2 6.5 %collective-permute-start.1 = (s32[8]{0:T(128)}, s32[8]{0:T(128)S(1)}, u32[]{:S(2)}, u32[]{:S(2)}) collective-permute-start(s32[8]{0:T(128)} %counts_own_ref.1), channel_id=1, source_target_pairs={{0,2},{2,0},{1,3},{3,1},{4,6},{6,4},{5,7},{7,5},{8,10},{10,8},{9,1... | collective-permute-start | bytes 104 | tf_op jit(solution)/shard_map/ppermute | solution.py:447
  6.4 24.6 %copy-start.1 = (s32[2]{0:T(128)}, s32[2]{0:T(128)S(1)}, u32[]{:S(2)}) copy-start(s32[2]{0:T(128)S(1)} %pad_add_fusion.place_ref.core_ref) | copy-start | bytes 28
  8.7 22.3 %copy-start.5 = (f32[4,384,128]{2,1,0:T(8,128)S(1)}, f32[4,384,128]{2,1,0:T(8,128)}, u32[]{:S(2)}) copy-start(f32[4,384,128]{2,1,0:T(8,128)} %wk_ref.1) | copy-start | bytes 2359300
  9.8 20.1 %collective-permute-start.6 = (bf16[512,256]{1,0:T(8,128)(2,1)S(1)}, bf16[512,256]{1,0:T(8,128)(2,1)S(1)}, u32[]{:S(2)}, u32[]{:S(2)}) collective-permute-start(bf16[512,256]{1,0:T(8,128)(2,1)S(1)} %dynamic-slice_select_fusion), channel_id=1, source_target_pairs={{0,8},{2,10},{4,12},{6,14},{8,16},{10,18},{12,20},{14,22},{16,24},... | collective-permute-start | bytes 786440 | tf_op jit(solution)/shard_map/ppermute | solution.py:579
  12.8 1.0 copy-start
  13.8 1.6 %copy-start.2 = (bf16[512,2048]{1,0:T(8,128)(2,1)S(1)}, bf16[512,2048]{1,0:T(8,128)(2,1)}, u32[]{:S(2)}) copy-start(bf16[512,2048]{1,0:T(8,128)(2,1)} %q_own_hbm.1) | copy-start | bytes 6291460
  15.4 1.2 %copy-start.3 = (f32[16,128,128]{2,1,0:T(8,128)S(1)}, f32[16,128,128]{2,1,0:T(8,128)}, u32[]{:S(2)}) copy-start(f32[16,128,128]{2,1,0:T(8,128)} %wq_hbm.1) | copy-start | bytes 3145732
  16.6 1.1 %copy-start.4 = (f32[4,384,128]{2,1,0:T(8,128)S(1)}, f32[4,384,128]{2,1,0:T(8,128)}, u32[]{:S(2)}) copy-start(f32[4,384,128]{2,1,0:T(8,128)} %wk_ref.1) | copy-start | bytes 2359300
  17.8 0.7 copy-start.6
  18.4 0.7 copy-start.7
  29.1 1.9 %collective-permute-start.5 = (bf16[512,256]{1,0:T(8,128)(2,1)S(1)}, bf16[512,256]{1,0:T(8,128)(2,1)S(1)}, u32[]{:S(2)}, u32[]{:S(2)}) collective-permute-start(bf16[512,256]{1,0:T(8,128)(2,1)S(1)} %cut_prev.1), channel_id=1, source_target_pairs={{0,2},{2,0},{1,3},{3,1},{4,6},{6,4},{5,7},{7,5},{8,10},{10,8},{9,1... | collective-permute-start | bytes 786440 | tf_op jit(solution)/shard_map/ppermute | solution.py:447
  63.9 8.7 %collective-permute-start.7 = (f32[120,128]{1,0:T(8,128)}, f32[120,128]{1,0:T(8,128)S(1)}, u32[]{:S(2)}, u32[]{:S(2)}) collective-permute-start(f32[120,128]{1,0:T(8,128)} %sum.1), channel_id=1, source_target_pairs={{0,64},{64,0},{128,192},{192,128},{1,65},{65,1},{129,193},{193,129... | collective-permute-start | bytes 184328 | tf_op jit(solution)/shard_map/ppermute | solution.py:594
  69.3 7.2 %collective-permute-start.8 = (f32[120,128]{1,0:T(8,128)}, f32[120,128]{1,0:T(8,128)S(1)}, u32[]{:S(2)}, u32[]{:S(2)}) collective-permute-start(f32[120,128]{1,0:T(8,128)} %sum.1), channel_id=1, source_target_pairs={{0,128},{64,192},{128,0},{192,64},{1,129},{65,193},{129,1},{193,65... | collective-permute-start | bytes 184328 | tf_op jit(solution)/shard_map/ppermute | solution.py:594
  70.4 6.1 %collective-permute-start.9 = (f32[120,128]{1,0:T(8,128)}, f32[120,128]{1,0:T(8,128)S(1)}, u32[]{:S(2)}, u32[]{:S(2)}) collective-permute-start(f32[120,128]{1,0:T(8,128)} %sum.1), channel_id=1, source_target_pairs={{0,192},{64,128},{128,64},{192,0},{1,193},{65,129},{129,65},{193,1... | collective-permute-start | bytes 184328 | tf_op jit(solution)/shard_map/ppermute | solution.py:594
  94.0 11.4 %copy-start.8 = (s16[16,128,128]{2,1,0:T(8,128)(2,1)}, s16[16,128,128]{2,1,0:T(8,128)(2,1)S(1)}, u32[]{:S(2)}) copy-start(s16[16,128,128]{2,1,0:T(8,128)(2,1)S(1)} %all_to_all.11.mine_ref) | copy-start | bytes 1572868
  94.0 11.4 %collective-permute-start.10 = (s16[16,128,128]{2,1,0:T(8,128)(2,1)S(1)}, s16[16,128,128]{2,1,0:T(8,128)(2,1)S(1)}, u32[]{:S(2)}, u32[]{:S(2)}) collective-permute-start(s16[16,128,128]{2,1,0:T(8,128)(2,1)S(1)} %all_to_all.11.mine_ref), channel_id=1, source_target_pairs={{0,2},{2,0},{1,3},{3,1},{4,6},{6,4},{5,7},{7,5},{8,10},{10,8},{9,1... | collective-permute-start | bytes 1572872 | tf_op jit(solution)/shard_map/ppermute | solution.py:447
  98.9 2.7 %collective-permute-start.11 = (f32[8,128]{1,0:T(8,128)}, f32[8,128]{1,0:T(8,128)S(1)}, u32[]{:S(2)}, u32[]{:S(2)}) collective-permute-start(f32[8,128]{1,0:T(8,128)} %get-tuple-element.26), channel_id=1, source_target_pairs={{0,1},{1,0},{2,3},{3,2},{4,5},{5,4},{6,7},{7,6},{8,9},{9,8},{10,11... | collective-permute-start | bytes 12296 | tf_op jit(solution)/shard_map/ppermute | solution.py:447
  102.2 2.0 %collective-permute-start.12 = (f32[8,128]{1,0:T(8,128)S(1)}, f32[8,128]{1,0:T(8,128)S(1)}, u32[]{:S(2)}, u32[]{:S(2)}) collective-permute-start(f32[8,128]{1,0:T(8,128)S(1)} %add.35), channel_id=1, source_target_pairs={{0,2},{2,0},{1,3},{3,1},{4,6},{6,4},{5,7},{7,5},{8,10},{10,8},{9,1... | collective-permute-start | bytes 12296 | tf_op jit(solution)/shard_map/ppermute | solution.py:447
  105.4 0.8 copy-start.9

commit v10 on v8

--- a/solution.py
+++ b/solution.py
@@ -594,8 +594,8 @@
         lax.ppermute(got, "za", [(i, i ^ step) for i in range(4)]) for step in (1, 2, 3)
     )
     coded, total = pack(got, one, two, three)
-    total = total + swap(total, "head")
-    total = total + swap(total, "core")
+    across = lax.ppermute(total, ("core", "head"), [(i, 3 - i) for i in range(4)])
+    total = (total + swap(total, "head")) + (swap(total, "core") + across)
     mine = lax.all_to_all(coded, group, 0, 0)
     query_gradient, key_gradient = unpack(place, mine, swap(mine, "core"))
     return (

time: 110 us -> 110 us (level)
    ppermute x8, starting transfers between devices: 11.8 us -> 10.1 us  [swap(): return lax.ppermute(x, axis, [(0, 1), (1, 0)])]
    ppermute x0 -> x1, waiting for transfers between devices: none -> 1.23 us  [body(): lax.ppermute(total, ('core', 'head'), [(i, 3 - i) for i in range(4)])]
    ppermute x8, waiting for transfers between devices: 5.48 us -> 4.26 us  [swap(): return lax.ppermute(x, axis, [(0, 1), (1, 0)])]
    ppermute x0 -> x1, starting transfers between devices: none -> 1.21 us  [body(): lax.ppermute(total, ('core', 'head'), [(i, 3 - i) for i in range(4)])]
  transfers between devices with their start and end apart: 13 -> 14, of which waited for: 6 -> 6; matrix products, arithmetic and copies ran while one was open for 2% -> 2% of each run, Pallas kernels for 8% -> 9%
where the time goes in v10:
time: 110 us; the launch traced here: 109 us
  blocking collectives  40.9 us (37%)
  starting transfers between devices  22.7 us (21%)
  Pallas kernels  21.3 us (19%)
  waiting for transfers between devices  11.2 us (10%)
  local copies, waits for them, and re-layouts  8.28 us (8%)
  between operations  2.55 us (2%)
  other arithmetic  1.85 us (2%)
    all_to_all x1, blocking collectives, body(): got = lax.all_to_all(parts, group, 0, 0)  27.1 us
    all_to_all x1, blocking collectives, body(): mine = lax.all_to_all(coded, group, 0, 0)  13.8 us
    ppermute x8, starting transfers between devices, swap(): return lax.ppermute(x, axis, [(0, 1), (1, 0)])  10.1 us
    pallas_call x1, Pallas kernels, near_call(): pl.pallas_call(near_kernel, grid_spec=pltpu.PrefetchScalarGridSpec(num_sc...  8.73 us
    unnamed x26, local copies, waits for them, and re-layouts  7.77 us
    ppermute x3, starting transfers between devices, body(): lax.ppermute(got, 'za', [(i, i ^ step) for i in range(4)])  7.05 us
    ppermute x3, waiting for transfers between devices, body(): lax.ppermute(got, 'za', [(i, i ^ step) for i in range(4)])  5.68 us
    pallas_call x1, Pallas kernels, far_call(): pl.pallas_call(far_kernel, grid_spec=pltpu.PrefetchScalarGridSpec(num_sca...  4.87 us
  transfers between devices with their start and end apart: 14, of which 6 were waited for; matrix products, arithmetic and copies ran while one was open for 2% of the time, Pallas kernels for 9%

profile of v10, /device:TPU:1, one launch (start us, length us, event | category | flops | bytes accessed | tf_op | source)
XLA Modules:
  0.0 108.8 jit_solution(4871969329701630450)
XLA Ops:
  0.6 3.3 %collective-permute-start.2 = (bf16[512,2048]{1,0:T(8,128)(2,1)}, bf16[512,2048]{1,0:T(8,128)(2,1)S(1)}, u32[]{:S(2)}, u32[]{:S(2)}) collective-permute-start(bf16[512,2048]{1,0:T(8,128)(2,1)} %q_own_hbm.1), channel_id=1, source_target_pairs={{0,2},{2,0},{1,3},{3,1},{4,6},{6,4},{5,7},{7,5},{8,10},{10,8},{9,1... | collective-permute-start | bytes 6291464 | tf_op jit(solution)/shard_map/ppermute | solution.py:447
  4.1 1.4 %collective-permute-start.4 = (bf16[512,512]{1,0:T(8,128)(2,1)}, bf16[512,512]{1,0:T(8,128)(2,1)S(1)}, u32[]{:S(2)}, u32[]{:S(2)}) collective-permute-start(bf16[512,512]{1,0:T(8,128)(2,1)} %k_own_hbm.1), channel_id=1, source_target_pairs={{0,4},{2,6},{4,8},{6,10},{8,12},{10,14},{12,16},{14,18},{16,20},{1... | collective-permute-start | bytes 1572872 | tf_op jit(solution)/shard_map/ppermute | solution.py:575
  6.4 2.3 %collective-permute-done.3.k_other_hbm = bf16[512,512]{1,0:T(8,128)(2,1)S(1)} collective-permute-done((bf16[512,512]{1,0:T(8,128)(2,1)}, bf16[512,512]{1,0:T(8,128)(2,1)S(1)}, u32[]{:S(2)}, u32[]{:S(2)}) %collective-permute-start.3) | collective-permute-done | bytes 524320 | tf_op jit(solution)/shard_map/ppermute | solution.py:447
  8.7 1.1 %dynamic-slice_select_fusion = bf16[512,256]{1,0:T(8,128)(2,1)S(1)} fusion(bf16[512,512]{1,0:T(8,128)(2,1)S(1)} %collective-permute-done.3.k_other_hbm, s32[]{:T(128)S(6)} %select_n.13, bf16[512,512]{1,0:T(8,128)(2,1)} %k_own_hbm.1, pred[]{:T(512)S(6)} %eq.3), kind=kLoop, calls=%fused_computation | loop fusion | flops 131072 | bytes 786437 | tf_op jit(solution)/shard_map/jit(_where)/select_n | solution.py:580
  9.8 2.9 %collective-permute-start.6 = (bf16[512,256]{1,0:T(8,128)(2,1)S(1)}, bf16[512,256]{1,0:T(8,128)(2,1)S(1)}, u32[]{:S(2)}, u32[]{:S(2)}) collective-permute-start(bf16[512,256]{1,0:T(8,128)(2,1)S(1)} %dynamic-slice_select_fusion), channel_id=1, source_target_pairs={{0,8},{2,10},{4,12},{6,14},{8,16},{10,18},{12,20},{14,22},{16,24},... | collective-permute-start | bytes 786440 | tf_op jit(solution)/shard_map/ppermute | solution.py:579
  12.8 1.0 copy-done
  13.8 1.6 %copy-done.2 = bf16[512,2048]{1,0:T(8,128)(2,1)S(1)} copy-done((bf16[512,2048]{1,0:T(8,128)(2,1)S(1)}, bf16[512,2048]{1,0:T(8,128)(2,1)}, u32[]{:S(2)}) %copy-start.2) | copy-done | bytes 2097176
  15.4 1.2 %copy-done.3 = f32[16,128,128]{2,1,0:T(8,128)S(1)} copy-done((f32[16,128,128]{2,1,0:T(8,128)S(1)}, f32[16,128,128]{2,1,0:T(8,128)}, u32[]{:S(2)}) %copy-start.3) | copy-done | bytes 1048600
  16.6 1.1 %copy-done.4 = f32[4,384,128]{2,1,0:T(8,128)S(1)} copy-done((f32[4,384,128]{2,1,0:T(8,128)S(1)}, f32[4,384,128]{2,1,0:T(8,128)}, u32[]{:S(2)}) %copy-start.4) | copy-done | bytes 786456
  19.1 8.7 %near.1 = (bf16[32,256,128]{2,1,0:T(8,128)(2,1)S(1)}, f32[32,32,256]{2,1,0:T(8,128)S(1)}, f32[32,32,256]{2,1,0:T(8,128)S(1)}, f32[2,64,128]{2,1,0:T(8,128)S(1)},...) custom-call(s32[2]{0:T(128)S(1)} %pad_add_fusion.place_ref.core_ref, ...), custom_call_target="tpu_custom_call" | custom-call | flops 2000000000 | bytes 8000000 | tf_op jit(solution)/shard_map/near/pallas_call | solution.py:501
  29.2 1.2 %collective-permute-done.5.k_prev_other_ref = bf16[512,256]{1,0:T(8,128)(2,1)S(1)} collective-permute-done((bf16[512,256]{1,0:T(8,128)(2,1)S(1)}, bf16[512,256]{1,0:T(8,128)(2,1)S(1)}, u32[]{:S(2)}, u32[]{:S(2)}) %collective-permute-start.5) | collective-permute-done | bytes 262176 | tf_op jit(solution)/shard_map/ppermute | solution.py:447
  30.3 4.9 %far.1 = f32[16,80,128]{2,1,0:T(8,128)S(1)} custom-call(s32[2]{0:T(128)S(1)} %pad_add_fusion.place_ref.core_ref, s32[16,128]{1,0:T(8,128)S(1)} %get-tuple-element.15.after_ref.far_list, bf16[512,512]{1,0:T(8,128)(2,1)S(1)} %collective-permute-done.4.keys_hbm.k_prev_hbm, bf16[512,256]{1,0:T(8,128)(2,1)S(1)} %collective-permute-done.5.k_prev_other_ref, ...), custom_call_target="tpu_custom_call" | custom-call | flops 2000000000 | bytes 8000000 | tf_op jit(solution)/shard_map/far/pallas_call | solution.py:534
  35.2 27.1 %all_to_all.10.parts_ref = f32[16,80,128]{2,1,0:T(8,128)} all-to-all(f32[16,80,128]{2,1,0:T(8,128)S(1)} %far.1), channel_id=1, replica_groups=mesh['za'=4,'zb'=2,'yh'=2,'x'=4,'core'=2,'head'=2] {'zb','yh','x'}, dimensions={0} | all-to-all | bytes 1310720 | tf_op jit(solution)/shard_map/all_to_all | solution.py:591
  62.4 2.0 %sum.1.own_ref = f32[120,128]{1,0:T(8,128)} custom-call(f32[16,80,128]{2,1,0:T(8,128)} %all_to_all.10.parts_ref), custom_call_target="tpu_custom_call" | custom-call | tf_op jit(solution)/shard_map/sum/pallas_call | solution.py:592
  64.3 3.2 %collective-permute-start.7 = (f32[120,128]{1,0:T(8,128)}, f32[120,128]{1,0:T(8,128)S(1)}, u32[]{:S(2)}, u32[]{:S(2)}) collective-permute-start(f32[120,128]{1,0:T(8,128)} %sum.1.own_ref), channel_id=1, source_target_pairs={{0,64},{64,0},{128,192},{192,128},{1,65},{65,1},{129,193},{193,129... | collective-permute-start | bytes 184328 | tf_op jit(solution)/shard_map/ppermute | solution.py:594
  67.6 3.8 %collective-permute-start.8 = (f32[120,128]{1,0:T(8,128)}, f32[120,128]{1,0:T(8,128)S(1)}, u32[]{:S(2)}, u32[]{:S(2)}) collective-permute-start(f32[120,128]{1,0:T(8,128)} %sum.1.own_ref), channel_id=1, source_target_pairs={{0,128},{64,192},{128,0},{192,64},{1,129},{65,193},{129,1},{193,65... | collective-permute-start | bytes 184328 | tf_op jit(solution)/shard_map/ppermute | solution.py:594
  71.4 3.5 %collective-permute-done.8.two_ref = f32[120,128]{1,0:T(8,128)S(1)} collective-permute-done((f32[120,128]{1,0:T(8,128)}, f32[120,128]{1,0:T(8,128)S(1)}, u32[]{:S(2)}, u32[]{:S(2)}) %collective-permute-start.8) | collective-permute-done | bytes 61472 | tf_op jit(solution)/shard_map/ppermute | solution.py:594
  74.9 2.1 %collective-permute-done.9.three_ref = f32[120,128]{1,0:T(8,128)S(1)} collective-permute-done((f32[120,128]{1,0:T(8,128)}, f32[120,128]{1,0:T(8,128)S(1)}, u32[]{:S(2)}, u32[]{:S(2)}) %collective-permute-start.9) | collective-permute-done | bytes 61472 | tf_op jit(solution)/shard_map/ppermute | solution.py:594
  77.7 1.8 %pack.1 = (s16[16,128,128]{2,1,0:T(8,128)(2,1)}, f32[8,128]{1,0:T(8,128)}) custom-call(f32[120,128]{1,0:T(8,128)} %sum.1.own_ref, f32[120,128]{1,0:T(8,128)} %copy-done.10, f32[120,128]{1,0:T(8,128)} %copy-done.11, f32[120,128]{1,0:T(8,128)} %copy-done.12), custom_call_target="tpu_custom_call" | custom-call | tf_op jit(solution)/shard_map/pack/pallas_call | solution.py:418
  79.5 13.8 %all_to_all.11.mine_ref = s16[16,128,128]{2,1,0:T(8,128)(2,1)S(1)} all-to-all(s16[16,128,128]{2,1,0:T(8,128)(2,1)} %get-tuple-element.23), channel_id=1, replica_groups=mesh['za'=4,'zb'=2,'yh'=2,'x'=4,'core'=2,'head'=2] {'zb','yh','x'}, dimensions={0} | all-to-all | bytes 1048576 | tf_op jit(solution)/shard_map/all_to_all | solution.py:599
  93.3 4.4 %collective-permute-start.10 = (s16[16,128,128]{2,1,0:T(8,128)(2,1)S(1)}, s16[16,128,128]{2,1,0:T(8,128)(2,1)S(1)}, u32[]{:S(2)}, u32[]{:S(2)}) collective-permute-start(s16[16,128,128]{2,1,0:T(8,128)(2,1)S(1)} %all_to_all.11.mine_ref), channel_id=1, source_target_pairs={{0,2},{2,0},{1,3},{3,1},{4,6},{6,4},{5,7},{7,5},{8,10},{10,8},{9,1... | collective-permute-start | bytes 1572872 | tf_op jit(solution)/shard_map/ppermute | solution.py:447
  98.4 1.2 %collective-permute-start.13 = (f32[8,128]{1,0:T(8,128)}, f32[8,128]{1,0:T(8,128)S(1)}, u32[]{:S(2)}, u32[]{:S(2)}) collective-permute-start(f32[8,128]{1,0:T(8,128)} %get-tuple-element.26), channel_id=1, source_target_pairs={{0,3},{1,2},{2,1},{3,0},{4,7},{5,6},{6,5},{7,4},{8,11},{9,10},{10,... | collective-permute-start | bytes 12296 | tf_op jit(solution)/shard_map/ppermute | solution.py:597
  100.4 1.2 %collective-permute-done.13 = f32[8,128]{1,0:T(8,128)S(1)} collective-permute-done((f32[8,128]{1,0:T(8,128)}, f32[8,128]{1,0:T(8,128)S(1)}, u32[]{:S(2)}, u32[]{:S(2)}) %collective-permute-start.13) | collective-permute-done | bytes 4128 | tf_op jit(solution)/shard_map/ppermute | solution.py:597
  104.3 3.3 %unpack.1 = (f32[2,1024,128]{2,1,0:T(8,128)}, f32[2,768,128]{2,1,0:T(8,128)}) custom-call(s32[2]{0:T(128)} %copy-done.1, s16[16,128,128]{2,1,0:T(8,128)(2,1)} %copy-done.8, s16[16,128,128]{2,1,0:T(8,128)(2,1)} %copy-done.9), custom_call_target="tpu_custom_call" | custom-call | tf_op jit(solution)/shard_map/unpack/pallas_call | solution.py:429
  (42 shorter events, 7.8 us)
Async XLA Ops:
  0.6 12.1 %collective-permute-start.2 = (bf16[512,2048]{1,0:T(8,128)(2,1)}, bf16[512,2048]{1,0:T(8,128)(2,1)S(1)}, u32[]{:S(2)}, u32[]{:S(2)}) collective-permute-start(bf16[512,2048]{1,0:T(8,128)(2,1)} %q_own_hbm.1), channel_id=1, source_target_pairs={{0,2},{2,0},{1,3},{3,1},{4,6},{6,4},{5,7},{7,5},{8,10},{10,8},{9,1... | collective-permute-start | bytes 6291464 | tf_op jit(solution)/shard_map/ppermute | solution.py:447
  4.0 4.7 %collective-permute-start.3 = (bf16[512,512]{1,0:T(8,128)(2,1)}, bf16[512,512]{1,0:T(8,128)(2,1)S(1)}, u32[]{:S(2)}, u32[]{:S(2)}) collective-permute-start(bf16[512,512]{1,0:T(8,128)(2,1)} %k_own_hbm.1), channel_id=1, source_target_pairs={{0,2},{2,0},{1,3},{3,1},{4,6},{6,4},{5,7},{7,5},{8,10},{10,8},{9,1... | collective-permute-start | bytes 1572872 | tf_op jit(solution)/shard_map/ppermute | solution.py:447
  4.1 23.8 %collective-permute-start.4 = (bf16[512,512]{1,0:T(8,128)(2,1)}, bf16[512,512]{1,0:T(8,128)(2,1)S(1)}, u32[]{:S(2)}, u32[]{:S(2)}) collective-permute-start(bf16[512,512]{1,0:T(8,128)(2,1)} %k_own_hbm.1), channel_id=1, source_target_pairs={{0,4},{2,6},{4,8},{6,10},{8,12},{10,14},{12,16},{14,18},{16,20},{1... | collective-permute-start | bytes 1572872 | tf_op jit(solution)/shard_map/ppermute | solution.py:575
  5.5 7.3 %collective-permute-start = (s32[8,24]{1,0:T(8,128)}, s32[8,24]{1,0:T(8,128)S(1)}, u32[]{:S(2)}, u32[]{:S(2)}) collective-permute-start(s32[8,24]{1,0:T(8,128)} %offsets_own_ref.1), channel_id=1, source_target_pairs={{0,2},{2,0},{1,3},{3,1},{4,6},{6,4},{5,7},{7,5},{8,10},{10,8},{9,1... | collective-permute-start | bytes 2312 | tf_op jit(solution)/shard_map/ppermute | solution.py:447
  6.2 6.5 %collective-permute-start.1 = (s32[8]{0:T(128)}, s32[8]{0:T(128)S(1)}, u32[]{:S(2)}, u32[]{:S(2)}) collective-permute-start(s32[8]{0:T(128)} %counts_own_ref.1), channel_id=1, source_target_pairs={{0,2},{2,0},{1,3},{3,1},{4,6},{6,4},{5,7},{7,5},{8,10},{10,8},{9,1... | collective-permute-start | bytes 104 | tf_op jit(solution)/shard_map/ppermute | solution.py:447
  6.4 23.9 %copy-start.1 = (s32[2]{0:T(128)}, s32[2]{0:T(128)S(1)}, u32[]{:S(2)}) copy-start(s32[2]{0:T(128)S(1)} %pad_add_fusion.place_ref.core_ref) | copy-start | bytes 28
  8.7 21.6 %copy-start.5 = (f32[4,384,128]{2,1,0:T(8,128)S(1)}, f32[4,384,128]{2,1,0:T(8,128)}, u32[]{:S(2)}) copy-start(f32[4,384,128]{2,1,0:T(8,128)} %wk_ref.1) | copy-start | bytes 2359300
  9.8 19.4 %collective-permute-start.6 = (bf16[512,256]{1,0:T(8,128)(2,1)S(1)}, bf16[512,256]{1,0:T(8,128)(2,1)S(1)}, u32[]{:S(2)}, u32[]{:S(2)}) collective-permute-start(bf16[512,256]{1,0:T(8,128)(2,1)S(1)} %dynamic-slice_select_fusion), channel_id=1, source_target_pairs={{0,8},{2,10},{4,12},{6,14},{8,16},{10,18},{12,20},{14,22},{16,24},... | collective-permute-start | bytes 786440 | tf_op jit(solution)/shard_map/ppermute | solution.py:579
  12.8 1.0 copy-start
  13.8 1.6 %copy-start.2 = (bf16[512,2048]{1,0:T(8,128)(2,1)S(1)}, bf16[512,2048]{1,0:T(8,128)(2,1)}, u32[]{:S(2)}) copy-start(bf16[512,2048]{1,0:T(8,128)(2,1)} %q_own_hbm.1) | copy-start | bytes 6291460
  15.4 1.2 %copy-start.3 = (f32[16,128,128]{2,1,0:T(8,128)S(1)}, f32[16,128,128]{2,1,0:T(8,128)}, u32[]{:S(2)}) copy-start(f32[16,128,128]{2,1,0:T(8,128)} %wq_hbm.1) | copy-start | bytes 3145732
  16.6 1.1 %copy-start.4 = (f32[4,384,128]{2,1,0:T(8,128)S(1)}, f32[4,384,128]{2,1,0:T(8,128)}, u32[]{:S(2)}) copy-start(f32[4,384,128]{2,1,0:T(8,128)} %wk_ref.1) | copy-start | bytes 2359300
  28.4 1.9 %collective-permute-start.5 = (bf16[512,256]{1,0:T(8,128)(2,1)S(1)}, bf16[512,256]{1,0:T(8,128)(2,1)S(1)}, u32[]{:S(2)}, u32[]{:S(2)}) collective-permute-start(bf16[512,256]{1,0:T(8,128)(2,1)S(1)} %cut_prev.1), channel_id=1, source_target_pairs={{0,2},{2,0},{1,3},{3,1},{4,6},{6,4},{5,7},{7,5},{8,10},{10,8},{9,1... | collective-permute-start | bytes 786440 | tf_op jit(solution)/shard_map/ppermute | solution.py:447
  64.3 7.1 %collective-permute-start.7 = (f32[120,128]{1,0:T(8,128)}, f32[120,128]{1,0:T(8,128)S(1)}, u32[]{:S(2)}, u32[]{:S(2)}) collective-permute-start(f32[120,128]{1,0:T(8,128)} %sum.1.own_ref), channel_id=1, source_target_pairs={{0,64},{64,0},{128,192},{192,128},{1,65},{65,1},{129,193},{193,129... | collective-permute-start | bytes 184328 | tf_op jit(solution)/shard_map/ppermute | solution.py:594
  67.6 7.4 %collective-permute-start.8 = (f32[120,128]{1,0:T(8,128)}, f32[120,128]{1,0:T(8,128)S(1)}, u32[]{:S(2)}, u32[]{:S(2)}) collective-permute-start(f32[120,128]{1,0:T(8,128)} %sum.1.own_ref), channel_id=1, source_target_pairs={{0,128},{64,192},{128,0},{192,64},{1,129},{65,193},{129,1},{193,65... | collective-permute-start | bytes 184328 | tf_op jit(solution)/shard_map/ppermute | solution.py:594
  71.4 5.7 %collective-permute-start.9 = (f32[120,128]{1,0:T(8,128)}, f32[120,128]{1,0:T(8,128)S(1)}, u32[]{:S(2)}, u32[]{:S(2)}) collective-permute-start(f32[120,128]{1,0:T(8,128)} %sum.1.own_ref), channel_id=1, source_target_pairs={{0,192},{64,128},{128,64},{192,0},{1,193},{65,129},{129,65},{193,1... | collective-permute-start | bytes 184328 | tf_op jit(solution)/shard_map/ppermute | solution.py:594
  71.4 5.7 %copy-start.10 = (f32[120,128]{1,0:T(8,128)}, f32[120,128]{1,0:T(8,128)S(1)}, u32[]{:S(2)}) copy-start(f32[120,128]{1,0:T(8,128)S(1)} %collective-permute-done.7.one_ref) | copy-start | bytes 184324
  74.9 2.1 %copy-start.11 = (f32[120,128]{1,0:T(8,128)}, f32[120,128]{1,0:T(8,128)S(1)}, u32[]{:S(2)}) copy-start(f32[120,128]{1,0:T(8,128)S(1)} %collective-permute-done.8.two_ref) | copy-start | bytes 184324
  93.3 10.2 %copy-start.8 = (s16[16,128,128]{2,1,0:T(8,128)(2,1)}, s16[16,128,128]{2,1,0:T(8,128)(2,1)S(1)}, u32[]{:S(2)}) copy-start(s16[16,128,128]{2,1,0:T(8,128)(2,1)S(1)} %all_to_all.11.mine_ref) | copy-start | bytes 1572868
  93.3 10.2 %collective-permute-start.10 = (s16[16,128,128]{2,1,0:T(8,128)(2,1)S(1)}, s16[16,128,128]{2,1,0:T(8,128)(2,1)S(1)}, u32[]{:S(2)}, u32[]{:S(2)}) collective-permute-start(s16[16,128,128]{2,1,0:T(8,128)(2,1)S(1)} %all_to_all.11.mine_ref), channel_id=1, source_target_pairs={{0,2},{2,0},{1,3},{3,1},{4,6},{6,4},{5,7},{7,5},{8,10},{10,8},{9,1... | collective-permute-start | bytes 1572872 | tf_op jit(solution)/shard_map/ppermute | solution.py:447
  97.7 2.7 %collective-permute-start.11 = (f32[8,128]{1,0:T(8,128)}, f32[8,128]{1,0:T(8,128)S(1)}, u32[]{:S(2)}, u32[]{:S(2)}) collective-permute-start(f32[8,128]{1,0:T(8,128)} %get-tuple-element.26), channel_id=1, source_target_pairs={{0,1},{1,0},{2,3},{3,2},{4,5},{5,4},{6,7},{7,6},{8,9},{9,8},{10,11... | collective-permute-start | bytes 12296 | tf_op jit(solution)/shard_map/ppermute | solution.py:447
  98.1 2.3 %collective-permute-start.12 = (f32[8,128]{1,0:T(8,128)}, f32[8,128]{1,0:T(8,128)S(1)}, u32[]{:S(2)}, u32[]{:S(2)}) collective-permute-start(f32[8,128]{1,0:T(8,128)} %get-tuple-element.26), channel_id=1, source_target_pairs={{0,2},{2,0},{1,3},{3,1},{4,6},{6,4},{5,7},{7,5},{8,10},{10,8},{9,1... | collective-permute-start | bytes 12296 | tf_op jit(solution)/shard_map/ppermute | solution.py:447
  98.4 3.2 %collective-permute-start.13 = (f32[8,128]{1,0:T(8,128)}, f32[8,128]{1,0:T(8,128)S(1)}, u32[]{:S(2)}, u32[]{:S(2)}) collective-permute-start(f32[8,128]{1,0:T(8,128)} %get-tuple-element.26), channel_id=1, source_target_pairs={{0,3},{1,2},{2,1},{3,0},{4,7},{5,6},{6,5},{7,4},{8,11},{9,10},{10,... | collective-permute-start | bytes 12296 | tf_op jit(solution)/shard_map/ppermute | solution.py:597
  103.5 0.8 copy-start.9
  (3 other events, 2.0 us)
